TPU v7x, 256 devices: a whole 4x4x8 slice. The times are simulated.
256 devices in a mesh: wide: 64 (over y_hi, z, x), narrow: 4 (over y_lo, core).
Axes of the slice: x: 4, y: 4 (y_hi: 2, y_lo: 2; y = y_hi * 2 + y_lo), z: 8, core: 2. Of those that a mesh axis runs over, the one named last changes fastest.
Arguments:
- volume: bfloat16 [128, 16, 64, 256], P('wide', 'narrow'), may hold values from -6 to 6
- volume_tangent: bfloat16 [128, 16, 64, 256], P('wide', 'narrow'), may hold values from -6 to 6
- shallow_weight: bfloat16 [3, 3, 3, 64, 64], replicated, may hold values from -0.15625 to 0.15625
- deep_weight: bfloat16 [3, 3, 3, 64, 256], replicated, may hold values from -0.15625 to 0.15625
Outputs:
- skip_features: bfloat16 [128, 16, 64, 256], P('wide', 'narrow')
- skip_tangent: bfloat16 [128, 16, 64, 256], P('wide', 'narrow')
- deep_features: bfloat16 [64, 8, 256, 128], P('wide', None, 'narrow')
- deep_tangent: bfloat16 [64, 8, 256, 128], P('wide', None, 'narrow')
All inputs are finite; a program needn't handle non-finite values.
Results may differ from a plain program's by a relative error of at most 0.0058.
Values may be sent and summed in bfloat16 or wider, within the bound.
No kernel may reach another device: no remote copies, remote signals or barrier semaphores. Data moves between devices by JAX's collectives and lax.ppermute only.
A program may use at most 64 MiB of HBM per device.

v0:
```python
import jax
import jax.numpy as jnp
from jax import lax
from jax.sharding import PartitionSpec as P


def with_halo(cells, sides, width):
    for axis, dim in sides:
        count = lax.axis_size(axis)
        ends = count - 1
        head = lax.slice_in_dim(cells, 0, width, axis=dim)
        tail = lax.slice_in_dim(cells, cells.shape[dim] - width, cells.shape[dim], axis=dim)
        cells = jnp.concatenate(
            [
                lax.ppermute(tail, axis, [(i, (i + 1) % count) for i in range(ends)]),
                cells,
                lax.ppermute(head, axis, [((i + 1) % count, i) for i in range(ends)]),
            ],
            axis=dim,
        )
    return cells


def conv_taps(padded, weight):
    return lax.conv_general_dilated(
        padded,
        weight,
        (1, 1, 1),
        ((0, 0), (0, 0), (1, 1)),
        dimension_numbers=("NDHCW", "DHWIO", "NDHCW"),
        preferred_element_type=jnp.float32,
    )


def activate(preact):
    sigmoid_v = jax.nn.sigmoid(preact[0])
    primal = (preact[0] * sigmoid_v).astype(jnp.bfloat16)
    slope = sigmoid_v * (1.0 + preact[0] * (1.0 - sigmoid_v))
    tangent = (slope * preact[1]).astype(jnp.bfloat16)
    return (primal, tangent)


def average_pool(stacked):
    count, planes, rows_y, channels, cells_x = stacked.shape
    blocks = stacked.astype(jnp.float32).reshape(
        count, planes // 2, 2, rows_y // 2, 2, channels, cells_x
    )
    summed = jnp.sum(blocks, axis=(2, 4))
    source = lax.broadcasted_iota(jnp.int32, (cells_x, cells_x // 2), 0)
    target = lax.broadcasted_iota(jnp.int32, (cells_x, cells_x // 2), 1)
    pairing = jnp.where(source // 2 == target, 0.125, 0.0).astype(jnp.float32)
    pooled = jnp.dot(
        summed, pairing, precision=lax.Precision.HIGHEST, preferred_element_type=jnp.float32
    )
    return pooled.astype(jnp.bfloat16)


def local(volume, volume_tangent, shallow_weight, deep_weight):
    stacked = jnp.stack([volume, volume_tangent])
    padded = with_halo(stacked, (("wide", 1), ("narrow", 2)), 1)
    skip_features, skip_tangent = activate(conv_taps(padded, shallow_weight))
    pooled = average_pool(jnp.stack([skip_features, skip_tangent]))
    whole_y = lax.all_gather(pooled, "narrow", axis=2, tiled=True)
    deep_padded = with_halo(whole_y, (("wide", 1),), 1)
    deep_padded = jnp.pad(deep_padded, ((0, 0), (0, 0), (1, 1), (0, 0), (0, 0)))
    filter_share = deep_weight.shape[4] // lax.axis_size("narrow")
    weight_share = lax.dynamic_slice_in_dim(
        deep_weight, lax.axis_index("narrow") * filter_share, filter_share, 4
    )
    deep_features, deep_tangent = activate(conv_taps(deep_padded, weight_share))
    return (skip_features, skip_tangent, deep_features, deep_tangent)


def solution(mesh):
    in_specs = (P("wide", "narrow", None, None), P("wide", "narrow", None, None), P(), P())
    out_specs = (
        P("wide", "narrow", None, None),
        P("wide", "narrow", None, None),
        P("wide", None, "narrow", None),
        P("wide", None, "narrow", None),
    )
    return jax.shard_map(local, mesh=mesh, in_specs=in_specs, out_specs=out_specs, check_vma=False)
```

profile of v0, /device:TPU:25, one launch (start us, length us, event | category | flops | bytes accessed | tf_op | source)
XLA Modules:
  0.0 94.7 jit_solution(7943298621391492195)
XLA Ops:
  0.7 1.2 %fusion.26 = (bf16[2,1,4,64,256]{4,3,2,1,0:T(8,128)(2,1)S(1)}, bf16[2,1,4,64,256]{4,3,2,1,0:T(8,128)(2,1)S(1)}) fusion(bf16[1,2,4,64,256]{4,3,2,1,0:T(8,128)(2,1)} %bitcast.81, bf16[1,2,4,64,256]{4,3,2,1,0:T(8,128)(2,1)} %bitcast.84), kind=kLoop, calls=%fused_computation.43 | loop fusion | flops 262144 | bytes 1048576 | tf_op jit(solution)/shard_map/stack | solution.py:59
  1.9 3.1 %collective-permute-start = (bf16[2,1,4,64,256]{4,3,2,1,0:T(8,128)(2,1)S(1)}, bf16[2,1,4,64,256]{4,3,2,1,0:T(8,128)(2,1)S(1)}, u32[]{:S(2)}, u32[]{:S(2)}) collective-permute-start(bf16[2,1,4,64,256]{4,3,2,1,0:T(8,128)(2,1)S(1)} %get-tuple-element.26), channel_id=1, source_target_pairs={{0,4},{4,8},{8,12},{12,16},{16,20},{20,24},{24,28},{28,32},{32,36}... | collective-permute-start | bytes 786440 | tf_op jit(solution)/shard_map/ppermute | solution.py:15
  5.0 9.2 %collective-permute-start.1 = (bf16[2,1,4,64,256]{4,3,2,1,0:T(8,128)(2,1)S(1)}, bf16[2,1,4,64,256]{4,3,2,1,0:T(8,128)(2,1)S(1)}, u32[]{:S(2)}, u32[]{:S(2)}) collective-permute-start(bf16[2,1,4,64,256]{4,3,2,1,0:T(8,128)(2,1)S(1)} %get-tuple-element.27), channel_id=1, source_target_pairs={{4,0},{8,4},{12,8},{16,12},{20,16},{24,20},{28,24},{32,28},{36,32}... | collective-permute-start | bytes 786440 | tf_op jit(solution)/shard_map/ppermute | solution.py:17
  14.2 4.1 %collective-permute-done = bf16[2,1,4,64,256]{4,3,2,1,0:T(8,128)(2,1)S(1)} collective-permute-done((bf16[2,1,4,64,256]{4,3,2,1,0:T(8,128)(2,1)S(1)}, bf16[2,1,4,64,256]{4,3,2,1,0:T(8,128)(2,1)S(1)}, u32[]{:S(2)}, u32[]{:S(2)}) %collective-permute-start) | collective-permute-done | bytes 262176 | tf_op jit(solution)/shard_map/ppermute | solution.py:15
  19.2 1.0 %pad_maximum_fusion.3 = (bf16[2,4,1,64,256]{4,3,2,1,0:T(8,128)(2,1)S(1)}, bf16[2,4,1,64,256]{4,3,2,1,0:T(8,128)(2,1)S(1)}) fusion(bf16[2,1,4,64,256]{4,3,2,1,0:T(8,128)(2,1)S(1)} %collective-permute-done.1, bf16[2,1,4,64,256]{4,3,2,1,0:T(8,128)(2,1)S(1)} %collective-permute-done, bf16[1,2,4,64,256]{4,3,2,1,0:T(8,128)(2,1)} %bitcast.85, ...), kind=kLoop, calls=%fused_computation.47 | loop fusion | flops 786432 | bytes 1572864 | tf_op jit(solution)/shard_map/slice | solution.py:12
  20.2 1.3 %collective-permute-start.2 = (bf16[2,4,1,64,256]{4,3,2,1,0:T(8,128)(2,1)S(1)}, bf16[2,4,1,64,256]{4,3,2,1,0:T(8,128)(2,1)S(1)}, u32[]{:S(2)}, u32[]{:S(2)}) collective-permute-start(bf16[2,4,1,64,256]{4,3,2,1,0:T(8,128)(2,1)S(1)} %get-tuple-element.24), channel_id=1, source_target_pairs={{0,1},{1,2},{2,3},{4,5},{5,6},{6,7},{8,9},{9,10},{10,11},{12,13},{... | collective-permute-start | bytes 786440 | tf_op jit(solution)/shard_map/ppermute | solution.py:15
  21.5 4.1 %collective-permute-start.3 = (bf16[2,4,1,64,256]{4,3,2,1,0:T(8,128)(2,1)S(1)}, bf16[2,4,1,64,256]{4,3,2,1,0:T(8,128)(2,1)S(1)}, u32[]{:S(2)}, u32[]{:S(2)}) collective-permute-start(bf16[2,4,1,64,256]{4,3,2,1,0:T(8,128)(2,1)S(1)} %get-tuple-element.25), channel_id=1, source_target_pairs={{1,0},{2,1},{3,2},{5,4},{6,5},{7,6},{9,8},{10,9},{11,10},{13,12},{... | collective-permute-start | bytes 786440 | tf_op jit(solution)/shard_map/ppermute | solution.py:17
  25.6 1.1 %collective-permute-done.3 = bf16[2,4,1,64,256]{4,3,2,1,0:T(8,128)(2,1)S(1)} collective-permute-done((bf16[2,4,1,64,256]{4,3,2,1,0:T(8,128)(2,1)S(1)}, bf16[2,4,1,64,256]{4,3,2,1,0:T(8,128)(2,1)S(1)}, u32[]{:S(2)}, u32[]{:S(2)}) %collective-permute-start.3) | collective-permute-done | bytes 262176 | tf_op jit(solution)/shard_map/ppermute | solution.py:17
  27.0 5.6 %copy.49 = bf16[4,6,64,2,256]{2,3,4,1,0:T(2,128)(2,1)} copy(bf16[4,6,64,2,256]{4,2,1,0,3:T(8,128)(2,1)S(1)} %maximum_bitcast_fusion) | data formatting | bytes 3145728
  32.5 5.2 %pad.2.clone = bf16[4,6,64,2,264]{2,3,4,1,0:T(2,128)(2,1)S(1)} pad(bf16[4,6,64,2,256]{2,3,4,1,0:T(2,128)(2,1)} %copy.49, bf16[]{:T(256)} %constant.37), padding=0_0x0_0x0_0x0_0x1_7 | pad | bytes 3194882 | tf_op jit(solution)/shard_map/concatenate | solution.py:13
  37.9 8.8 %fusion.1 = bf16[4,6,64,2,8,35]{2,3,5,4,1,0:T(2,128)(2,1)S(1)} fusion(bf16[4,6,64,2,7,2]{2,3,5,4,1,0:T(2,128)(2,1)S(1)} %slice.42, bf16[4,6,64,2,8,33]{2,3,5,4,1,0:T(2,128)(2,1)S(1)} %bitcast.74), kind=kLoop, calls=%fused_computation.3 | loop fusion | flops 5160960 | bytes 3428352 | tf_op jit(solution)/shard_map/conv_general_dilated | solution.py:25
  46.7 4.3 %fusion.9 = f32[2,4,16,33,64]{4,2,3,1,0:T(8,128)S(1)} fusion(bf16[3,3,3,64,64]{4,3,2,1,0:T(8,128)(2,1)S(1)} %copy-done.3, bf16[4,6,64,2,8,35]{2,3,5,4,1,0:T(2,128)(2,1)S(1)} %fusion.1, pred[16,33]{0,1:T(8,128)(4,1)S(1)} %copy-done.4), kind=kOutput, calls=%fused_computation.13 | convolution fusion | flops 934551552 | bytes 3023376 | tf_op jit(solution)/shard_map/conv_general_dilated | solution.py:25
  51.8 1.5 %slice.43 = f32[2,4,2,256,64]{4,1,3,2,0:T(4,128)} slice(f32[2,4,2,264,64]{4,1,3,2,0:T(4,128)S(1)} %bitcast.77), slice={[0:2], [0:4], [0:2], [0:256], [0:64]} | slice | bytes 2097152 | tf_op jit(solution)/shard_map/conv_general_dilated | solution.py:25
  53.3 1.9 %copy.48 = f32[2,4,2,256,64]{3,4,1,0,2:T(8,128)S(1)} copy(f32[2,4,2,256,64]{4,1,3,2,0:T(4,128)} %slice.43) | data formatting | bytes 2097152
  56.4 2.7 %convert_reduce_fusion = f32[2,2,64,256]{2,1,3,0:T(2,128)S(1)} fusion(bf16[1,1,2,2,2,64,256]{5,4,3,6,2,1,0:T(2,128)(2,1)S(1)} %copy.39, bf16[1,1,2,2,2,64,256]{5,4,3,6,2,1,0:T(2,128)(2,1)S(1)} %copy.38), kind=kLoop, calls=%fused_computation.7 | loop fusion | flops 720896 | bytes 786432 | tf_op jit(solution)/shard_map/reduce_sum | solution.py:48
  59.1 1.1 %convolution_convert_fusion = bf16[2,2,64,128]{3,2,1,0:T(8,128)(2,1)S(1)} fusion(f32[2,2,64,256]{2,1,3,0:T(2,128)S(1)} %convert_reduce_fusion, s32[256]{0:T(256)S(1)} %get-tuple-element.28, s32[256]{0:T(256)S(1)} %get-tuple-element.29, pred[256]{0:T(512)(128)(4,1)S(1)} %compare_and_fusion), kind=kOutput, calls=%fused_computation.15 | convolution fusion | flops 100794368 | bytes 329984 | tf_op jit(solution)/shard_map/dot_general | solution.py:52
  60.2 10.4 %all-gather = bf16[2,8,64,128]{3,2,1,0:T(8,128)(2,1)S(1)} all-gather(bf16[2,2,64,128]{3,2,1,0:T(8,128)(2,1)S(1)} %convolution_convert_fusion), channel_id=2, replica_groups=mesh['wide'=64,'narrow'=4] {'narrow'}, dimensions={1}, use_global_device_ids=true | all-gather | bytes 327680 | tf_op jit(solution)/shard_map/all_gather | solution.py:63
  70.6 1.9 %collective-permute-start.4 = (bf16[2,1,8,64,128]{4,3,2,0,1:T(8,128)(2,1)S(1)}, bf16[2,1,8,64,128]{4,3,2,0,1:T(8,128)(2,1)S(1)}, u32[]{:S(2)}, u32[]{:S(2)}) collective-permute-start(bf16[2,1,8,64,128]{4,3,2,0,1:T(8,128)(2,1)S(1)} %bitcast.89), channel_id=1, source_target_pairs={{0,4},{4,8},{8,12},{12,16},{16,20},{20,24},{24,28},{28,32},{32,36}... | collective-permute-start | bytes 786440 | tf_op jit(solution)/shard_map/ppermute | solution.py:15
  72.5 9.8 %collective-permute-start.5 = (bf16[2,1,8,64,128]{4,3,2,0,1:T(8,128)(2,1)S(1)}, bf16[2,1,8,64,128]{4,3,2,0,1:T(8,128)(2,1)S(1)}, u32[]{:S(2)}, u32[]{:S(2)}) collective-permute-start(bf16[2,1,8,64,128]{4,3,2,0,1:T(8,128)(2,1)S(1)} %bitcast.90), channel_id=1, source_target_pairs={{4,0},{8,4},{12,8},{16,12},{20,16},{24,20},{28,24},{32,28},{36,32}... | collective-permute-start | bytes 786440 | tf_op jit(solution)/shard_map/ppermute | solution.py:17
  82.4 1.0 %fusion.17 = (bf16[2,4,64,256]{3,2,1,0:T(8,128)(2,1)}, bf16[2,4,64,256]{3,2,1,0:T(8,128)(2,1)}) fusion(f32[2,2,4,64,256]{4,3,2,1,0:T(8,128)S(1)} %bitcast.76), kind=kLoop, calls=%fused_computation.26 | loop fusion | flops 1441792 | bytes 1572864 | tf_op jit(solution)/shard_map/convert_element_type | solution.py:39
  83.4 3.6 %collective-permute-done.4 = bf16[2,1,8,64,128]{4,3,2,0,1:T(8,128)(2,1)S(1)} collective-permute-done((bf16[2,1,8,64,128]{4,3,2,0,1:T(8,128)(2,1)S(1)}, bf16[2,1,8,64,128]{4,3,2,0,1:T(8,128)(2,1)S(1)}, u32[]{:S(2)}, u32[]{:S(2)}) %collective-permute-start.4) | collective-permute-done | bytes 262176 | tf_op jit(solution)/shard_map/ppermute | solution.py:15
  87.0 1.0 %collective-permute-done.5 = bf16[2,1,8,64,128]{4,3,2,0,1:T(8,128)(2,1)S(1)} collective-permute-done((bf16[2,1,8,64,128]{4,3,2,0,1:T(8,128)(2,1)S(1)}, bf16[2,1,8,64,128]{4,3,2,0,1:T(8,128)(2,1)S(1)}, u32[]{:S(2)}, u32[]{:S(2)}) %collective-permute-start.5) | collective-permute-done | bytes 262176 | tf_op jit(solution)/shard_map/ppermute | solution.py:17
  88.0 0.9 copy.50
  90.0 2.3 %fusion.12 = f32[1,8,16,17,64]{4,2,3,1,0:T(8,128)S(1)} fusion(bf16[3,8,64,2,8,19]{2,1,5,4,3,0:T(8,128)(2,1)S(1)} %fusion.5, pred[16,17]{0,1:T(8,128)(4,1)S(1)} %copy-done.5, bf16[3,3,3,64,256]{4,3,2,1,0:T(8,128)(2,1)S(1)} %copy-done, s32[]{:T(128)S(6)} %select_n.14), kind=kOutput, calls=%fused_computation.14 | convolution fusion | flops 441327616 | bytes 2870276 | tf_op jit(solution)/shard_map/conv_general_dilated | solution.py:25
  (31 shorter events, 6.8 us)
Async XLA Ops:
  0.6 89.0 %copy-start = (bf16[3,3,3,64,256]{4,3,2,1,0:T(8,128)(2,1)S(1)}, bf16[3,3,3,64,256]{4,3,2,1,0:T(8,128)(2,1)}, u32[]{:S(2)}) copy-start(bf16[3,3,3,64,256]{4,3,2,1,0:T(8,128)(2,1)} %param.7) | copy-start | bytes 2654212
  0.6 26.1 %copy-start.1 = (bf16[2,4,64,256]{3,2,1,0:T(8,128)(2,1)S(1)}, bf16[2,4,64,256]{3,2,1,0:T(8,128)(2,1)}, u32[]{:S(2)}) copy-start(bf16[2,4,64,256]{3,2,1,0:T(8,128)(2,1)} %param.4) | copy-start | bytes 786436
  0.7 26.0 %copy-start.2 = (bf16[2,4,64,256]{3,2,1,0:T(8,128)(2,1)S(1)}, bf16[2,4,64,256]{3,2,1,0:T(8,128)(2,1)}, u32[]{:S(2)}) copy-start(bf16[2,4,64,256]{3,2,1,0:T(8,128)(2,1)} %param.5) | copy-start | bytes 786436
  1.9 16.4 %collective-permute-start = (bf16[2,1,4,64,256]{4,3,2,1,0:T(8,128)(2,1)S(1)}, bf16[2,1,4,64,256]{4,3,2,1,0:T(8,128)(2,1)S(1)}, u32[]{:S(2)}, u32[]{:S(2)}) collective-permute-start(bf16[2,1,4,64,256]{4,3,2,1,0:T(8,128)(2,1)S(1)} %get-tuple-element.26), channel_id=1, source_target_pairs={{0,4},{4,8},{8,12},{12,16},{16,20},{20,24},{24,28},{28,32},{32,36}... | collective-permute-start | bytes 786440 | tf_op jit(solution)/shard_map/ppermute | solution.py:15
  5.0 14.1 %collective-permute-start.1 = (bf16[2,1,4,64,256]{4,3,2,1,0:T(8,128)(2,1)S(1)}, bf16[2,1,4,64,256]{4,3,2,1,0:T(8,128)(2,1)S(1)}, u32[]{:S(2)}, u32[]{:S(2)}) collective-permute-start(bf16[2,1,4,64,256]{4,3,2,1,0:T(8,128)(2,1)S(1)} %get-tuple-element.27), channel_id=1, source_target_pairs={{4,0},{8,4},{12,8},{16,12},{20,16},{24,20},{28,24},{32,28},{36,32}... | collective-permute-start | bytes 786440 | tf_op jit(solution)/shard_map/ppermute | solution.py:17
  20.2 5.4 %collective-permute-start.2 = (bf16[2,4,1,64,256]{4,3,2,1,0:T(8,128)(2,1)S(1)}, bf16[2,4,1,64,256]{4,3,2,1,0:T(8,128)(2,1)S(1)}, u32[]{:S(2)}, u32[]{:S(2)}) collective-permute-start(bf16[2,4,1,64,256]{4,3,2,1,0:T(8,128)(2,1)S(1)} %get-tuple-element.24), channel_id=1, source_target_pairs={{0,1},{1,2},{2,3},{4,5},{5,6},{6,7},{8,9},{9,10},{10,11},{12,13},{... | collective-permute-start | bytes 786440 | tf_op jit(solution)/shard_map/ppermute | solution.py:15
  21.5 5.2 %collective-permute-start.3 = (bf16[2,4,1,64,256]{4,3,2,1,0:T(8,128)(2,1)S(1)}, bf16[2,4,1,64,256]{4,3,2,1,0:T(8,128)(2,1)S(1)}, u32[]{:S(2)}, u32[]{:S(2)}) collective-permute-start(bf16[2,4,1,64,256]{4,3,2,1,0:T(8,128)(2,1)S(1)} %get-tuple-element.25), channel_id=1, source_target_pairs={{1,0},{2,1},{3,2},{5,4},{6,5},{7,6},{9,8},{10,9},{11,10},{13,12},{... | collective-permute-start | bytes 786440 | tf_op jit(solution)/shard_map/ppermute | solution.py:17
  37.8 8.8 %copy-start.3 = (bf16[3,3,3,64,64]{4,3,2,1,0:T(8,128)(2,1)S(1)}, bf16[3,3,3,64,64]{4,3,2,1,0:T(8,128)(2,1)}, u32[]{:S(2)}) copy-start(bf16[3,3,3,64,64]{4,3,2,1,0:T(8,128)(2,1)} %param.6) | copy-start | bytes 663556
  37.8 8.8 %copy-start.4 = (pred[16,33]{0,1:T(8,128)(4,1)S(1)}, pred[16,33]{0,1:T(8,128)(4,1)}, u32[]{:S(2)}) copy-start(pred[16,33]{0,1:T(8,128)(4,1)} %constant.45) | copy-start | bytes 1588
  70.6 16.3 %collective-permute-start.4 = (bf16[2,1,8,64,128]{4,3,2,0,1:T(8,128)(2,1)S(1)}, bf16[2,1,8,64,128]{4,3,2,0,1:T(8,128)(2,1)S(1)}, u32[]{:S(2)}, u32[]{:S(2)}) collective-permute-start(bf16[2,1,8,64,128]{4,3,2,0,1:T(8,128)(2,1)S(1)} %bitcast.89), channel_id=1, source_target_pairs={{0,4},{4,8},{8,12},{12,16},{16,20},{20,24},{24,28},{28,32},{32,36}... | collective-permute-start | bytes 786440 | tf_op jit(solution)/shard_map/ppermute | solution.py:15
  72.5 15.4 %collective-permute-start.5 = (bf16[2,1,8,64,128]{4,3,2,0,1:T(8,128)(2,1)S(1)}, bf16[2,1,8,64,128]{4,3,2,0,1:T(8,128)(2,1)S(1)}, u32[]{:S(2)}, u32[]{:S(2)}) collective-permute-start(bf16[2,1,8,64,128]{4,3,2,0,1:T(8,128)(2,1)S(1)} %bitcast.90), channel_id=1, source_target_pairs={{4,0},{8,4},{12,8},{16,12},{20,16},{24,20},{28,24},{32,28},{36,32}... | collective-permute-start | bytes 786440 | tf_op jit(solution)/shard_map/ppermute | solution.py:17
  89.3 0.7 copy-start.5
where the time goes:
time: 95.4 us; the launch traced here: 94.7 us
  starting transfers between devices  29.4 us (31%)
  local copies, waits for them, and re-layouts  19.8 us (21%)
  other arithmetic  16 us (17%)
  waiting for transfers between devices  10.6 us (11%)
  blocking collectives  10.4 us (11%)
  matrix products  7.68 us (8%)
    ppermute x3, starting transfers between devices, with_halo(): lax.ppermute(head, axis, [((i + 1) % count, i) for i in range(ends)])  23.1 us
    unnamed x17, local copies, waits for them, and re-layouts  10.4 us
    all_gather x1, blocking collectives, local(): whole_y = lax.all_gather(pooled, 'narrow', axis=2, tiled=True)  10.4 us
    conv_general_dilated x2, other arithmetic, conv_taps(): lax.conv_general_dilated(padded, weight, (1, 1, 1), ((0, 0), (0, 0), (1,...  9.18 us
    ppermute x3, waiting for transfers between devices, with_halo(): lax.ppermute(tail, axis, [(i, (i + 1) % count) for i in range(ends)])  7.64 us
    conv_general_dilated x2, matrix products, conv_taps(): lax.conv_general_dilated(padded, weight, (1, 1, 1), ((0, 0), (0, 0), (1,...  6.56 us
    ppermute x3, starting transfers between devices, with_halo(): lax.ppermute(tail, axis, [(i, (i + 1) % count) for i in range(ends)])  6.32 us
    concatenate x2, local copies, waits for them, and re-layouts, with_halo(): jnp.concatenate([lax.ppermute(tail, axis, [(i, (i + 1) % count) for i in...  5.48 us
  transfers between devices with their start and end apart: 6, of which 5 were waited for; matrix products, arithmetic and copies ran while one was open for 1% of the time, Pallas kernels for 0%

commit v1 on v0

v1 whole, which is shorter than its diff:
```python
import functools

import jax
import jax.numpy as jnp
from jax import lax
from jax.experimental import pallas as pl
from jax.experimental.pallas import tpu as pltpu
from jax.sharding import PartitionSpec as P

BOTH = ("wide", "narrow")
BF16 = jnp.bfloat16
F32 = jnp.float32
ANY = pl.BlockSpec(memory_space=pl.ANY)
VMEM = pl.BlockSpec(memory_space=pltpu.VMEM)


def exchange(wide, narrow, kind, route):
    pairs = []
    for w in range(wide):
        for n in range(narrow):
            if kind == "E":
                pw = w ^ 1
            elif kind == "O":
                pw = w + 1 if w % 2 else w - 1
            else:
                pw = w
            if not 0 <= pw < wide:
                pw, pn = w, n ^ 1
            elif route == "same" or (route == "near" and min(w, pw) != wide // 2 - 1):
                pn = n
            elif route == "core":
                pn = n ^ 1
            elif route == "mirror":
                pn = narrow - 1 - n
            else:
                pn = n ^ 2
            pairs.append((w * narrow + n, pw * narrow + pn))
    return pairs


def start_copies(copies, sems):
    for k, (cond, src, dst) in enumerate(copies):
        copy = pltpu.make_async_copy(src, dst, sems.at[k])
        if cond is None:
            copy.start()
        else:
            pl.when(cond)(copy.start)


def wait_copies(copies, sems):
    for k, (cond, src, dst) in enumerate(copies):
        copy = pltpu.make_async_copy(src, dst, sems.at[k])
        if cond is None:
            copy.wait()
        else:
            pl.when(cond)(copy.wait)


def slices_kernel(vol, tan, s_o, s_e, s_c, s_m, s_do, s_de, sems):
    w, n = lax.axis_index("wide"), lax.axis_index("narrow")
    last = vol.shape[1] - 1
    odd = lax.rem(w, 2)
    row_c = jnp.where(lax.rem(n, 2) == 0, last, 0)
    row_m = jnp.where(n < 2, last, 0)
    copies = []
    for t, src in enumerate((vol, tan)):
        copies.append((None, src.at[odd], s_o.at[t]))
    for t, src in enumerate((vol, tan)):
        copies.append((None, src.at[odd, row_m], s_do.at[t]))
        copies.append((None, src.at[1 - odd], s_e.at[t]))
        copies.append((None, src.at[1 - odd, row_m], s_de.at[t]))
        copies.append((None, src.at[:, row_c], s_c.at[t]))
        copies.append((None, src.at[:, row_m], s_m.at[t]))
    start_copies(copies, sems)
    wait_copies(copies, sems)


def weights_kernel(sw, dw, t_s, t_d, dw_half, band, dband, sem):
    n = lax.axis_index("narrow")
    copy = pltpu.make_async_copy(
        dw.at[:, :, :, :, pl.ds(pl.multiple_of((n // 2) * 128, 128), 128)], dw_half, sem
    )
    copy.start()
    band[...] = jnp.zeros_like(band)
    dband[...] = jnp.zeros_like(dband)
    nt = (((1,), (1,)), ((), ()))

    def build(source, scratch, pick, out):
        for a in range(3):
            for c in range(3):
                for b in range(3):
                    scratch[a * 3 + c, 64 * (b + 1) : 64 * (b + 2), :] = source[a, b, c]
                for r in range(2):
                    rows = scratch[a * 3 + c, 64 * (1 - r) : 64 * (1 - r) + 256, :]
                    placed = lax.dot_general(pick, rows, nt, preferred_element_type=F32)
                    out[c * 128 + r * 64 : c * 128 + r * 64 + 64, a * 256 : a * 256 + 256] = (
                        placed.astype(BF16)
                    )

    def selector(width, shift):
        row = lax.broadcasted_iota(jnp.int32, (64, width), 0)
        col = lax.broadcasted_iota(jnp.int32, (64, width), 1)
        return jnp.where(col == row + shift, 1.0, 0.0).astype(BF16)

    build(sw, band, selector(64, 0), t_s)
    copy.wait()
    build(dw_half, dband, selector(128, 64 * lax.rem(n, 2)), t_d)


def shifted_sum(acc, lane, first, final):
    left = pltpu.roll(acc[0:128], 1, 1)
    right = pltpu.roll(acc[256:384], acc.shape[1] - 1, 1)
    return acc[128:256] + jnp.where(first(lane), 0.0, left) + jnp.where(final(lane), 0.0, right)


def activate(pre, dot):
    s = 0.5 * jnp.tanh(0.5 * pre) + 0.5
    primal = (pre * s).astype(BF16)
    tangent = (s * (1.0 + pre * (1.0 - s)) * dot).astype(BF16)
    return primal, tangent


def shallow_kernel(wide, narrow, vol, tan, r_o, r_e, r_c, r_m, c_o, c_e, d_o, d_e, t_s,
                   skip_f, skip_t, pooled, x, sems):
    w, n = lax.axis_index("wide"), lax.axis_index("narrow")
    odd = lax.rem(w, 2)
    rows = vol.shape[1]
    plane_o, plane_e = 3 * odd, 3 * (1 - odd)
    slot_c = jnp.where(lax.rem(n, 2) == 0, rows + 1, 0)
    slot_m = jnp.where(lax.rem(n, 2) == 0, 0, rows + 1)
    has_o = (w > 0) & (w < wide - 1)
    has_m = (n > 0) & (n < narrow - 1)
    both = has_o & has_m
    copies = []
    for t, src in enumerate((vol, tan)):
        copies += [
            (None, src, x.at[t, pl.ds(1, 2), pl.ds(1, rows)]),
            (None, r_c.at[t], x.at[t, pl.ds(1, 2), slot_c]),
            (has_m, r_m.at[t], x.at[t, pl.ds(1, 2), slot_m]),
            (None, r_e.at[t], x.at[t, plane_e, pl.ds(1, rows)]),
            (None, c_e.at[t], x.at[t, plane_e, slot_c]),
            (has_m, d_e.at[t], x.at[t, plane_e, slot_m]),
            (has_o, r_o.at[t], x.at[t, plane_o, pl.ds(1, rows)]),
            (has_o, c_o.at[t], x.at[t, plane_o, slot_c]),
            (both, d_o.at[t], x.at[t, plane_o, slot_m]),
        ]
    start_copies(copies, sems)

    @pl.when(jnp.logical_not(has_o))
    def _():
        for t in range(2):
            x[t, plane_o] = jnp.zeros(x.shape[2:], BF16)

    @pl.when(jnp.logical_not(has_m))
    def _():
        for t in range(2):
            for p in range(4):
                x[t, p, slot_m] = jnp.zeros(x.shape[3:], BF16)

    cells = vol.shape[3]
    lane = lax.broadcasted_iota(jnp.int32, (128, cells), 1)
    first, final = (lambda v: v == 0), (lambda v: v == cells - 1)
    source = lax.broadcasted_iota(jnp.int32, (cells, cells // 2), 0)
    target = lax.broadcasted_iota(jnp.int32, (cells, cells // 2), 1)
    pairing = jnp.where(source // 2 == target, 0.125, 0.0).astype(BF16)
    wait_copies(copies, sems)
    for win in range(rows // 2):
        sums = [None, None]
        for q in range(2):
            pre = []
            for t in range(2):
                stack = jnp.concatenate(
                    [x[t, q + a, 2 * win : 2 * win + 4].reshape(256, cells) for a in range(3)], axis=0
                )
                acc = jnp.dot(t_s[...], stack, preferred_element_type=F32)
                pre.append(shifted_sum(acc, lane, first, final))
            out = activate(*pre)
            for t, ref in enumerate((skip_f, skip_t)):
                ref[q, 2 * win : 2 * win + 2] = out[t].reshape(2, 64, cells)
                half = jnp.dot(out[t], pairing, preferred_element_type=F32)
                half = half[0:64] + half[64:128]
                sums[t] = half if sums[t] is None else sums[t] + half
        pooled[win] = jnp.concatenate(sums, axis=1).astype(BF16)


def deep_kernel(wide, narrow, own, other, g_c, r_o, r_e, o_c, e_c, t_d, out_f, out_t, x, sems):
    w, n = lax.axis_index("wide"), lax.axis_index("narrow")
    odd = lax.rem(w, 2)
    plane_o, plane_e = 2 * odd, 2 * (1 - odd)
    has_o = (w > 0) & (w < wide - 1)
    far = (w == wide // 2 - 1) | (w == wide // 2)
    core = lax.rem(n, 2)
    across = lax.rem(n + 2, narrow)
    sib = n + 1 - 2 * core
    sib_across = lax.rem(sib + 2, narrow)
    pair = own.shape[0]

    def place(plane, member):
        return x.at[plane, pl.ds(member * pair + 1, pair)]

    o_0, o_1 = jnp.where(far, across, n), jnp.where(far, n, across)
    oc_0, oc_1 = jnp.where(far, sib_across, sib), jnp.where(far, sib, sib_across)
    copies = [
        (None, own, place(1, n)),
        (None, other, place(1, across)),
        (None, g_c.at[0], place(1, sib)),
        (None, g_c.at[1], place(1, sib_across)),
        (None, r_e.at[0], place(plane_e, n)),
        (None, r_e.at[1], place(plane_e, across)),
        (None, e_c.at[0], place(plane_e, sib)),
        (None, e_c.at[1], place(plane_e, sib_across)),
        (has_o, r_o.at[0], place(plane_o, o_0)),
        (has_o, r_o.at[1], place(plane_o, o_1)),
        (has_o, o_c.at[0], place(plane_o, oc_0)),
        (has_o, o_c.at[1], place(plane_o, oc_1)),
    ]
    start_copies(copies, sems)
    rows = narrow * pair
    for p in range(3):
        x[p, 0] = jnp.zeros(x.shape[2:], BF16)
        x[p, rows + 1] = jnp.zeros(x.shape[2:], BF16)

    @pl.when(jnp.logical_not(has_o))
    def _():
        x[plane_o] = jnp.zeros(x.shape[1:], BF16)

    cells = own.shape[2] // 2
    lane = lax.broadcasted_iota(jnp.int32, (128, 2 * cells), 1)
    first = lambda v: (v == 0) | (v == cells)
    final = lambda v: (v == cells - 1) | (v == 2 * cells - 1)
    wait_copies(copies, sems)
    for j in range(rows // 2):
        stack = jnp.concatenate(
            [x[a, 2 * j : 2 * j + 4].reshape(256, 2 * cells) for a in range(3)], axis=0
        )
        acc = jnp.dot(t_d[...], stack, preferred_element_type=F32)
        both = shifted_sum(acc, lane, first, final)
        primal, tangent = activate(both[:, :cells], both[:, cells:])
        out_f[0, 2 * j : 2 * j + 2] = primal.reshape(2, 64, cells)
        out_t[0, 2 * j : 2 * j + 2] = tangent.reshape(2, 64, cells)


def call(body, outs, in_specs, out_specs, scratch, flops=0, nbytes=0):
    return pl.pallas_call(
        body,
        out_shape=[jax.ShapeDtypeStruct(s, BF16) for s in outs],
        in_specs=in_specs,
        out_specs=out_specs,
        scratch_shapes=scratch,
        compiler_params=pltpu.CompilerParams(vmem_limit_bytes=32 * 1024 * 1024),
        cost_estimate=pl.CostEstimate(flops=flops, bytes_accessed=nbytes, transcendentals=0),
    )


def local(wide, narrow, volume, volume_tangent, shallow_weight, deep_weight):
    planes, rows, chans, cells = volume.shape
    n = lax.axis_index("narrow")

    def swap(v, kind, route):
        return lax.ppermute(v, BOTH, exchange(wide, narrow, kind, route))

    face, edge, corner = (2, rows, chans, cells), (2, planes, chans, cells), (2, chans, cells)
    s_o, s_e, s_c, s_m, s_do, s_de = call(
        slices_kernel, [face, face, edge, edge, corner, corner], [ANY] * 2, [ANY] * 6,
        [pltpu.SemaphoreType.DMA((12,))], nbytes=2 << 20,
    )(volume, volume_tangent)
    r_o = swap(s_o, "O", "same")
    d_o = swap(s_do, "O", "mirror")
    r_e = swap(s_e, "E", "same")
    d_e = swap(s_de, "E", "mirror")
    r_c = swap(s_c, "", "core")
    r_m = swap(s_m, "", "mirror")
    band = (384, 768)
    t_s, t_d = call(
        weights_kernel, [band, band], [VMEM, ANY], [VMEM, VMEM],
        [
            pltpu.VMEM((3, 3, 3, 64, 128), BF16),
            pltpu.VMEM((9, 320, 64), BF16),
            pltpu.VMEM((9, 320, 128), BF16),
            pltpu.SemaphoreType.DMA,
        ],
        flops=10**8, nbytes=2 << 20,
    )(shallow_weight, deep_weight)
    row_c = jnp.where(n % 2 == 0, rows - 1, 0)
    c_e = swap(lax.dynamic_index_in_dim(r_e, row_c, 1, keepdims=False), "", "core")
    c_o = swap(lax.dynamic_index_in_dim(r_o, row_c, 1, keepdims=False), "", "core")
    skip_f, skip_t, pooled = call(
        functools.partial(shallow_kernel, wide, narrow),
        [volume.shape, volume.shape, (rows // 2, chans, cells)],
        [ANY] * 10 + [VMEM], [VMEM] * 3,
        [pltpu.VMEM((2, planes + 2, rows + 2, chans, cells), BF16), pltpu.SemaphoreType.DMA((18,))],
        flops=12 * 10**8, nbytes=4 << 20,
    )(volume, volume_tangent, r_o, r_e, r_c, r_m, c_o, c_e, d_o, d_e, t_s)
    other = swap(pooled, "", "across")
    group = jnp.stack([pooled, other])
    o2 = swap(group, "O", "near")
    e2 = swap(group, "E", "same")
    g_c = swap(group, "", "core")
    e_c = swap(e2, "", "core")
    o_c = swap(o2, "", "core")
    deep_shape = (1, rows // 2 * narrow, 64, cells // 2)
    deep_f, deep_t = call(
        functools.partial(deep_kernel, wide, narrow),
        [deep_shape, deep_shape],
        [ANY] * 7 + [VMEM], [VMEM] * 2,
        [
            pltpu.VMEM((3, rows // 2 * narrow + 2, chans, cells), BF16),
            pltpu.SemaphoreType.DMA((12,)),
        ],
        flops=6 * 10**8, nbytes=3 << 20,
    )(pooled, other, g_c, o2, e2, o_c, e_c, t_d)
    return skip_f, skip_t, deep_f, deep_t


def solution(mesh):
    wide, narrow = mesh.shape["wide"], mesh.shape["narrow"]
    in_specs = (P("wide", "narrow", None, None), P("wide", "narrow", None, None), P(), P())
    out_specs = (
        P("wide", "narrow", None, None),
        P("wide", "narrow", None, None),
        P("wide", None, "narrow", None),
        P("wide", None, "narrow", None),
    )
    return jax.shard_map(
        functools.partial(local, wide, narrow), mesh=mesh, in_specs=in_specs, out_specs=out_specs,
        check_vma=False,
    )
```

time: 95.4 us -> 49.4 us (0.52)
  local copies, waits for them, and re-layouts: 19.8 us -> 3.08 us
  other arithmetic: 16 us -> 0.01 us
  blocking collectives: 10.4 us -> 0 us
  Pallas kernels: 0 us -> 9.48 us
  matrix products: 7.68 us -> 0 us
  starting transfers between devices: 29.4 us -> 25.4 us
    all_gather x1 -> x0, blocking collectives: 10.4 us -> none  [local(): whole_y = lax.all_gather(pooled, 'narrow', axis=2, tiled=True)]
    pallas_call x0 -> x4, Pallas kernels: none -> 9.48 us  [the longest x1 4.26 us: local(): call(functools.partial(shallow_kernel, wide, narrow), [volume.shape, volu...]
    conv_general_dilated x2 -> x0, other arithmetic: 9.18 us -> none  [conv_taps(): lax.conv_general_dilated(padded, weight, (1, 1, 1), ((0, 0), (0, 0), (1,...]
    unnamed x17 -> x12, local copies, waits for them, and re-layouts: 10.4 us -> 3.07 us
    conv_general_dilated x2 -> x0, matrix products: 6.56 us -> none  [conv_taps(): lax.conv_general_dilated(padded, weight, (1, 1, 1), ((0, 0), (0, 0), (1,...]
    concatenate x2 -> x0, local copies, waits for them, and re-layouts: 5.48 us -> none  [with_halo(): jnp.concatenate([lax.ppermute(tail, axis, [(i, (i + 1) % count) for i in...]
    ppermute x6 -> x14, starting transfers between devices: 29.4 us -> 25.4 us  [swap(): return lax.ppermute(v, BOTH, exchange(wide, narrow, kind, route))]
    conv_general_dilated x6 -> x0, local copies, waits for them, and re-layouts: 2.94 us -> none  [conv_taps(): lax.conv_general_dilated(padded, weight, (1, 1, 1), ((0, 0), (0, 0), (1,...]
  transfers between devices with their start and end apart: 6 -> 14, of which waited for: 5 -> 5; matrix products, arithmetic and copies ran while one was open for 1% -> 0% of each run, Pallas kernels for 0% -> 3%
where the time goes in v1:
time: 49.4 us; the launch traced here: 49.3 us
  starting transfers between devices  25.4 us (51%)
  waiting for transfers between devices  10.5 us (21%)
  Pallas kernels  9.48 us (19%)
  local copies, waits for them, and re-layouts  3.08 us (6%)
  between operations  0.75 us (2%)
    ppermute x14, starting transfers between devices, swap(): return lax.ppermute(v, BOTH, exchange(wide, narrow, kind, route))  25.4 us
    ppermute x14, waiting for transfers between devices, swap(): return lax.ppermute(v, BOTH, exchange(wide, narrow, kind, route))  10.5 us
    pallas_call x1, Pallas kernels, local(): call(functools.partial(shallow_kernel, wide, narrow), [volume.shape, volu...  4.26 us
    unnamed x12, local copies, waits for them, and re-layouts  3.07 us
    pallas_call x1, Pallas kernels, local(): call(functools.partial(deep_kernel, wide, narrow), [deep_shape, deep_shap...  2.74 us
    pallas_call x1, Pallas kernels, local(): call(weights_kernel, [band, band], [VMEM, ANY], [VMEM, VMEM], [pltpu.VMEM...  1.35 us
    pallas_call x1, Pallas kernels, local(): call(slices_kernel, [face, face, edge, edge, corner, corner], [ANY] * 2,...  1.12 us
  transfers between devices with their start and end apart: 14, of which 5 were waited for; matrix products, arithmetic and copies ran while one was open for 0% of the time, Pallas kernels for 3%

profile of v1, /device:TPU:25, one launch (start us, length us, event | category | flops | bytes accessed | tf_op | source)
XLA Modules:
  0.0 49.3 jit_solution(12226308007214865033)
XLA Ops:
  0.6 0.0 copy-start.2
  0.6 0.9 %copy-done.2 = bf16[2,4,64,256]{3,2,1,0:T(8,128)(2,1)S(1)} copy-done((bf16[2,4,64,256]{3,2,1,0:T(8,128)(2,1)S(1)}, bf16[2,4,64,256]{3,2,1,0:T(8,128)(2,1)}, u32[]{:S(2)}) %copy-start.2) | copy-done | bytes 262168
  1.6 0.9 %copy-done.4 = bf16[2,4,64,256]{3,2,1,0:T(8,128)(2,1)S(1)} copy-done((bf16[2,4,64,256]{3,2,1,0:T(8,128)(2,1)S(1)}, bf16[2,4,64,256]{3,2,1,0:T(8,128)(2,1)}, u32[]{:S(2)}) %copy-start.4) | copy-done | bytes 262168
  2.5 1.1 %shard_map.75 = (bf16[2,4,64,256]{3,2,1,0:T(8,128)(2,1)S(1)}, bf16[2,4,64,256]{3,2,1,0:T(8,128)(2,1)S(1)}, bf16[2,2,64,256]{3,2,1,0:T(8,128)(2,1)S(1)}, bf16[2,2...) custom-call(bf16[2,4,64,256]{3,2,1,0:T(8,128)(2,1)S(1)} %copy-done.2, ...), custom_call_target="tpu_custom_call" | custom-call | bytes 2097152 | tf_op jit(solution)/shard_map/pallas_call | solution.py:263
  3.7 8.5 %collective-permute-start = (bf16[2,4,64,256]{3,2,1,0:T(8,128)(2,1)S(1)}, bf16[2,4,64,256]{3,2,1,0:T(8,128)(2,1)S(1)}, u32[]{:S(2)}, u32[]{:S(2)}) collective-permute-start(bf16[2,4,64,256]{3,2,1,0:T(8,128)(2,1)S(1)} %get-tuple-element.17), channel_id=1, source_target_pairs={{0,1},{1,0},{2,3},{3,2},{4,8},{5,9},{6,10},{7,11},{8,4},{9,5},{10,... | collective-permute-start | bytes 786440 | tf_op jit(solution)/shard_map/ppermute | solution.py:260
  12.2 0.9 %collective-permute-start.6 = (bf16[2,64,256]{2,1,0:T(8,128)(2,1)S(1)}, bf16[2,64,256]{2,1,0:T(8,128)(2,1)S(1)}, u32[]{:S(2)}, u32[]{:S(2)}) collective-permute-start(bf16[2,64,256]{2,1,0:T(8,128)(2,1)S(1)} %get-tuple-element.21), channel_id=1, source_target_pairs={{0,1},{1,0},{2,3},{3,2},{4,11},{5,10},{6,9},{7,8},{8,7},{9,6},{10,... | collective-permute-start | bytes 196616 | tf_op jit(solution)/shard_map/ppermute | solution.py:260
  13.1 1.0 %collective-permute-start.7 = (bf16[2,64,256]{2,1,0:T(8,128)(2,1)S(1)}, bf16[2,64,256]{2,1,0:T(8,128)(2,1)S(1)}, u32[]{:S(2)}, u32[]{:S(2)}) collective-permute-start(bf16[2,64,256]{2,1,0:T(8,128)(2,1)S(1)} %get-tuple-element.22), channel_id=1, source_target_pairs={{0,7},{1,6},{2,5},{3,4},{4,3},{5,2},{6,1},{7,0},{8,15},{9,14},{10,... | collective-permute-start | bytes 196616 | tf_op jit(solution)/shard_map/ppermute | solution.py:260
  14.1 4.9 %collective-permute-done.r_o = bf16[2,4,64,256]{3,2,1,0:T(8,128)(2,1)S(1)} collective-permute-done((bf16[2,4,64,256]{3,2,1,0:T(8,128)(2,1)S(1)}, bf16[2,4,64,256]{3,2,1,0:T(8,128)(2,1)S(1)}, u32[]{:S(2)}, u32[]{:S(2)}) %collective-permute-start) | collective-permute-done | bytes 262176 | tf_op jit(solution)/shard_map/ppermute | solution.py:260
  19.0 1.4 %collective-permute-start.3 = (bf16[2,2,64,256]{3,2,1,0:T(8,128)(2,1)S(1)}, bf16[2,2,64,256]{3,2,1,0:T(8,128)(2,1)S(1)}, u32[]{:S(2)}, u32[]{:S(2)}) collective-permute-start(bf16[2,2,64,256]{3,2,1,0:T(8,128)(2,1)S(1)} %get-tuple-element.20), channel_id=1, source_target_pairs={{0,3},{1,2},{2,1},{3,0},{4,7},{5,6},{6,5},{7,4},{8,11},{9,10},{10,... | collective-permute-start | bytes 393224 | tf_op jit(solution)/shard_map/ppermute | solution.py:260
  20.4 1.2 %collective-permute-start.4 = (bf16[2,64,256]{2,1,0:T(8,128)(2,1)S(1)}, bf16[2,64,256]{2,1,0:T(8,128)(2,1)S(1)}, u32[]{:S(2)}, u32[]{:S(2)}) collective-permute-start(bf16[2,64,256]{2,1,0:T(8,128)(2,1)S(1)} %dynamic-slice_bitcast_fusion.1), channel_id=1, source_target_pairs={{0,1},{1,0},{2,3},{3,2},{4,5},{5,4},{6,7},{7,6},{8,9},{9,8},{10,11... | collective-permute-start | bytes 196616 | tf_op jit(solution)/shard_map/ppermute | solution.py:260
  21.6 0.4 collective-permute-done.6.d_o
  22.0 0.7 %collective-permute-start.5 = (bf16[2,64,256]{2,1,0:T(8,128)(2,1)S(1)}, bf16[2,64,256]{2,1,0:T(8,128)(2,1)S(1)}, u32[]{:S(2)}, u32[]{:S(2)}) collective-permute-start(bf16[2,64,256]{2,1,0:T(8,128)(2,1)S(1)} %dynamic-slice_bitcast_fusion), channel_id=1, source_target_pairs={{0,1},{1,0},{2,3},{3,2},{4,5},{5,4},{6,7},{7,6},{8,9},{9,8},{10,11... | collective-permute-start | bytes 196616 | tf_op jit(solution)/shard_map/ppermute | solution.py:260
  22.7 1.2 %copy-done = bf16[3,3,3,64,256]{4,3,2,1,0:T(8,128)(2,1)S(1)} copy-done((bf16[3,3,3,64,256]{4,3,2,1,0:T(8,128)(2,1)S(1)}, bf16[3,3,3,64,256]{4,3,2,1,0:T(8,128)(2,1)}, u32[]{:S(2)}) %copy-start) | copy-done | bytes 884760
  23.9 1.4 %shard_map.76 = (bf16[384,768]{1,0:T(8,128)(2,1)S(1)}, bf16[384,768]{1,0:T(8,128)(2,1)S(1)}) custom-call(bf16[3,3,3,64,64]{4,3,2,1,0:T(8,128)(2,1)S(1)} %copy-done.1, bf16[3,3,3,64,256]{4,3,2,1,0:T(8,128)(2,1)S(1)} %copy-done), custom_call_target="tpu_custom_call" | custom-call | flops 100000000 | bytes 2097152 | tf_op jit(solution)/shard_map/pallas_call | solution.py:274
  25.3 4.3 %shard_map.77 = (bf16[2,4,64,256]{3,2,1,0:T(8,128)(2,1)}, bf16[2,4,64,256]{3,2,1,0:T(8,128)(2,1)}, bf16[2,64,256]{2,1,0:T(8,128)(2,1)S(1)}) custom-call(bf16[2,4,64,256]{3,2,1,0:T(8,128)(2,1)S(1)} %copy-done.3, bf16[2,4,64,256]{3,2,1,0:T(8,128)(2,1)S(1)} %copy-done.5, bf16[2,4,64,256]{3,2,1,0:T(8,128)(2,1)S(1)} %collective-permute-done.r_o, ...), custom_call_target="tpu_custom_call" | custom-call | flops 1200000000 | bytes 4194304 | tf_op jit(solution)/shard_map/pallas_call | solution.py:287
  29.6 0.7 %collective-permute-start.8 = (bf16[2,64,256]{2,1,0:T(8,128)(2,1)S(1)}, bf16[2,64,256]{2,1,0:T(8,128)(2,1)S(1)}, u32[]{:S(2)}, u32[]{:S(2)}) collective-permute-start(bf16[2,64,256]{2,1,0:T(8,128)(2,1)S(1)} %get-tuple-element.26.own), channel_id=1, source_target_pairs={{0,2},{1,3},{2,0},{3,1},{4,6},{5,7},{6,4},{7,5},{8,10},{9,11},{10,... | collective-permute-start | bytes 196616 | tf_op jit(solution)/shard_map/ppermute | solution.py:260
  30.3 2.5 %collective-permute-done.8.other = bf16[2,64,256]{2,1,0:T(8,128)(2,1)S(1)} collective-permute-done((bf16[2,64,256]{2,1,0:T(8,128)(2,1)S(1)}, bf16[2,64,256]{2,1,0:T(8,128)(2,1)S(1)}, u32[]{:S(2)}, u32[]{:S(2)}) %collective-permute-start.8) | collective-permute-done | bytes 65568 | tf_op jit(solution)/shard_map/ppermute | solution.py:260
  32.8 0.1 collective-permute-start.11
  32.9 8.2 %collective-permute-start.10 = (bf16[2,2,64,256]{3,2,1,0:T(8,128)(2,1)S(1)}, bf16[2,2,64,256]{3,2,1,0:T(8,128)(2,1)S(1)}, u32[]{:S(2)}, u32[]{:S(2)}) collective-permute-start(bf16[2,2,64,256]{3,2,1,0:T(8,128)(2,1)S(1)} %pad_maximum_fusion), channel_id=1, source_target_pairs={{0,1},{1,0},{2,3},{3,2},{4,8},{5,9},{6,10},{7,11},{8,4},{9,5},{10,... | collective-permute-start | bytes 393224 | tf_op jit(solution)/shard_map/ppermute | solution.py:260
  41.1 1.2 %collective-permute-start.9 = (bf16[2,2,64,256]{3,2,1,0:T(8,128)(2,1)S(1)}, bf16[2,2,64,256]{3,2,1,0:T(8,128)(2,1)S(1)}, u32[]{:S(2)}, u32[]{:S(2)}) collective-permute-start(bf16[2,2,64,256]{3,2,1,0:T(8,128)(2,1)S(1)} %pad_maximum_fusion), channel_id=1, source_target_pairs={{0,1},{1,0},{2,3},{3,2},{4,5},{5,4},{6,7},{7,6},{8,9},{9,8},{10,11... | collective-permute-start | bytes 393224 | tf_op jit(solution)/shard_map/ppermute | solution.py:260
  42.3 1.7 %collective-permute-done.10.r_o = bf16[2,2,64,256]{3,2,1,0:T(8,128)(2,1)S(1)} collective-permute-done((bf16[2,2,64,256]{3,2,1,0:T(8,128)(2,1)S(1)}, bf16[2,2,64,256]{3,2,1,0:T(8,128)(2,1)S(1)}, u32[]{:S(2)}, u32[]{:S(2)}) %collective-permute-start.10) | collective-permute-done | bytes 131104 | tf_op jit(solution)/shard_map/ppermute | solution.py:260
  44.0 1.6 %collective-permute-start.12 = (bf16[2,2,64,256]{3,2,1,0:T(8,128)(2,1)S(1)}, bf16[2,2,64,256]{3,2,1,0:T(8,128)(2,1)S(1)}, u32[]{:S(2)}, u32[]{:S(2)}) collective-permute-start(bf16[2,2,64,256]{3,2,1,0:T(8,128)(2,1)S(1)} %collective-permute-done.10.r_o), channel_id=1, source_target_pairs={{0,1},{1,0},{2,3},{3,2},{4,5},{5,4},{6,7},{7,6},{8,9},{9,8},{10,11... | collective-permute-start | bytes 393224 | tf_op jit(solution)/shard_map/ppermute | solution.py:260
  45.5 1.0 %collective-permute-done.12.o_c = bf16[2,2,64,256]{3,2,1,0:T(8,128)(2,1)S(1)} collective-permute-done((bf16[2,2,64,256]{3,2,1,0:T(8,128)(2,1)S(1)}, bf16[2,2,64,256]{3,2,1,0:T(8,128)(2,1)S(1)}, u32[]{:S(2)}, u32[]{:S(2)}) %collective-permute-start.12) | collective-permute-done | bytes 131104 | tf_op jit(solution)/shard_map/ppermute | solution.py:260
  46.5 2.7 %shard_map.78 = (bf16[1,8,64,128]{3,2,1,0:T(8,128)(2,1)}, bf16[1,8,64,128]{3,2,1,0:T(8,128)(2,1)}) custom-call(bf16[2,64,256]{2,1,0:T(8,128)(2,1)S(1)} %get-tuple-element.26.own, bf16[2,64,256]{2,1,0:T(8,128)(2,1)S(1)} %collective-permute-done.8.other, bf16[2,2,64,256]{3,2,1,0:T(8,128)(2,1)S(1)} %collective-permute-done.9.g_c, ...), custom_call_target="tpu_custom_call" | custom-call | flops 600000000 | bytes 3145728 | tf_op jit(solution)/shard_map/pallas_call | solution.py:302
  (23 shorter events, 0.1 us)
Async XLA Ops:
  0.6 1.0 %copy-start.2 = (bf16[2,4,64,256]{3,2,1,0:T(8,128)(2,1)S(1)}, bf16[2,4,64,256]{3,2,1,0:T(8,128)(2,1)}, u32[]{:S(2)}) copy-start(bf16[2,4,64,256]{3,2,1,0:T(8,128)(2,1)} %vol.3) | copy-start | bytes 786436
  1.6 0.9 %copy-start.4 = (bf16[2,4,64,256]{3,2,1,0:T(8,128)(2,1)S(1)}, bf16[2,4,64,256]{3,2,1,0:T(8,128)(2,1)}, u32[]{:S(2)}) copy-start(bf16[2,4,64,256]{3,2,1,0:T(8,128)(2,1)} %tan.3) | copy-start | bytes 786436
  2.5 20.2 %copy-start.1 = (bf16[3,3,3,64,64]{4,3,2,1,0:T(8,128)(2,1)S(1)}, bf16[3,3,3,64,64]{4,3,2,1,0:T(8,128)(2,1)}, u32[]{:S(2)}) copy-start(bf16[3,3,3,64,64]{4,3,2,1,0:T(8,128)(2,1)} %sw.1) | copy-start | bytes 663556
  3.7 15.3 %collective-permute-start = (bf16[2,4,64,256]{3,2,1,0:T(8,128)(2,1)S(1)}, bf16[2,4,64,256]{3,2,1,0:T(8,128)(2,1)S(1)}, u32[]{:S(2)}, u32[]{:S(2)}) collective-permute-start(bf16[2,4,64,256]{3,2,1,0:T(8,128)(2,1)S(1)} %get-tuple-element.17), channel_id=1, source_target_pairs={{0,1},{1,0},{2,3},{3,2},{4,8},{5,9},{6,10},{7,11},{8,4},{9,5},{10,... | collective-permute-start | bytes 786440 | tf_op jit(solution)/shard_map/ppermute | solution.py:260
  12.2 8.2 %collective-permute-start.1 = (bf16[2,4,64,256]{3,2,1,0:T(8,128)(2,1)S(1)}, bf16[2,4,64,256]{3,2,1,0:T(8,128)(2,1)S(1)}, u32[]{:S(2)}, u32[]{:S(2)}) collective-permute-start(bf16[2,4,64,256]{3,2,1,0:T(8,128)(2,1)S(1)} %get-tuple-element.18), channel_id=1, source_target_pairs={{0,4},{1,5},{2,6},{3,7},{4,0},{5,1},{6,2},{7,3},{8,12},{9,13},{10,... | collective-permute-start | bytes 786440 | tf_op jit(solution)/shard_map/ppermute | solution.py:260
  12.2 9.8 %collective-permute-start.6 = (bf16[2,64,256]{2,1,0:T(8,128)(2,1)S(1)}, bf16[2,64,256]{2,1,0:T(8,128)(2,1)S(1)}, u32[]{:S(2)}, u32[]{:S(2)}) collective-permute-start(bf16[2,64,256]{2,1,0:T(8,128)(2,1)S(1)} %get-tuple-element.21), channel_id=1, source_target_pairs={{0,1},{1,0},{2,3},{3,2},{4,11},{5,10},{6,9},{7,8},{8,7},{9,6},{10,... | collective-permute-start | bytes 196616 | tf_op jit(solution)/shard_map/ppermute | solution.py:260
  13.1 12.1 %collective-permute-start.7 = (bf16[2,64,256]{2,1,0:T(8,128)(2,1)S(1)}, bf16[2,64,256]{2,1,0:T(8,128)(2,1)S(1)}, u32[]{:S(2)}, u32[]{:S(2)}) collective-permute-start(bf16[2,64,256]{2,1,0:T(8,128)(2,1)S(1)} %get-tuple-element.22), channel_id=1, source_target_pairs={{0,7},{1,6},{2,5},{3,4},{4,3},{5,2},{6,1},{7,0},{8,15},{9,14},{10,... | collective-permute-start | bytes 196616 | tf_op jit(solution)/shard_map/ppermute | solution.py:260
  14.1 11.2 %collective-permute-start.2 = (bf16[2,2,64,256]{3,2,1,0:T(8,128)(2,1)S(1)}, bf16[2,2,64,256]{3,2,1,0:T(8,128)(2,1)S(1)}, u32[]{:S(2)}, u32[]{:S(2)}) collective-permute-start(bf16[2,2,64,256]{3,2,1,0:T(8,128)(2,1)S(1)} %get-tuple-element.19), channel_id=1, source_target_pairs={{0,1},{1,0},{2,3},{3,2},{4,5},{5,4},{6,7},{7,6},{8,9},{9,8},{10,11... | collective-permute-start | bytes 393224 | tf_op jit(solution)/shard_map/ppermute | solution.py:260
  19.0 6.3 %collective-permute-start.3 = (bf16[2,2,64,256]{3,2,1,0:T(8,128)(2,1)S(1)}, bf16[2,2,64,256]{3,2,1,0:T(8,128)(2,1)S(1)}, u32[]{:S(2)}, u32[]{:S(2)}) collective-permute-start(bf16[2,2,64,256]{3,2,1,0:T(8,128)(2,1)S(1)} %get-tuple-element.20), channel_id=1, source_target_pairs={{0,3},{1,2},{2,1},{3,0},{4,7},{5,6},{6,5},{7,4},{8,11},{9,10},{10,... | collective-permute-start | bytes 393224 | tf_op jit(solution)/shard_map/ppermute | solution.py:260
  20.4 4.9 %collective-permute-start.4 = (bf16[2,64,256]{2,1,0:T(8,128)(2,1)S(1)}, bf16[2,64,256]{2,1,0:T(8,128)(2,1)S(1)}, u32[]{:S(2)}, u32[]{:S(2)}) collective-permute-start(bf16[2,64,256]{2,1,0:T(8,128)(2,1)S(1)} %dynamic-slice_bitcast_fusion.1), channel_id=1, source_target_pairs={{0,1},{1,0},{2,3},{3,2},{4,5},{5,4},{6,7},{7,6},{8,9},{9,8},{10,11... | collective-permute-start | bytes 196616 | tf_op jit(solution)/shard_map/ppermute | solution.py:260
  22.0 3.2 %collective-permute-start.5 = (bf16[2,64,256]{2,1,0:T(8,128)(2,1)S(1)}, bf16[2,64,256]{2,1,0:T(8,128)(2,1)S(1)}, u32[]{:S(2)}, u32[]{:S(2)}) collective-permute-start(bf16[2,64,256]{2,1,0:T(8,128)(2,1)S(1)} %dynamic-slice_bitcast_fusion), channel_id=1, source_target_pairs={{0,1},{1,0},{2,3},{3,2},{4,5},{5,4},{6,7},{7,6},{8,9},{9,8},{10,11... | collective-permute-start | bytes 196616 | tf_op jit(solution)/shard_map/ppermute | solution.py:260
  22.7 1.2 %copy-start = (bf16[3,3,3,64,256]{4,3,2,1,0:T(8,128)(2,1)S(1)}, bf16[3,3,3,64,256]{4,3,2,1,0:T(8,128)(2,1)}, u32[]{:S(2)}) copy-start(bf16[3,3,3,64,256]{4,3,2,1,0:T(8,128)(2,1)} %dw.1) | copy-start | bytes 2654212
  23.9 1.4 %copy-start.3 = (bf16[2,4,64,256]{3,2,1,0:T(8,128)(2,1)S(1)}, bf16[2,4,64,256]{3,2,1,0:T(8,128)(2,1)}, u32[]{:S(2)}) copy-start(bf16[2,4,64,256]{3,2,1,0:T(8,128)(2,1)} %vol.3) | copy-start | bytes 786436
  23.9 1.4 %copy-start.5 = (bf16[2,4,64,256]{3,2,1,0:T(8,128)(2,1)S(1)}, bf16[2,4,64,256]{3,2,1,0:T(8,128)(2,1)}, u32[]{:S(2)}) copy-start(bf16[2,4,64,256]{3,2,1,0:T(8,128)(2,1)} %tan.3) | copy-start | bytes 786436
  29.6 3.2 %collective-permute-start.8 = (bf16[2,64,256]{2,1,0:T(8,128)(2,1)S(1)}, bf16[2,64,256]{2,1,0:T(8,128)(2,1)S(1)}, u32[]{:S(2)}, u32[]{:S(2)}) collective-permute-start(bf16[2,64,256]{2,1,0:T(8,128)(2,1)S(1)} %get-tuple-element.26.own), channel_id=1, source_target_pairs={{0,2},{1,3},{2,0},{3,1},{4,6},{5,7},{6,4},{7,5},{8,10},{9,11},{10,... | collective-permute-start | bytes 196616 | tf_op jit(solution)/shard_map/ppermute | solution.py:260
  32.8 9.5 %collective-permute-start.11 = (bf16[2,2,64,256]{3,2,1,0:T(8,128)(2,1)S(1)}, bf16[2,2,64,256]{3,2,1,0:T(8,128)(2,1)S(1)}, u32[]{:S(2)}, u32[]{:S(2)}) collective-permute-start(bf16[2,2,64,256]{3,2,1,0:T(8,128)(2,1)S(1)} %pad_maximum_fusion), channel_id=1, source_target_pairs={{0,4},{1,5},{2,6},{3,7},{4,0},{5,1},{6,2},{7,3},{8,12},{9,13},{10,... | collective-permute-start | bytes 393224 | tf_op jit(solution)/shard_map/ppermute | solution.py:260
  32.9 11.1 %collective-permute-start.10 = (bf16[2,2,64,256]{3,2,1,0:T(8,128)(2,1)S(1)}, bf16[2,2,64,256]{3,2,1,0:T(8,128)(2,1)S(1)}, u32[]{:S(2)}, u32[]{:S(2)}) collective-permute-start(bf16[2,2,64,256]{3,2,1,0:T(8,128)(2,1)S(1)} %pad_maximum_fusion), channel_id=1, source_target_pairs={{0,1},{1,0},{2,3},{3,2},{4,8},{5,9},{6,10},{7,11},{8,4},{9,5},{10,... | collective-permute-start | bytes 393224 | tf_op jit(solution)/shard_map/ppermute | solution.py:260
  41.1 4.5 %collective-permute-start.9 = (bf16[2,2,64,256]{3,2,1,0:T(8,128)(2,1)S(1)}, bf16[2,2,64,256]{3,2,1,0:T(8,128)(2,1)S(1)}, u32[]{:S(2)}, u32[]{:S(2)}) collective-permute-start(bf16[2,2,64,256]{3,2,1,0:T(8,128)(2,1)S(1)} %pad_maximum_fusion), channel_id=1, source_target_pairs={{0,1},{1,0},{2,3},{3,2},{4,5},{5,4},{6,7},{7,6},{8,9},{9,8},{10,11... | collective-permute-start | bytes 393224 | tf_op jit(solution)/shard_map/ppermute | solution.py:260
  42.3 3.2 %collective-permute-start.13 = (bf16[2,2,64,256]{3,2,1,0:T(8,128)(2,1)S(1)}, bf16[2,2,64,256]{3,2,1,0:T(8,128)(2,1)S(1)}, u32[]{:S(2)}, u32[]{:S(2)}) collective-permute-start(bf16[2,2,64,256]{3,2,1,0:T(8,128)(2,1)S(1)} %collective-permute-done.11.r_e), channel_id=1, source_target_pairs={{0,1},{1,0},{2,3},{3,2},{4,5},{5,4},{6,7},{7,6},{8,9},{9,8},{10,11... | collective-permute-start | bytes 393224 | tf_op jit(solution)/shard_map/ppermute | solution.py:260
  44.0 2.5 %collective-permute-start.12 = (bf16[2,2,64,256]{3,2,1,0:T(8,128)(2,1)S(1)}, bf16[2,2,64,256]{3,2,1,0:T(8,128)(2,1)S(1)}, u32[]{:S(2)}, u32[]{:S(2)}) collective-permute-start(bf16[2,2,64,256]{3,2,1,0:T(8,128)(2,1)S(1)} %collective-permute-done.10.r_o), channel_id=1, source_target_pairs={{0,1},{1,0},{2,3},{3,2},{4,5},{5,4},{6,7},{7,6},{8,9},{9,8},{10,11... | collective-permute-start | bytes 393224 | tf_op jit(solution)/shard_map/ppermute | solution.py:260

commit v2 on v0

v2 whole, which is shorter than its diff:
```python
import functools

import jax
import jax.numpy as jnp
from jax import lax
from jax.experimental import pallas as pl
from jax.experimental.pallas import tpu as pltpu
from jax.sharding import PartitionSpec as P

BOTH = ("wide", "narrow")
BF16 = jnp.bfloat16
F32 = jnp.float32
ANY = pl.BlockSpec(memory_space=pl.ANY)
VMEM = pl.BlockSpec(memory_space=pltpu.VMEM)
HBM = pl.BlockSpec(memory_space=pltpu.HBM)


def exchange(wide, narrow, kind, route):
    pairs = []
    for w in range(wide):
        for n in range(narrow):
            if kind == "E":
                pw = w ^ 1
            elif kind == "O":
                pw = w + 1 if w % 2 else w - 1
            else:
                pw = w
            if not 0 <= pw < wide:
                pw, pn = w, n ^ 1
            elif route == "same" or (route == "near" and min(w, pw) != wide // 2 - 1):
                pn = n
            elif route == "core":
                pn = n ^ 1
            elif route == "mirror":
                pn = narrow - 1 - n
            else:
                pn = n ^ 2
            pairs.append((w * narrow + n, pw * narrow + pn))
    return pairs


def run_copies(copies, sems):
    started = [pltpu.make_async_copy(src, dst, sems.at[k]) for k, (src, dst) in enumerate(copies)]
    for copy in started:
        copy.start()

    def wait():
        for copy in started:
            copy.wait()

    return wait


def slices_kernel(vol, tan, s_o, s_e, s_c, s_m, sems):
    w, n = lax.axis_index("wide"), lax.axis_index("narrow")
    odd = lax.rem(w, 2)
    last = vol.shape[1] - 1
    row_c = jnp.where(lax.rem(n, 2) == 0, last, 0)
    row_m = jnp.where(n < 2, last, 0)
    copies = []
    for t, src in enumerate((vol, tan)):
        copies += [
            (src.at[odd], s_o.at[t]),
            (src.at[1 - odd], s_e.at[t]),
            (src.at[:, row_c], s_c.at[:, t]),
            (src.at[:, row_m], s_m.at[:, t]),
        ]
    run_copies(copies, sems)()


def weights_kernel(sw, dw, t_s, t_d, dw_half, sw_all, band, dband, sem):
    n = lax.axis_index("narrow")
    shallow = pltpu.make_async_copy(sw, sw_all, sem.at[0])
    deep = pltpu.make_async_copy(
        dw.at[:, :, :, :, pl.ds(pl.multiple_of((n // 2) * 128, 128), 128)], dw_half, sem.at[1]
    )
    shallow.start()
    deep.start()
    band[...] = jnp.zeros_like(band)
    dband[...] = jnp.zeros_like(dband)
    nt = (((1,), (1,)), ((), ()))

    def build(source, scratch, pick, out):
        for a in range(3):
            for c in range(3):
                for b in range(3):
                    scratch[a * 3 + c, 64 * (b + 1) : 64 * (b + 2), :] = source[a, b, c]
                for r in range(2):
                    rows = scratch[a * 3 + c, 64 * (1 - r) : 64 * (1 - r) + 256, :]
                    placed = lax.dot_general(pick, rows, nt, preferred_element_type=F32)
                    out[a, c * 128 + r * 64 : c * 128 + r * 64 + 64, :] = placed.astype(BF16)

    def selector(width, shift):
        row = lax.broadcasted_iota(jnp.int32, (64, width), 0)
        col = lax.broadcasted_iota(jnp.int32, (64, width), 1)
        return jnp.where(col == row + shift, 1.0, 0.0).astype(BF16)

    shallow.wait()
    build(sw_all, band, selector(64, 0), t_s)
    deep.wait()
    build(dw_half, dband, selector(128, 64 * lax.rem(n, 2)), t_d)


def shifted_sum(acc, lane, first, final):
    left = pltpu.roll(acc[0:128], 1, 1)
    right = pltpu.roll(acc[256:384], acc.shape[1] - 1, 1)
    return acc[128:256] + jnp.where(first(lane), 0.0, left) + jnp.where(final(lane), 0.0, right)


def activate(pre, dot):
    s = 0.5 * jnp.tanh(0.5 * pre) + 0.5
    primal = (pre * s).astype(BF16)
    tangent = (s * (1.0 + pre * (1.0 - s)) * dot).astype(BF16)
    return primal, tangent


def pair_matrix(cells):
    source = lax.broadcasted_iota(jnp.int32, (cells, cells // 2), 0)
    target = lax.broadcasted_iota(jnp.int32, (cells, cells // 2), 1)
    return jnp.where(source // 2 == target, 0.125, 0.0).astype(BF16)


def pool_plane(out, pairing):
    halves = []
    for value in out:
        half = jnp.dot(value, pairing, preferred_element_type=F32)
        halves.append(half[0:64] + half[64:128])
    return jnp.concatenate(halves, axis=1)


def shallow_lanes(cells):
    lane = lax.broadcasted_iota(jnp.int32, (128, cells), 1)
    return lane, (lambda v: v == 0), (lambda v: v == cells - 1)


def row_windows(face, core_row, far_row, n, narrow):
    rows, chans, cells = face.shape
    far_row = jnp.where((n > 0) & (n < narrow - 1), far_row, jnp.zeros_like(far_row))
    even = lax.rem(n, 2) == 0
    top, bottom = jnp.where(even, far_row, core_row), jnp.where(even, core_row, far_row)
    flat = face.reshape(rows * chans, cells)
    return (
        jnp.concatenate([top, flat[: 3 * chans]], axis=0),
        jnp.concatenate([flat[chans:], bottom], axis=0),
    )


def own_kernel(narrow, vol, tan, r_c, r_m, t_s, part, x, sems):
    n = lax.axis_index("narrow")
    cells = vol.shape[3]
    run_copies([(vol, x.at[0]), (tan, x.at[1])], sems)()
    lane, first, final = shallow_lanes(cells)
    for t in range(2):
        stacks = [row_windows(x[t, p], r_c[p, t], r_m[p, t], n, narrow) for p in range(2)]
        for win in range(2):
            stack = jnp.concatenate([stacks[0][win], stacks[1][win]], axis=0)
            for q in range(2):
                taps = jnp.concatenate([t_s[1 - q], t_s[2 - q]], axis=1)
                acc = jnp.dot(taps, stack, preferred_element_type=F32)
                part[q, t, win] = shifted_sum(acc, lane, first, final)


def finish_plane(narrow, q, taps, face, rim, part, emit):
    n = lax.axis_index("narrow")
    cells = face.shape[3]
    lane, first, final = shallow_lanes(cells)
    pairing = pair_matrix(cells)
    stacks = [row_windows(face[t], rim[0, t], rim[1, t], n, narrow) for t in range(2)]
    for win in range(2):
        pre = []
        for t in range(2):
            acc = jnp.dot(taps, stacks[t][win], preferred_element_type=F32)
            pre.append(part[q, t, win] + shifted_sum(acc, lane, first, final))
        out = activate(*pre)
        emit(win, [v.reshape(2, 64, cells) for v in out], pool_plane(out, pairing))


def near_kernel(narrow, r_e, x_e, t_s, part, skip_f, skip_t, pool_part):
    odd = lax.rem(lax.axis_index("wide"), 2)

    def emit(win, out, pool):
        for t, ref in enumerate((skip_f, skip_t)):
            ref[2 * win : 2 * win + 2] = out[t]
        pool_part[win] = pool

    finish_plane(narrow, 1 - odd, t_s[2 - 2 * odd], r_e, x_e, part, emit)


def far_kernel(wide, narrow, r_o, x_o, t_s, part, pool_part, skip_f, skip_t, pooled):
    w = lax.axis_index("wide")
    odd = lax.rem(w, 2)

    def emit(win, out, pool):
        for t, ref in enumerate((skip_f, skip_t)):
            ref[2 * win : 2 * win + 2] = out[t]
        pooled[win] = (pool_part[win] + pool).astype(BF16)

    taps = t_s[2 * odd]
    taps = jnp.where((w > 0) & (w < wide - 1), taps, jnp.zeros_like(taps))
    finish_plane(narrow, odd, taps, r_o, x_o, part, emit)


def deep_lanes(cells):
    lane = lax.broadcasted_iota(jnp.int32, (128, 2 * cells), 1)
    first = lambda v: (v == 0) | (v == cells)
    final = lambda v: (v == cells - 1) | (v == 2 * cells - 1)
    return lane, first, final


def gather_rows(x, mine, sibling, far, narrow):
    n = lax.axis_index("narrow")
    sib = n + 1 - 2 * lax.rem(n, 2)
    pair = mine.shape[1]
    x[0] = jnp.zeros(x.shape[1:], BF16)
    x[narrow * pair + 1] = jnp.zeros(x.shape[1:], BF16)
    for source, member in ((mine, n), (sibling, sib)):
        for k in range(2):
            owner = lax.rem(member + 2 * k, narrow)
            if far is not None:
                owner = jnp.where(far, lax.rem(member + 2 - 2 * k, narrow), owner)
            x[pl.ds(owner * pair + 1, pair)] = source[k]


def deep_sum(x, taps, j, lane, first, final):
    stack = x[2 * j : 2 * j + 4].reshape(256, x.shape[2])
    acc = jnp.dot(taps, stack, preferred_element_type=F32)
    return shifted_sum(acc, lane, first, final)


def deep_own_kernel(narrow, group, g_c, t_d, near_f, near_t, far_f, far_t, part, order, skip_f, skip_t,
                    x, sems):
    odd = lax.rem(lax.axis_index("wide"), 2)
    wait = run_copies(
        [
            (near_f, skip_f.at[1 - odd]),
            (near_t, skip_t.at[1 - odd]),
            (far_f, skip_f.at[odd]),
            (far_t, skip_t.at[odd]),
        ],
        sems,
    )
    order[...] = jnp.zeros_like(order)
    gather_rows(x, group, g_c, None, narrow)
    lanes = deep_lanes(x.shape[2] // 2)
    for j in range(part.shape[0]):
        part[j] = deep_sum(x, t_d[1], j, *lanes)
    wait()


def deep_near_kernel(narrow, r_e, e_c, t_d, part, total, x):
    odd = lax.rem(lax.axis_index("wide"), 2)
    gather_rows(x, r_e, e_c, None, narrow)
    lanes = deep_lanes(x.shape[2] // 2)
    taps = t_d[2 - 2 * odd]
    for j in range(part.shape[0]):
        total[j] = part[j] + deep_sum(x, taps, j, *lanes)


def deep_far_kernel(wide, narrow, r_o, o_c, t_d, part, out_f, out_t, x):
    w = lax.axis_index("wide")
    cells = x.shape[2] // 2
    far = (w == wide // 2 - 1) | (w == wide // 2)
    gather_rows(x, r_o, o_c, far, narrow)
    lanes = deep_lanes(cells)
    taps = t_d[2 * lax.rem(w, 2)]
    taps = jnp.where((w > 0) & (w < wide - 1), taps, jnp.zeros_like(taps))
    for j in range(part.shape[0]):
        both = part[j] + deep_sum(x, taps, j, *lanes)
        primal, tangent = activate(both[:, :cells], both[:, cells:])
        out_f[0, 2 * j : 2 * j + 2] = primal.reshape(2, 64, cells)
        out_t[0, 2 * j : 2 * j + 2] = tangent.reshape(2, 64, cells)


def call(body, outs, in_specs, out_specs, scratch=()):
    return pl.pallas_call(
        body,
        out_shape=[o if hasattr(o, "dtype") else jax.ShapeDtypeStruct(o, BF16) for o in outs],
        in_specs=in_specs,
        out_specs=out_specs,
        scratch_shapes=list(scratch),
        compiler_params=pltpu.CompilerParams(vmem_limit_bytes=32 * 1024 * 1024),
        cost_estimate=pl.CostEstimate(flops=0, bytes_accessed=0, transcendentals=0),
    )


def local(wide, narrow, volume, volume_tangent, shallow_weight, deep_weight):
    planes, rows, chans, cells = volume.shape
    volume, volume_tangent, shallow_weight, deep_weight = (
        pltpu.with_memory_space_constraint(v, pltpu.HBM)
        for v in (volume, volume_tangent, shallow_weight, deep_weight)
    )
    odd = lax.axis_index("wide") % 2
    dma = pltpu.SemaphoreType.DMA

    def swap(v, kind, route):
        return lax.ppermute(v, BOTH, exchange(wide, narrow, kind, route))

    def full(*shape):
        return jax.ShapeDtypeStruct(shape, F32)

    face, edge = (2, rows, chans, cells), (planes, 2, chans, cells)
    s_o, s_e, s_c, s_m = call(
        slices_kernel, [face, face, edge, edge], [HBM] * 2, [ANY] * 4, [dma((8,))]
    )(volume, volume_tangent)
    r_o = swap(s_o, "O", "same")
    r_e = swap(s_e, "E", "same")
    r_c = swap(s_c, "", "core")
    r_m = swap(s_m, "", "mirror")
    rim = jnp.stack([r_c, r_m])
    x_o = swap(lax.dynamic_index_in_dim(rim, odd, 1, keepdims=False), "O", "same")
    x_e = swap(lax.dynamic_index_in_dim(rim, 1 - odd, 1, keepdims=False), "E", "same")
    band = (3, 384, 256)
    t_s, t_d = call(
        weights_kernel, [band, band], [HBM] * 2, [VMEM, VMEM],
        [
            pltpu.VMEM((3, 3, 3, 64, 128), BF16),
            pltpu.VMEM((3, 3, 3, 64, 64), BF16),
            pltpu.VMEM((9, 320, 64), BF16),
            pltpu.VMEM((9, 320, 128), BF16),
            dma((2,)),
        ],
    )(shallow_weight, deep_weight)
    wins = rows // 2
    (part,) = call(
        functools.partial(own_kernel, narrow),
        [full(planes, 2, wins, 128, cells)], [HBM] * 2 + [VMEM] * 3, [VMEM],
        [pltpu.VMEM((2, planes, rows, chans, cells), BF16), dma((2,))],
    )(volume, volume_tangent, r_c, r_m, t_s)
    plane = (rows, chans, cells)
    near_f, near_t, pool_part = call(
        functools.partial(near_kernel, narrow),
        [plane, plane, full(wins, chans, cells)], [VMEM] * 4, [VMEM] * 3,
    )(r_e, x_e, t_s, part)
    far_f, far_t, pooled = call(
        functools.partial(far_kernel, wide, narrow),
        [plane, plane, (wins, chans, cells)], [VMEM] * 5, [VMEM] * 3,
    )(r_o, x_o, t_s, part, pool_part)
    other = swap(pooled, "", "across")
    group = jnp.stack([pooled, other])
    o2 = swap(group, "O", "near")
    e2 = swap(group, "E", "same")
    g_c = swap(group, "", "core")
    deep_rows = wins * narrow
    sums = full(deep_rows // 2, 128, cells)
    gathered = pltpu.VMEM((deep_rows + 2, chans, cells), BF16)
    part_d, order, skip_f, skip_t = call(
        functools.partial(deep_own_kernel, narrow),
        [sums, (chans, cells), volume.shape, volume.shape],
        [VMEM] * 7, [VMEM, VMEM, HBM, HBM], [gathered, dma((4,))],
    )(group, g_c, t_d, near_f, near_t, far_f, far_t)
    e_c = swap(e2, "", "core")
    o_c = swap(o2 + order, "", "core")
    (total_d,) = call(
        functools.partial(deep_near_kernel, narrow), [sums], [VMEM] * 4, [VMEM], [gathered]
    )(e2, e_c, t_d, part_d)
    deep_shape = (1, deep_rows, 64, cells // 2)
    deep_f, deep_t = call(
        functools.partial(deep_far_kernel, wide, narrow),
        [deep_shape, deep_shape], [VMEM] * 4, [VMEM] * 2, [gathered],
    )(o2, o_c, t_d, total_d)
    return skip_f, skip_t, deep_f, deep_t


def solution(mesh):
    wide, narrow = mesh.shape["wide"], mesh.shape["narrow"]
    in_specs = (P("wide", "narrow", None, None), P("wide", "narrow", None, None), P(), P())
    out_specs = (
        P("wide", "narrow", None, None),
        P("wide", "narrow", None, None),
        P("wide", None, "narrow", None),
        P("wide", None, "narrow", None),
    )
    return jax.shard_map(
        functools.partial(local, wide, narrow), mesh=mesh, in_specs=in_specs, out_specs=out_specs,
        check_vma=False,
    )
```

time: 95.4 us -> 43 us (0.45)
  local copies, waits for them, and re-layouts: 19.8 us -> 0 us
  other arithmetic: 16 us -> 0.05 us
  Pallas kernels: 0 us -> 10.4 us
  blocking collectives: 10.4 us -> 0 us
  matrix products: 7.68 us -> 0 us
  starting transfers between devices: 29.4 us -> 24.8 us
  waiting for transfers between devices: 10.6 us -> 6.92 us
    unnamed x17 -> x0, local copies, waits for them, and re-layouts: 10.4 us -> none
    all_gather x1 -> x0, blocking collectives: 10.4 us -> none  [local(): whole_y = lax.all_gather(pooled, 'narrow', axis=2, tiled=True)]
    pallas_call x0 -> x8, Pallas kernels: none -> 10.4 us  [the longest x1 2.14 us: local(): call(functools.partial(own_kernel, narrow), [full(planes, 2, wins, 128, c...]
    conv_general_dilated x2 -> x0, other arithmetic: 9.18 us -> none  [conv_taps(): lax.conv_general_dilated(padded, weight, (1, 1, 1), ((0, 0), (0, 0), (1,...]
    conv_general_dilated x2 -> x0, matrix products: 6.56 us -> none  [conv_taps(): lax.conv_general_dilated(padded, weight, (1, 1, 1), ((0, 0), (0, 0), (1,...]
    concatenate x2 -> x0, local copies, waits for them, and re-layouts: 5.48 us -> none  [with_halo(): jnp.concatenate([lax.ppermute(tail, axis, [(i, (i + 1) % count) for i in...]
    ppermute x6 -> x12, starting transfers between devices: 29.4 us -> 24.8 us  [swap(): return lax.ppermute(v, BOTH, exchange(wide, narrow, kind, route))]
    ppermute x6 -> x12, waiting for transfers between devices: 10.6 us -> 6.92 us  [swap(): return lax.ppermute(v, BOTH, exchange(wide, narrow, kind, route))]
  transfers between devices with their start and end apart: 6 -> 12, of which waited for: 5 -> 3; matrix products, arithmetic and copies ran while one was open for 1% -> 0% of each run, Pallas kernels for 0% -> 16%
where the time goes in v2:
time: 43 us; the launch traced here: 42.9 us
  starting transfers between devices  24.8 us (58%)
  Pallas kernels  10.4 us (24%)
  waiting for transfers between devices  6.92 us (16%)
  between operations  0.76 us (2%)
    ppermute x12, starting transfers between devices, swap(): return lax.ppermute(v, BOTH, exchange(wide, narrow, kind, route))  24.8 us
    ppermute x12, waiting for transfers between devices, swap(): return lax.ppermute(v, BOTH, exchange(wide, narrow, kind, route))  6.92 us
    pallas_call x1, Pallas kernels, local(): call(functools.partial(own_kernel, narrow), [full(planes, 2, wins, 128, c...  2.14 us
    pallas_call x1, Pallas kernels, local(): call(weights_kernel, [band, band], [HBM] * 2, [VMEM, VMEM], [pltpu.VMEM((...  2.12 us
    pallas_call x1, Pallas kernels, local(): call(functools.partial(deep_own_kernel, narrow), [sums, (chans, cells), v...  1.29 us
    pallas_call x1, Pallas kernels, local(): call(functools.partial(deep_far_kernel, wide, narrow), [deep_shape, deep_...  1.26 us
    pallas_call x1, Pallas kernels, local(): call(slices_kernel, [face, face, edge, edge], [HBM] * 2, [ANY] * 4, [dma(...  1.25 us
    pallas_call x1, Pallas kernels, local(): call(functools.partial(far_kernel, wide, narrow), [plane, plane, (wins, c...  0.88 us
  transfers between devices with their start and end apart: 12, of which 3 were waited for; matrix products, arithmetic and copies ran while one was open for 0% of the time, Pallas kernels for 16%

profile of v2, /device:TPU:25, one launch (start us, length us, event | category | flops | bytes accessed | tf_op | source)
XLA Modules:
  0.0 42.9 jit_solution(16162922350237357136)
XLA Ops:
  0.6 1.3 %shard_map.75 = (bf16[2,4,64,256]{3,2,1,0:T(8,128)(2,1)S(1)}, bf16[2,4,64,256]{3,2,1,0:T(8,128)(2,1)S(1)}, bf16[2,2,64,256]{3,2,1,0:T(8,128)(2,1)S(1)}, bf16[2,2,64,256]{3,2,1,0:T(8,128)(2,1)S(1)}) custom-call(bf16[2,4,64,256]{3,2,1,0:T(8,128)(2,1)} %vol.3, bf16[2,4,64,256]{3,2,1,0:T(8,128)(2,1)} %tan.3), custom_call_target="tpu_custom_call" | custom-call | tf_op jit(solution)/shard_map/pallas_call | solution.py:302
  1.9 0.8 %collective-permute-start.1 = (bf16[2,2,64,256]{3,2,1,0:T(8,128)(2,1)S(1)}, bf16[2,2,64,256]{3,2,1,0:T(8,128)(2,1)S(1)}, u32[]{:S(2)}, u32[]{:S(2)}) collective-permute-start(bf16[2,2,64,256]{3,2,1,0:T(8,128)(2,1)S(1)} %get-tuple-element.23), channel_id=1, source_target_pairs={{0,1},{1,0},{2,3},{3,2},{4,5},{5,4},{6,7},{7,6},{8,9},{9,8},{10,11... | collective-permute-start | bytes 393224 | tf_op jit(solution)/shard_map/ppermute | solution.py:296
  2.7 0.4 %collective-permute-start.2 = (bf16[2,2,64,256]{3,2,1,0:T(8,128)(2,1)S(1)}, bf16[2,2,64,256]{3,2,1,0:T(8,128)(2,1)S(1)}, u32[]{:S(2)}, u32[]{:S(2)}) collective-permute-start(bf16[2,2,64,256]{3,2,1,0:T(8,128)(2,1)S(1)} %get-tuple-element.24), channel_id=1, source_target_pairs={{0,3},{1,2},{2,1},{3,0},{4,7},{5,6},{6,5},{7,4},{8,11},{9,10},{10,... | collective-permute-start | bytes 393224 | tf_op jit(solution)/shard_map/ppermute | solution.py:296
  3.1 1.2 %collective-permute-start.4 = (bf16[2,4,64,256]{3,2,1,0:T(8,128)(2,1)S(1)}, bf16[2,4,64,256]{3,2,1,0:T(8,128)(2,1)S(1)}, u32[]{:S(2)}, u32[]{:S(2)}) collective-permute-start(bf16[2,4,64,256]{3,2,1,0:T(8,128)(2,1)S(1)} %get-tuple-element.26), channel_id=1, source_target_pairs={{0,4},{1,5},{2,6},{3,7},{4,0},{5,1},{6,2},{7,3},{8,12},{9,13},{10,... | collective-permute-start | bytes 786440 | tf_op jit(solution)/shard_map/ppermute | solution.py:296
  4.3 7.5 %collective-permute-start = (bf16[2,4,64,256]{3,2,1,0:T(8,128)(2,1)S(1)}, bf16[2,4,64,256]{3,2,1,0:T(8,128)(2,1)S(1)}, u32[]{:S(2)}, u32[]{:S(2)}) collective-permute-start(bf16[2,4,64,256]{3,2,1,0:T(8,128)(2,1)S(1)} %get-tuple-element.22), channel_id=1, source_target_pairs={{0,1},{1,0},{2,3},{3,2},{4,8},{5,9},{6,10},{7,11},{8,4},{9,5},{10,... | collective-permute-start | bytes 786440 | tf_op jit(solution)/shard_map/ppermute | solution.py:296
  11.8 0.0 collective-permute-done.1.r_c
  11.8 0.1 collective-permute-start.5
  11.9 5.3 %collective-permute-start.3 = (bf16[2,2,64,256]{3,2,1,0:T(8,128)(2,1)S(1)}, bf16[2,2,64,256]{3,2,1,0:T(8,128)(2,1)S(1)}, u32[]{:S(2)}, u32[]{:S(2)}) collective-permute-start(bf16[2,2,64,256]{3,2,1,0:T(8,128)(2,1)S(1)} %get-tuple-element.41), channel_id=1, source_target_pairs={{0,1},{1,0},{2,3},{3,2},{4,8},{5,9},{6,10},{7,11},{8,4},{9,5},{10,... | collective-permute-start | bytes 393224 | tf_op jit(solution)/shard_map/ppermute | solution.py:296
  17.3 2.1 %shard_map.76 = (bf16[3,384,256]{2,1,0:T(8,128)(2,1)S(1)}, bf16[3,384,256]{2,1,0:T(8,128)(2,1)S(1)}) custom-call(bf16[3,3,3,64,64]{4,3,2,1,0:T(8,128)(2,1)} %sw.1, bf16[3,3,3,64,256]{4,3,2,1,0:T(8,128)(2,1)} %dw.1), custom_call_target="tpu_custom_call" | custom-call | tf_op jit(solution)/shard_map/pallas_call | solution.py:313
  19.4 2.1 %shard_map.77.part = f32[2,2,2,128,256]{4,3,2,1,0:T(8,128)S(1)} custom-call(bf16[2,4,64,256]{3,2,1,0:T(8,128)(2,1)} %vol.3, bf16[2,4,64,256]{3,2,1,0:T(8,128)(2,1)} %tan.3, bf16[2,2,64,256]{3,2,1,0:T(8,128)(2,1)S(1)} %collective-permute-done.1.r_c, bf16[2,2,64,256]{3,2,1,0:T(8,128)(2,1)S(1)} %collective-permute-done.2.r_m, ...), custom_call_target="tpu_custom_call" | custom-call | tf_op jit(solution)/shard_map/pallas_call | solution.py:324
  21.6 0.9 %shard_map.78 = (bf16[4,64,256]{2,1,0:T(8,128)(2,1)S(1)}, bf16[4,64,256]{2,1,0:T(8,128)(2,1)S(1)}, f32[2,64,256]{2,1,0:T(8,128)S(1)}) custom-call(bf16[2,4,64,256]{3,2,1,0:T(8,128)(2,1)S(1)} %collective-permute-done.4.r_e, bf16[2,2,64,256]{3,2,1,0:T(8,128)(2,1)S(1)} %collective-permute-done.5.x_e, bf16[3,384,256]{2,1,0:T(8,128)(2,1)S(1)} %get-tuple-element.25.t_s, ...), custom_call_target="tpu_custom_call" | custom-call | tf_op jit(solution)/shard_map/pallas_call | solution.py:330
  22.5 0.9 %shard_map.79 = (bf16[4,64,256]{2,1,0:T(8,128)(2,1)S(1)}, bf16[4,64,256]{2,1,0:T(8,128)(2,1)S(1)}, bf16[2,64,256]{2,1,0:T(8,128)(2,1)S(1)}) custom-call(bf16[2,4,64,256]{3,2,1,0:T(8,128)(2,1)S(1)} %collective-permute-done.r_o, bf16[2,2,64,256]{3,2,1,0:T(8,128)(2,1)S(1)} %collective-permute-done.3.x_o, bf16[3,384,256]{2,1,0:T(8,128)(2,1)S(1)} %get-tuple-element.25.t_s, ...), custom_call_target="tpu_custom_call" | custom-call | tf_op jit(solution)/shard_map/pallas_call | solution.py:334
  23.3 0.1 collective-permute-start.6
  23.4 3.1 %collective-permute-done.6 = bf16[2,64,256]{2,1,0:T(8,128)(2,1)S(1)} collective-permute-done((bf16[2,64,256]{2,1,0:T(8,128)(2,1)S(1)}, bf16[2,64,256]{2,1,0:T(8,128)(2,1)S(1)}, u32[]{:S(2)}, u32[]{:S(2)}) %collective-permute-start.6) | collective-permute-done | bytes 65568 | tf_op jit(solution)/shard_map/ppermute | solution.py:296
  26.6 0.1 collective-permute-start.10
  26.7 2.5 %collective-permute-start.7 = (bf16[2,2,64,256]{3,2,1,0:T(8,128)(2,1)S(1)}, bf16[2,2,64,256]{3,2,1,0:T(8,128)(2,1)S(1)}, u32[]{:S(2)}, u32[]{:S(2)}) collective-permute-start(bf16[2,2,64,256]{3,2,1,0:T(8,128)(2,1)S(1)} %pad_maximum_fusion.group), channel_id=1, source_target_pairs={{0,1},{1,0},{2,3},{3,2},{4,5},{5,4},{6,7},{7,6},{8,9},{9,8},{10,11... | collective-permute-start | bytes 393224 | tf_op jit(solution)/shard_map/ppermute | solution.py:296
  29.2 5.5 %collective-permute-start.8 = (bf16[2,2,64,256]{3,2,1,0:T(8,128)(2,1)S(1)}, bf16[2,2,64,256]{3,2,1,0:T(8,128)(2,1)S(1)}, u32[]{:S(2)}, u32[]{:S(2)}) collective-permute-start(bf16[2,2,64,256]{3,2,1,0:T(8,128)(2,1)S(1)} %pad_maximum_fusion.group), channel_id=1, source_target_pairs={{0,1},{1,0},{2,3},{3,2},{4,8},{5,9},{6,10},{7,11},{8,4},{9,5},{10,... | collective-permute-start | bytes 393224 | tf_op jit(solution)/shard_map/ppermute | solution.py:296
  34.7 0.4 collective-permute-start.11
  35.0 1.3 %shard_map.80 = (f32[4,128,256]{2,1,0:T(8,128)S(1)}, bf16[64,256]{1,0:T(8,128)(2,1)S(1)}, bf16[2,4,64,256]{3,2,1,0:T(8,128)(2,1)}, bf16[2,4,64,256]{3,2,1,0:T(8,128)(2,1)}) custom-call(bf16[2,2,64,256]{3,2,1,0:T(8,128)(2,1)S(1)} %pad_maximum_fusion.group, bf16[2,2,64,256]{3,2,1,0:T(8,128)(2,1)S(1)} %collective-permute-done.7.g_c, ...), custom_call_target="tpu_custom_call" | custom-call | tf_op jit(solution)/shard_map/pallas_call | solution.py:346
  36.3 3.4 %collective-permute-done.8.r_o = bf16[2,2,64,256]{3,2,1,0:T(8,128)(2,1)S(1)} collective-permute-done((bf16[2,2,64,256]{3,2,1,0:T(8,128)(2,1)S(1)}, bf16[2,2,64,256]{3,2,1,0:T(8,128)(2,1)S(1)}, u32[]{:S(2)}, u32[]{:S(2)}) %collective-permute-start.8) | collective-permute-done | bytes 131104 | tf_op jit(solution)/shard_map/ppermute | solution.py:296
  39.7 1.0 %collective-permute-start.9 = (bf16[2,2,64,256]{3,2,1,0:T(8,128)(2,1)S(1)}, bf16[2,2,64,256]{3,2,1,0:T(8,128)(2,1)S(1)}, u32[]{:S(2)}, u32[]{:S(2)}) collective-permute-start(bf16[2,2,64,256]{3,2,1,0:T(8,128)(2,1)S(1)} %broadcast_add_fusion), channel_id=1, source_target_pairs={{0,1},{1,0},{2,3},{3,2},{4,5},{5,4},{6,7},{7,6},{8,9},{9,8},{10,11... | collective-permute-start | bytes 393224 | tf_op jit(solution)/shard_map/ppermute | solution.py:296
  40.7 0.5 %shard_map.81.part = f32[4,128,256]{2,1,0:T(8,128)S(1)} custom-call(bf16[2,2,64,256]{3,2,1,0:T(8,128)(2,1)S(1)} %collective-permute-done.10.r_e, bf16[2,2,64,256]{3,2,1,0:T(8,128)(2,1)S(1)} %collective-permute-done.11.e_c, bf16[3,384,256]{2,1,0:T(8,128)(2,1)S(1)} %get-tuple-element.29.t_d, f32[4,128,256]{2,1,0:T(8,128)S(1)} %get-tuple-element.37.part), custom_call_target="tpu_custom_call" | custom-call | tf_op jit(solution)/shard_map/pallas_call | solution.py:353
  41.2 0.4 %collective-permute-done.9.o_c = bf16[2,2,64,256]{3,2,1,0:T(8,128)(2,1)S(1)} collective-permute-done((bf16[2,2,64,256]{3,2,1,0:T(8,128)(2,1)S(1)}, bf16[2,2,64,256]{3,2,1,0:T(8,128)(2,1)S(1)}, u32[]{:S(2)}, u32[]{:S(2)}) %collective-permute-start.9) | collective-permute-done | bytes 131104 | tf_op jit(solution)/shard_map/ppermute | solution.py:296
  41.6 1.3 %shard_map.82 = (bf16[1,8,64,128]{3,2,1,0:T(8,128)(2,1)}, bf16[1,8,64,128]{3,2,1,0:T(8,128)(2,1)}) custom-call(bf16[2,2,64,256]{3,2,1,0:T(8,128)(2,1)S(1)} %collective-permute-done.8.r_o, bf16[2,2,64,256]{3,2,1,0:T(8,128)(2,1)S(1)} %collective-permute-done.9.o_c, bf16[3,384,256]{2,1,0:T(8,128)(2,1)S(1)} %get-tuple-element.29.t_d, ...), custom_call_target="tpu_custom_call" | custom-call | tf_op jit(solution)/shard_map/pallas_call | solution.py:357
  (11 shorter events, 0.1 us)
Async XLA Ops:
  1.9 9.9 %collective-permute-start.1 = (bf16[2,2,64,256]{3,2,1,0:T(8,128)(2,1)S(1)}, bf16[2,2,64,256]{3,2,1,0:T(8,128)(2,1)S(1)}, u32[]{:S(2)}, u32[]{:S(2)}) collective-permute-start(bf16[2,2,64,256]{3,2,1,0:T(8,128)(2,1)S(1)} %get-tuple-element.23), channel_id=1, source_target_pairs={{0,1},{1,0},{2,3},{3,2},{4,5},{5,4},{6,7},{7,6},{8,9},{9,8},{10,11... | collective-permute-start | bytes 393224 | tf_op jit(solution)/shard_map/ppermute | solution.py:296
  2.7 9.2 %collective-permute-start.2 = (bf16[2,2,64,256]{3,2,1,0:T(8,128)(2,1)S(1)}, bf16[2,2,64,256]{3,2,1,0:T(8,128)(2,1)S(1)}, u32[]{:S(2)}, u32[]{:S(2)}) collective-permute-start(bf16[2,2,64,256]{3,2,1,0:T(8,128)(2,1)S(1)} %get-tuple-element.24), channel_id=1, source_target_pairs={{0,3},{1,2},{2,1},{3,0},{4,7},{5,6},{6,5},{7,4},{8,11},{9,10},{10,... | collective-permute-start | bytes 393224 | tf_op jit(solution)/shard_map/ppermute | solution.py:296
  3.1 18.5 %collective-permute-start.4 = (bf16[2,4,64,256]{3,2,1,0:T(8,128)(2,1)S(1)}, bf16[2,4,64,256]{3,2,1,0:T(8,128)(2,1)S(1)}, u32[]{:S(2)}, u32[]{:S(2)}) collective-permute-start(bf16[2,4,64,256]{3,2,1,0:T(8,128)(2,1)S(1)} %get-tuple-element.26), channel_id=1, source_target_pairs={{0,4},{1,5},{2,6},{3,7},{4,0},{5,1},{6,2},{7,3},{8,12},{9,13},{10,... | collective-permute-start | bytes 786440 | tf_op jit(solution)/shard_map/ppermute | solution.py:296
  4.3 18.1 %collective-permute-start = (bf16[2,4,64,256]{3,2,1,0:T(8,128)(2,1)S(1)}, bf16[2,4,64,256]{3,2,1,0:T(8,128)(2,1)S(1)}, u32[]{:S(2)}, u32[]{:S(2)}) collective-permute-start(bf16[2,4,64,256]{3,2,1,0:T(8,128)(2,1)S(1)} %get-tuple-element.22), channel_id=1, source_target_pairs={{0,1},{1,0},{2,3},{3,2},{4,8},{5,9},{6,10},{7,11},{8,4},{9,5},{10,... | collective-permute-start | bytes 786440 | tf_op jit(solution)/shard_map/ppermute | solution.py:296
  11.8 9.7 %collective-permute-start.5 = (bf16[2,2,64,256]{3,2,1,0:T(8,128)(2,1)S(1)}, bf16[2,2,64,256]{3,2,1,0:T(8,128)(2,1)S(1)}, u32[]{:S(2)}, u32[]{:S(2)}) collective-permute-start(bf16[2,2,64,256]{3,2,1,0:T(8,128)(2,1)S(1)} %get-tuple-element.40), channel_id=1, source_target_pairs={{0,4},{1,5},{2,6},{3,7},{4,0},{5,1},{6,2},{7,3},{8,12},{9,13},{10,... | collective-permute-start | bytes 393224 | tf_op jit(solution)/shard_map/ppermute | solution.py:296
  11.9 10.5 %collective-permute-start.3 = (bf16[2,2,64,256]{3,2,1,0:T(8,128)(2,1)S(1)}, bf16[2,2,64,256]{3,2,1,0:T(8,128)(2,1)S(1)}, u32[]{:S(2)}, u32[]{:S(2)}) collective-permute-start(bf16[2,2,64,256]{3,2,1,0:T(8,128)(2,1)S(1)} %get-tuple-element.41), channel_id=1, source_target_pairs={{0,1},{1,0},{2,3},{3,2},{4,8},{5,9},{6,10},{7,11},{8,4},{9,5},{10,... | collective-permute-start | bytes 393224 | tf_op jit(solution)/shard_map/ppermute | solution.py:296
  23.3 3.2 %collective-permute-start.6 = (bf16[2,64,256]{2,1,0:T(8,128)(2,1)S(1)}, bf16[2,64,256]{2,1,0:T(8,128)(2,1)S(1)}, u32[]{:S(2)}, u32[]{:S(2)}) collective-permute-start(bf16[2,64,256]{2,1,0:T(8,128)(2,1)S(1)} %get-tuple-element.28), channel_id=1, source_target_pairs={{0,2},{1,3},{2,0},{3,1},{4,6},{5,7},{6,4},{7,5},{8,10},{9,11},{10,... | collective-permute-start | bytes 196616 | tf_op jit(solution)/shard_map/ppermute | solution.py:296
  26.6 8.1 %collective-permute-start.10 = (bf16[2,2,64,256]{3,2,1,0:T(8,128)(2,1)S(1)}, bf16[2,2,64,256]{3,2,1,0:T(8,128)(2,1)S(1)}, u32[]{:S(2)}, u32[]{:S(2)}) collective-permute-start(bf16[2,2,64,256]{3,2,1,0:T(8,128)(2,1)S(1)} %pad_maximum_fusion.group), channel_id=1, source_target_pairs={{0,4},{1,5},{2,6},{3,7},{4,0},{5,1},{6,2},{7,3},{8,12},{9,13},{10,... | collective-permute-start | bytes 393224 | tf_op jit(solution)/shard_map/ppermute | solution.py:296
  26.7 8.4 %collective-permute-start.7 = (bf16[2,2,64,256]{3,2,1,0:T(8,128)(2,1)S(1)}, bf16[2,2,64,256]{3,2,1,0:T(8,128)(2,1)S(1)}, u32[]{:S(2)}, u32[]{:S(2)}) collective-permute-start(bf16[2,2,64,256]{3,2,1,0:T(8,128)(2,1)S(1)} %pad_maximum_fusion.group), channel_id=1, source_target_pairs={{0,1},{1,0},{2,3},{3,2},{4,5},{5,4},{6,7},{7,6},{8,9},{9,8},{10,11... | collective-permute-start | bytes 393224 | tf_op jit(solution)/shard_map/ppermute | solution.py:296
  29.2 10.5 %collective-permute-start.8 = (bf16[2,2,64,256]{3,2,1,0:T(8,128)(2,1)S(1)}, bf16[2,2,64,256]{3,2,1,0:T(8,128)(2,1)S(1)}, u32[]{:S(2)}, u32[]{:S(2)}) collective-permute-start(bf16[2,2,64,256]{3,2,1,0:T(8,128)(2,1)S(1)} %pad_maximum_fusion.group), channel_id=1, source_target_pairs={{0,1},{1,0},{2,3},{3,2},{4,8},{5,9},{6,10},{7,11},{8,4},{9,5},{10,... | collective-permute-start | bytes 393224 | tf_op jit(solution)/shard_map/ppermute | solution.py:296
  34.7 6.0 %collective-permute-start.11 = (bf16[2,2,64,256]{3,2,1,0:T(8,128)(2,1)S(1)}, bf16[2,2,64,256]{3,2,1,0:T(8,128)(2,1)S(1)}, u32[]{:S(2)}, u32[]{:S(2)}) collective-permute-start(bf16[2,2,64,256]{3,2,1,0:T(8,128)(2,1)S(1)} %collective-permute-done.10.r_e), channel_id=1, source_target_pairs={{0,1},{1,0},{2,3},{3,2},{4,5},{5,4},{6,7},{7,6},{8,9},{9,8},{10,11... | collective-permute-start | bytes 393224 | tf_op jit(solution)/shard_map/ppermute | solution.py:296
  39.7 1.9 %collective-permute-start.9 = (bf16[2,2,64,256]{3,2,1,0:T(8,128)(2,1)S(1)}, bf16[2,2,64,256]{3,2,1,0:T(8,128)(2,1)S(1)}, u32[]{:S(2)}, u32[]{:S(2)}) collective-permute-start(bf16[2,2,64,256]{3,2,1,0:T(8,128)(2,1)S(1)} %broadcast_add_fusion), channel_id=1, source_target_pairs={{0,1},{1,0},{2,3},{3,2},{4,5},{5,4},{6,7},{7,6},{8,9},{9,8},{10,11... | collective-permute-start | bytes 393224 | tf_op jit(solution)/shard_map/ppermute | solution.py:296

commit v3 on v2

--- a/solution.py
+++ b/solution.py
@@ -8,6 +8,7 @@
 from jax.sharding import PartitionSpec as P
 
 BOTH = ("wide", "narrow")
+PAD = 16
 BF16 = jnp.bfloat16
 F32 = jnp.float32
 ANY = pl.BlockSpec(memory_space=pl.ANY)
@@ -25,14 +26,21 @@
                 pw = w + 1 if w % 2 else w - 1
             else:
                 pw = w
+            if route == "mirror" and not 0 <= pw < wide:
+                pw = w
             if not 0 <= pw < wide:
                 pw, pn = w, n ^ 1
             elif route == "same" or (route == "near" and min(w, pw) != wide // 2 - 1):
                 pn = n
             elif route == "core":
                 pn = n ^ 1
+            elif route == "mirror" and 0 < n < narrow - 1:
+                pn = narrow - 1 - n
             elif route == "mirror":
-                pn = narrow - 1 - n
+                if wide % 8 == 0 and (w | 4) % (wide // 2) != wide // 2 - 1:
+                    pw, pn = w ^ 4, n
+                else:
+                    pw, pn = (w + wide // 2) % wide, narrow - 1 - n
             else:
                 pn = n ^ 2
             pairs.append((w * narrow + n, pw * narrow + pn))
@@ -68,8 +76,9 @@
     run_copies(copies, sems)()
 
 
-def weights_kernel(sw, dw, t_s, t_d, dw_half, sw_all, band, dband, sem):
-    n = lax.axis_index("narrow")
+def weights_kernel(vol, tan, sw, dw, t_s, t_d, own, dw_half, sw_all, band, dband, sem, sems):
+    n = lax.axis_index("narrow")
+    wait = run_copies([(vol, own.at[0]), (tan, own.at[1])], sems)
     shallow = pltpu.make_async_copy(sw, sw_all, sem.at[0])
     deep = pltpu.make_async_copy(
         dw.at[:, :, :, :, pl.ds(pl.multiple_of((n // 2) * 128, 128), 128)], dw_half, sem.at[1]
@@ -99,6 +108,7 @@
     build(sw_all, band, selector(64, 0), t_s)
     deep.wait()
     build(dw_half, dband, selector(128, 64 * lax.rem(n, 2)), t_d)
+    wait()
 
 
 def shifted_sum(acc, lane, first, final):
@@ -145,10 +155,19 @@
     )
 
 
-def own_kernel(narrow, vol, tan, r_c, r_m, t_s, part, x, sems):
-    n = lax.axis_index("narrow")
-    cells = vol.shape[3]
-    run_copies([(vol, x.at[0]), (tan, x.at[1])], sems)()
+def edge_kernel(face, *rest):
+    row_c, row_m = rest[-2:]
+    n = lax.axis_index("narrow")
+    last = face.shape[1] - 1
+    for t in range(2):
+        row_c[t] = jnp.where(lax.rem(n, 2) == 0, face[t, last], face[t, 0])
+        row_m[t, 0 : face.shape[2]] = jnp.where(n < 2, face[t, last], face[t, 0])
+        row_m[t, face.shape[2] :] = jnp.zeros((PAD, face.shape[3]), BF16)
+
+
+def own_kernel(narrow, x, r_c, r_m, t_s, part):
+    n = lax.axis_index("narrow")
+    cells = x.shape[4]
     lane, first, final = shallow_lanes(cells)
     for t in range(2):
         stacks = [row_windows(x[t, p], r_c[p, t], r_m[p, t], n, narrow) for p in range(2)]
@@ -160,12 +179,12 @@
                 part[q, t, win] = shifted_sum(acc, lane, first, final)
 
 
-def finish_plane(narrow, q, taps, face, rim, part, emit):
-    n = lax.axis_index("narrow")
-    cells = face.shape[3]
+def finish_plane(narrow, q, taps, face, core_row, far_row, part, emit):
+    n = lax.axis_index("narrow")
+    chans, cells = face.shape[2:]
     lane, first, final = shallow_lanes(cells)
     pairing = pair_matrix(cells)
-    stacks = [row_windows(face[t], rim[0, t], rim[1, t], n, narrow) for t in range(2)]
+    stacks = [row_windows(face[t], core_row[t], far_row[t, 0:chans], n, narrow) for t in range(2)]
     for win in range(2):
         pre = []
         for t in range(2):
@@ -175,7 +194,7 @@
         emit(win, [v.reshape(2, 64, cells) for v in out], pool_plane(out, pairing))
 
 
-def near_kernel(narrow, r_e, x_e, t_s, part, skip_f, skip_t, pool_part):
+def near_kernel(narrow, r_e, c_e, m_e, t_s, part, skip_f, skip_t, pool_part):
     odd = lax.rem(lax.axis_index("wide"), 2)
 
     def emit(win, out, pool):
@@ -183,10 +202,10 @@
             ref[2 * win : 2 * win + 2] = out[t]
         pool_part[win] = pool
 
-    finish_plane(narrow, 1 - odd, t_s[2 - 2 * odd], r_e, x_e, part, emit)
-
-
-def far_kernel(wide, narrow, r_o, x_o, t_s, part, pool_part, skip_f, skip_t, pooled):
+    finish_plane(narrow, 1 - odd, t_s[2 - 2 * odd], r_e, c_e, m_e, part, emit)
+
+
+def far_kernel(wide, narrow, r_o, c_o, m_o, t_s, part, pool_part, skip_f, skip_t, pooled):
     w = lax.axis_index("wide")
     odd = lax.rem(w, 2)
 
@@ -197,7 +216,7 @@
 
     taps = t_s[2 * odd]
     taps = jnp.where((w > 0) & (w < wide - 1), taps, jnp.zeros_like(taps))
-    finish_plane(narrow, odd, taps, r_o, x_o, part, emit)
+    finish_plane(narrow, odd, taps, r_o, c_o, m_o, part, emit)
 
 
 def deep_lanes(cells):
@@ -207,18 +226,18 @@
     return lane, first, final
 
 
-def gather_rows(x, mine, sibling, far, narrow):
+def gather_rows(x, parts, far, narrow):
     n = lax.axis_index("narrow")
     sib = n + 1 - 2 * lax.rem(n, 2)
-    pair = mine.shape[1]
+    pair = parts[0].shape[0]
     x[0] = jnp.zeros(x.shape[1:], BF16)
     x[narrow * pair + 1] = jnp.zeros(x.shape[1:], BF16)
-    for source, member in ((mine, n), (sibling, sib)):
-        for k in range(2):
-            owner = lax.rem(member + 2 * k, narrow)
-            if far is not None:
-                owner = jnp.where(far, lax.rem(member + 2 - 2 * k, narrow), owner)
-            x[pl.ds(owner * pair + 1, pair)] = source[k]
+    for k, source in enumerate(parts):
+        member = n if k < 2 else sib
+        owner = lax.rem(member + 2 * (k % 2), narrow)
+        if far is not None:
+            owner = jnp.where(far, lax.rem(member + 2 - 2 * (k % 2), narrow), owner)
+        x[pl.ds(owner * pair + 1, pair)] = source[...]
 
 
 def deep_sum(x, taps, j, lane, first, final):
@@ -227,8 +246,8 @@
     return shifted_sum(acc, lane, first, final)
 
 
-def deep_own_kernel(narrow, group, g_c, t_d, near_f, near_t, far_f, far_t, part, order, skip_f, skip_t,
-                    x, sems):
+def deep_near_kernel(narrow, own, across, own_c, across_c, e, e_across, e_c, e_across_c, t_d, near_f, near_t, far_f, far_t,
+                     total, skip_f, skip_t, x, y, sems):
     odd = lax.rem(lax.axis_index("wide"), 2)
     wait = run_copies(
         [
@@ -239,28 +258,23 @@
         ],
         sems,
     )
-    order[...] = jnp.zeros_like(order)
-    gather_rows(x, group, g_c, None, narrow)
-    lanes = deep_lanes(x.shape[2] // 2)
-    for j in range(part.shape[0]):
-        part[j] = deep_sum(x, t_d[1], j, *lanes)
+    gather_rows(x, (own, across, own_c, across_c), None, narrow)
+    gather_rows(y, (e, e_across, e_c, e_across_c), None, narrow)
+    cells = x.shape[2]
+    lanes = deep_lanes(cells // 2)
+    taps = jnp.concatenate([t_d[1], t_d[2 - 2 * odd]], axis=1)
+    for j in range(total.shape[0]):
+        stack = [v[2 * j : 2 * j + 4].reshape(256, cells) for v in (x, y)]
+        acc = jnp.dot(taps, jnp.concatenate(stack, axis=0), preferred_element_type=F32)
+        total[j] = shifted_sum(acc, *lanes)
     wait()
 
 
-def deep_near_kernel(narrow, r_e, e_c, t_d, part, total, x):
-    odd = lax.rem(lax.axis_index("wide"), 2)
-    gather_rows(x, r_e, e_c, None, narrow)
-    lanes = deep_lanes(x.shape[2] // 2)
-    taps = t_d[2 - 2 * odd]
-    for j in range(part.shape[0]):
-        total[j] = part[j] + deep_sum(x, taps, j, *lanes)
-
-
-def deep_far_kernel(wide, narrow, r_o, o_c, t_d, part, out_f, out_t, x):
+def deep_far_kernel(wide, narrow, o, o_across, o_c, o_across_c, t_d, part, out_f, out_t, x):
     w = lax.axis_index("wide")
     cells = x.shape[2] // 2
     far = (w == wide // 2 - 1) | (w == wide // 2)
-    gather_rows(x, r_o, o_c, far, narrow)
+    gather_rows(x, (o, o_across, o_c, o_across_c), far, narrow)
     lanes = deep_lanes(cells)
     taps = t_d[2 * lax.rem(w, 2)]
     taps = jnp.where((w > 0) & (w < wide - 1), taps, jnp.zeros_like(taps))
@@ -289,7 +303,6 @@
         pltpu.with_memory_space_constraint(v, pltpu.HBM)
         for v in (volume, volume_tangent, shallow_weight, deep_weight)
     )
-    odd = lax.axis_index("wide") % 2
     dma = pltpu.SemaphoreType.DMA
 
     def swap(v, kind, route):
@@ -298,66 +311,66 @@
     def full(*shape):
         return jax.ShapeDtypeStruct(shape, F32)
 
-    face, edge = (2, rows, chans, cells), (planes, 2, chans, cells)
+    plane, edge = (rows, chans, cells), (planes, 2, chans, cells)
     s_o, s_e, s_c, s_m = call(
-        slices_kernel, [face, face, edge, edge], [HBM] * 2, [ANY] * 4, [dma((8,))]
+        slices_kernel, [(2,) + plane, (2,) + plane, edge, edge],
+        [HBM] * 2, [ANY] * 4, [dma((8,))],
     )(volume, volume_tangent)
     r_o = swap(s_o, "O", "same")
     r_e = swap(s_e, "E", "same")
     r_c = swap(s_c, "", "core")
     r_m = swap(s_m, "", "mirror")
-    rim = jnp.stack([r_c, r_m])
-    x_o = swap(lax.dynamic_index_in_dim(rim, odd, 1, keepdims=False), "O", "same")
-    x_e = swap(lax.dynamic_index_in_dim(rim, 1 - odd, 1, keepdims=False), "E", "same")
     band = (3, 384, 256)
-    t_s, t_d = call(
-        weights_kernel, [band, band], [HBM] * 2, [VMEM, VMEM],
+    t_s, t_d, own = call(
+        weights_kernel, [band, band, (2,) + volume.shape], [HBM] * 4, [VMEM, VMEM, ANY],
         [
             pltpu.VMEM((3, 3, 3, 64, 128), BF16),
             pltpu.VMEM((3, 3, 3, 64, 64), BF16),
             pltpu.VMEM((9, 320, 64), BF16),
             pltpu.VMEM((9, 320, 128), BF16),
             dma((2,)),
+            dma((2,)),
         ],
-    )(shallow_weight, deep_weight)
+    )(volume, volume_tangent, shallow_weight, deep_weight)
     wins = rows // 2
     (part,) = call(
         functools.partial(own_kernel, narrow),
-        [full(planes, 2, wins, 128, cells)], [HBM] * 2 + [VMEM] * 3, [VMEM],
-        [pltpu.VMEM((2, planes, rows, chans, cells), BF16), dma((2,))],
-    )(volume, volume_tangent, r_c, r_m, t_s)
-    plane = (rows, chans, cells)
+        [full(planes, 2, wins, 128, cells)], [VMEM] * 4, [VMEM],
+    )(own, r_c, r_m, t_s)
+    corners = [(2, chans, cells), (2, chans + PAD, cells)]
+    row_ec, row_em = call(edge_kernel, corners, [VMEM], [VMEM] * 2)(r_e)
+    c_e, m_e = swap(row_ec, "", "core"), swap(row_em, "", "mirror")
+    row_oc, row_om = call(edge_kernel, corners, [VMEM] * 3, [VMEM] * 2)(r_o, part, row_ec)
+    c_o, m_o = swap(row_oc, "", "core"), swap(row_om, "", "mirror")
     near_f, near_t, pool_part = call(
         functools.partial(near_kernel, narrow),
-        [plane, plane, full(wins, chans, cells)], [VMEM] * 4, [VMEM] * 3,
-    )(r_e, x_e, t_s, part)
+        [plane, plane, full(wins, chans, cells)], [VMEM] * 5, [VMEM] * 3,
+    )(r_e, c_e, m_e, t_s, part)
     far_f, far_t, pooled = call(
         functools.partial(far_kernel, wide, narrow),
-        [plane, plane, (wins, chans, cells)], [VMEM] * 5, [VMEM] * 3,
-    )(r_o, x_o, t_s, part, pool_part)
-    other = swap(pooled, "", "across")
-    group = jnp.stack([pooled, other])
-    o2 = swap(group, "O", "near")
-    e2 = swap(group, "E", "same")
-    g_c = swap(group, "", "core")
+        [plane, plane, (wins, chans, cells)], [VMEM] * 6, [VMEM] * 3,
+    )(r_o, c_o, m_o, t_s, part, pool_part)
+    o2 = swap(pooled, "O", "near")
+    e2 = swap(pooled, "E", "same")
+    across = swap(pooled, "", "across")
+    e_across = swap(e2, "", "across")
+    o_across = swap(o2, "", "across")
+    own_c, across_c = swap(pooled, "", "core"), swap(across, "", "core")
+    e_c, e_across_c = swap(e2, "", "core"), swap(e_across, "", "core")
+    o_c, o_across_c = swap(o2, "", "core"), swap(o_across, "", "core")
     deep_rows = wins * narrow
     sums = full(deep_rows // 2, 128, cells)
     gathered = pltpu.VMEM((deep_rows + 2, chans, cells), BF16)
-    part_d, order, skip_f, skip_t = call(
-        functools.partial(deep_own_kernel, narrow),
-        [sums, (chans, cells), volume.shape, volume.shape],
-        [VMEM] * 7, [VMEM, VMEM, HBM, HBM], [gathered, dma((4,))],
-    )(group, g_c, t_d, near_f, near_t, far_f, far_t)
-    e_c = swap(e2, "", "core")
-    o_c = swap(o2 + order, "", "core")
-    (total_d,) = call(
-        functools.partial(deep_near_kernel, narrow), [sums], [VMEM] * 4, [VMEM], [gathered]
-    )(e2, e_c, t_d, part_d)
+    total_d, skip_f, skip_t = call(
+        functools.partial(deep_near_kernel, narrow),
+        [sums, volume.shape, volume.shape],
+        [VMEM] * 13, [VMEM, HBM, HBM], [gathered, gathered, dma((4,))],
+    )(pooled, across, own_c, across_c, e2, e_across, e_c, e_across_c, t_d, near_f, near_t, far_f, far_t)
     deep_shape = (1, deep_rows, 64, cells // 2)
     deep_f, deep_t = call(
         functools.partial(deep_far_kernel, wide, narrow),
-        [deep_shape, deep_shape], [VMEM] * 4, [VMEM] * 2, [gathered],
-    )(o2, o_c, t_d, total_d)
+        [deep_shape, deep_shape], [VMEM] * 6, [VMEM] * 2, [gathered],
+    )(o2, o_across, o_c, o_across_c, t_d, total_d)
     return skip_f, skip_t, deep_f, deep_t
 
 

time: 43 us -> 40.9 us (0.951); the launches traced: 42.9 us -> 40.3 us
  waiting for transfers between devices: 6.92 us -> 3.53 us
  starting transfers between devices: 24.8 us -> 27 us
  Pallas kernels: 10.4 us -> 9.02 us
    ppermute x12 -> x19, waiting for transfers between devices: 6.92 us -> 3.53 us  [swap(): return lax.ppermute(v, BOTH, exchange(wide, narrow, kind, route))]
    ppermute x12 -> x19, starting transfers between devices: 24.8 us -> 27 us  [swap(): return lax.ppermute(v, BOTH, exchange(wide, narrow, kind, route))]
    pallas_call x1, Pallas kernels: 2.14 us -> 1.09 us  [local(): call(functools.partial(own_kernel, narrow), [full(planes, 2, wins, 128, c...]
    pallas_call x4 -> x5, Pallas kernels: 5.2 us -> 4.92 us  [the longest x1 2.22 us: local(): call(weights_kernel, [band, band, (2,) + volume.shape], [HBM] * 4, [VMEM,...]
  transfers between devices with their start and end apart: 12 -> 19, of which waited for: 3 -> 4; matrix products, arithmetic and copies ran while one was open for 0% -> 0% of each run, Pallas kernels for 16% -> 14%
where the time goes in v3:
time: 40.9 us; the launch traced here: 40.3 us
  starting transfers between devices  27 us (66%)
  Pallas kernels  9.02 us (22%)
  waiting for transfers between devices  3.53 us (9%)
  between operations  0.77 us (2%)
    ppermute x19, starting transfers between devices, swap(): return lax.ppermute(v, BOTH, exchange(wide, narrow, kind, route))  27 us
    ppermute x19, waiting for transfers between devices, swap(): return lax.ppermute(v, BOTH, exchange(wide, narrow, kind, route))  3.53 us
    pallas_call x1, Pallas kernels, local(): call(weights_kernel, [band, band, (2,) + volume.shape], [HBM] * 4, [VMEM,...  2.22 us
    pallas_call x1, Pallas kernels, local(): call(functools.partial(deep_near_kernel, narrow), [sums, volume.shape, vo...  1.4 us
    pallas_call x1, Pallas kernels, local(): call(functools.partial(deep_far_kernel, wide, narrow), [deep_shape, deep_...  1.27 us
    pallas_call x1, Pallas kernels, local(): call(slices_kernel, [(2,) + plane, (2,) + plane, edge, edge], [HBM] * 2,...  1.25 us
    pallas_call x1, Pallas kernels, local(): call(functools.partial(own_kernel, narrow), [full(planes, 2, wins, 128, c...  1.09 us
    pallas_call x1, Pallas kernels, local(): call(functools.partial(far_kernel, wide, narrow), [plane, plane, (wins, c...  0.88 us
  transfers between devices with their start and end apart: 19, of which 4 were waited for; matrix products, arithmetic and copies ran while one was open for 0% of the time, Pallas kernels for 14%

profile of v3, /device:TPU:25, one launch (start us, length us, event | category | flops | bytes accessed | tf_op | source)
XLA Modules:
  0.0 40.3 jit_solution(4469913175580747510)
XLA Ops:
  0.6 1.3 %shard_map.75 = (bf16[2,4,64,256]{3,2,1,0:T(8,128)(2,1)S(1)}, bf16[2,4,64,256]{3,2,1,0:T(8,128)(2,1)S(1)}, bf16[2,2,64,256]{3,2,1,0:T(8,128)(2,1)S(1)}, bf16[2,2,64,256]{3,2,1,0:T(8,128)(2,1)S(1)}) custom-call(bf16[2,4,64,256]{3,2,1,0:T(8,128)(2,1)} %vol.3, bf16[2,4,64,256]{3,2,1,0:T(8,128)(2,1)} %tan.3), custom_call_target="tpu_custom_call" | custom-call | tf_op jit(solution)/shard_map/pallas_call | solution.py:315
  1.9 1.3 %collective-permute-start.3 = (bf16[2,4,64,256]{3,2,1,0:T(8,128)(2,1)S(1)}, bf16[2,4,64,256]{3,2,1,0:T(8,128)(2,1)S(1)}, u32[]{:S(2)}, u32[]{:S(2)}) collective-permute-start(bf16[2,4,64,256]{3,2,1,0:T(8,128)(2,1)S(1)} %get-tuple-element.31), channel_id=1, source_target_pairs={{0,4},{1,5},{2,6},{3,7},{4,0},{5,1},{6,2},{7,3},{8,12},{9,13},{10,... | collective-permute-start | bytes 786440 | tf_op jit(solution)/shard_map/ppermute | solution.py:309
  3.2 7.8 %collective-permute-start = (bf16[2,4,64,256]{3,2,1,0:T(8,128)(2,1)S(1)}, bf16[2,4,64,256]{3,2,1,0:T(8,128)(2,1)S(1)}, u32[]{:S(2)}, u32[]{:S(2)}) collective-permute-start(bf16[2,4,64,256]{3,2,1,0:T(8,128)(2,1)S(1)} %get-tuple-element.26), channel_id=1, source_target_pairs={{0,1},{1,0},{2,3},{3,2},{4,8},{5,9},{6,10},{7,11},{8,4},{9,5},{10,... | collective-permute-start | bytes 786440 | tf_op jit(solution)/shard_map/ppermute | solution.py:309
  11.0 1.2 %collective-permute-start.1 = (bf16[2,2,64,256]{3,2,1,0:T(8,128)(2,1)S(1)}, bf16[2,2,64,256]{3,2,1,0:T(8,128)(2,1)S(1)}, u32[]{:S(2)}, u32[]{:S(2)}) collective-permute-start(bf16[2,2,64,256]{3,2,1,0:T(8,128)(2,1)S(1)} %get-tuple-element.28), channel_id=1, source_target_pairs={{0,1},{1,0},{2,3},{3,2},{4,5},{5,4},{6,7},{7,6},{8,9},{9,8},{10,11... | collective-permute-start | bytes 393224 | tf_op jit(solution)/shard_map/ppermute | solution.py:309
  12.2 2.2 %shard_map.76 = (bf16[3,384,256]{2,1,0:T(8,128)(2,1)S(1)}, bf16[3,384,256]{2,1,0:T(8,128)(2,1)S(1)}, bf16[2,2,4,64,256]{4,3,2,1,0:T(8,128)(2,1)S(1)}) custom-call(bf16[2,4,64,256]{3,2,1,0:T(8,128)(2,1)} %vol.3, bf16[2,4,64,256]{3,2,1,0:T(8,128)(2,1)} %tan.3, bf16[3,3,3,64,64]{4,3,2,1,0:T(8,128)(2,1)} %sw.1, bf16[3,3,3,64,256]{4,3,2,1,0:T(8,128)(2,1)} %dw.1), custom_call_target="tpu_custom_call" | custom-call | tf_op jit(solution)/shard_map/pallas_call | solution.py:324
  14.4 1.9 %collective-permute-done.2.r_m = bf16[2,2,64,256]{3,2,1,0:T(8,128)(2,1)S(1)} collective-permute-done((bf16[2,2,64,256]{3,2,1,0:T(8,128)(2,1)S(1)}, bf16[2,2,64,256]{3,2,1,0:T(8,128)(2,1)S(1)}, u32[]{:S(2)}, u32[]{:S(2)}) %collective-permute-start.2) | collective-permute-done | bytes 131104 | tf_op jit(solution)/shard_map/ppermute | solution.py:309
  16.3 1.1 %shard_map.77.rest_0_.part = f32[2,2,2,128,256]{4,3,2,1,0:T(8,128)S(1)} custom-call(bf16[2,2,4,64,256]{4,3,2,1,0:T(8,128)(2,1)S(1)} %get-tuple-element.27.x, bf16[2,2,64,256]{3,2,1,0:T(8,128)(2,1)S(1)} %collective-permute-done.1.r_c, bf16[2,2,64,256]{3,2,1,0:T(8,128)(2,1)S(1)} %collective-permute-done.2.r_m, bf16[3,384,256]{2,1,0:T(8,128)(2,1)S(1)} %get-tuple-element.30.t_s), custom_call_target="tpu_custom_call" | custom-call | tf_op jit(solution)/shard_map/pallas_call | solution.py:336
  17.6 1.5 %collective-permute-start.5 = (bf16[2,80,256]{2,1,0:T(8,128)(2,1)S(1)}, bf16[2,80,256]{2,1,0:T(8,128)(2,1)S(1)}, u32[]{:S(2)}, u32[]{:S(2)}) collective-permute-start(bf16[2,80,256]{2,1,0:T(8,128)(2,1)S(1)} %get-tuple-element.34), channel_id=1, source_target_pairs={{0,16},{1,2},{2,1},{3,19},{4,20},{5,6},{6,5},{7,23},{8,24},{9,10},... | collective-permute-start | bytes 245768 | tf_op jit(solution)/shard_map/ppermute | solution.py:309
  19.1 0.6 %collective-permute-start.6 = (bf16[2,64,256]{2,1,0:T(8,128)(2,1)S(1)}, bf16[2,64,256]{2,1,0:T(8,128)(2,1)S(1)}, u32[]{:S(2)}, u32[]{:S(2)}) collective-permute-start(bf16[2,64,256]{2,1,0:T(8,128)(2,1)S(1)} %get-tuple-element.32.rest_1_), channel_id=1, source_target_pairs={{0,1},{1,0},{2,3},{3,2},{4,5},{5,4},{6,7},{7,6},{8,9},{9,8},{10,11... | collective-permute-start | bytes 196616 | tf_op jit(solution)/shard_map/ppermute | solution.py:309
  19.7 0.9 %collective-permute-done.6.c_e = bf16[2,64,256]{2,1,0:T(8,128)(2,1)S(1)} collective-permute-done((bf16[2,64,256]{2,1,0:T(8,128)(2,1)S(1)}, bf16[2,64,256]{2,1,0:T(8,128)(2,1)S(1)}, u32[]{:S(2)}, u32[]{:S(2)}) %collective-permute-start.6) | collective-permute-done | bytes 65568 | tf_op jit(solution)/shard_map/ppermute | solution.py:309
  20.6 0.5 %collective-permute-done.7.m_e = bf16[2,80,256]{2,1,0:T(8,128)(2,1)S(1)} collective-permute-done((bf16[2,80,256]{2,1,0:T(8,128)(2,1)S(1)}, bf16[2,80,256]{2,1,0:T(8,128)(2,1)S(1)}, u32[]{:S(2)}, u32[]{:S(2)}) %collective-permute-start.7) | collective-permute-done | bytes 81952 | tf_op jit(solution)/shard_map/ppermute | solution.py:309
  21.1 0.9 %shard_map.80 = (bf16[4,64,256]{2,1,0:T(8,128)(2,1)S(1)}, bf16[4,64,256]{2,1,0:T(8,128)(2,1)S(1)}, f32[2,64,256]{2,1,0:T(8,128)S(1)}) custom-call(bf16[2,4,64,256]{3,2,1,0:T(8,128)(2,1)S(1)} %collective-permute-done.3.face.r_e, bf16[2,64,256]{2,1,0:T(8,128)(2,1)S(1)} %collective-permute-done.6.c_e, bf16[2,80,256]{2,1,0:T(8,128)(2,1)S(1)} %collective-permute-done.7.m_e, ...), custom_call_target="tpu_custom_call" | custom-call | tf_op jit(solution)/shard_map/pallas_call | solution.py:345
  22.0 0.9 %shard_map.81 = (bf16[4,64,256]{2,1,0:T(8,128)(2,1)S(1)}, bf16[4,64,256]{2,1,0:T(8,128)(2,1)S(1)}, bf16[2,64,256]{2,1,0:T(8,128)(2,1)S(1)}) custom-call(bf16[2,4,64,256]{3,2,1,0:T(8,128)(2,1)S(1)} %collective-permute-done.face.r_o, bf16[2,64,256]{2,1,0:T(8,128)(2,1)S(1)} %collective-permute-done.4.c_o, bf16[2,80,256]{2,1,0:T(8,128)(2,1)S(1)} %collective-permute-done.5.m_o, ...), custom_call_target="tpu_custom_call" | custom-call | tf_op jit(solution)/shard_map/pallas_call | solution.py:349
  22.9 0.1 collective-permute-start.11
  23.0 6.1 %collective-permute-start.15 = (bf16[2,64,256]{2,1,0:T(8,128)(2,1)S(1)}, bf16[2,64,256]{2,1,0:T(8,128)(2,1)S(1)}, u32[]{:S(2)}, u32[]{:S(2)}) collective-permute-start(bf16[2,64,256]{2,1,0:T(8,128)(2,1)S(1)} %get-tuple-element.37.own), channel_id=1, source_target_pairs={{0,1},{1,0},{2,3},{3,2},{4,8},{5,9},{6,10},{7,11},{8,4},{9,5},{10,... | collective-permute-start | bytes 196616 | tf_op jit(solution)/shard_map/ppermute | solution.py:309
  29.1 1.5 %collective-permute-start.12 = (bf16[2,64,256]{2,1,0:T(8,128)(2,1)S(1)}, bf16[2,64,256]{2,1,0:T(8,128)(2,1)S(1)}, u32[]{:S(2)}, u32[]{:S(2)}) collective-permute-start(bf16[2,64,256]{2,1,0:T(8,128)(2,1)S(1)} %collective-permute-done.11.e), channel_id=1, source_target_pairs={{0,2},{1,3},{2,0},{3,1},{4,6},{5,7},{6,4},{7,5},{8,10},{9,11},{10,... | collective-permute-start | bytes 196616 | tf_op jit(solution)/shard_map/ppermute | solution.py:309
  30.5 2.6 %collective-permute-start.9 = (bf16[2,64,256]{2,1,0:T(8,128)(2,1)S(1)}, bf16[2,64,256]{2,1,0:T(8,128)(2,1)S(1)}, u32[]{:S(2)}, u32[]{:S(2)}) collective-permute-start(bf16[2,64,256]{2,1,0:T(8,128)(2,1)S(1)} %get-tuple-element.37.own), channel_id=1, source_target_pairs={{0,1},{1,0},{2,3},{3,2},{4,5},{5,4},{6,7},{7,6},{8,9},{9,8},{10,11... | collective-permute-start | bytes 196616 | tf_op jit(solution)/shard_map/ppermute | solution.py:309
  33.1 0.3 collective-permute-start.13
  33.3 2.0 %collective-permute-start.10 = (bf16[2,64,256]{2,1,0:T(8,128)(2,1)S(1)}, bf16[2,64,256]{2,1,0:T(8,128)(2,1)S(1)}, u32[]{:S(2)}, u32[]{:S(2)}) collective-permute-start(bf16[2,64,256]{2,1,0:T(8,128)(2,1)S(1)} %collective-permute-done.8.across), channel_id=1, source_target_pairs={{0,1},{1,0},{2,3},{3,2},{4,5},{5,4},{6,7},{7,6},{8,9},{9,8},{10,11... | collective-permute-start | bytes 196616 | tf_op jit(solution)/shard_map/ppermute | solution.py:309
  35.3 0.7 %collective-permute-start.14 = (bf16[2,64,256]{2,1,0:T(8,128)(2,1)S(1)}, bf16[2,64,256]{2,1,0:T(8,128)(2,1)S(1)}, u32[]{:S(2)}, u32[]{:S(2)}) collective-permute-start(bf16[2,64,256]{2,1,0:T(8,128)(2,1)S(1)} %collective-permute-done.12.e_across), channel_id=1, source_target_pairs={{0,1},{1,0},{2,3},{3,2},{4,5},{5,4},{6,7},{7,6},{8,9},{9,8},{10,11... | collective-permute-start | bytes 196616 | tf_op jit(solution)/shard_map/ppermute | solution.py:309
  36.0 0.2 collective-permute-done.16.o_across
  36.2 1.4 %collective-permute-start.18 = (bf16[2,64,256]{2,1,0:T(8,128)(2,1)S(1)}, bf16[2,64,256]{2,1,0:T(8,128)(2,1)S(1)}, u32[]{:S(2)}, u32[]{:S(2)}) collective-permute-start(bf16[2,64,256]{2,1,0:T(8,128)(2,1)S(1)} %collective-permute-done.16.o_across), channel_id=1, source_target_pairs={{0,1},{1,0},{2,3},{3,2},{4,5},{5,4},{6,7},{7,6},{8,9},{9,8},{10,11... | collective-permute-start | bytes 196616 | tf_op jit(solution)/shard_map/ppermute | solution.py:309
  37.6 1.4 %shard_map.82 = (f32[4,128,256]{2,1,0:T(8,128)S(1)}, bf16[2,4,64,256]{3,2,1,0:T(8,128)(2,1)}, bf16[2,4,64,256]{3,2,1,0:T(8,128)(2,1)}) custom-call(bf16[2,64,256]{2,1,0:T(8,128)(2,1)S(1)} %get-tuple-element.37.own, bf16[2,64,256]{2,1,0:T(8,128)(2,1)S(1)} %collective-permute-done.8.across, bf16[2,64,256]{2,1,0:T(8,128)(2,1)S(1)} %collective-permute-done.9.own_c, ...), custom_call_target="tpu_custom_call" | custom-call | tf_op jit(solution)/shard_map/pallas_call | solution.py:364
  39.1 1.3 %shard_map.83 = (bf16[1,8,64,128]{3,2,1,0:T(8,128)(2,1)}, bf16[1,8,64,128]{3,2,1,0:T(8,128)(2,1)}) custom-call(bf16[2,64,256]{2,1,0:T(8,128)(2,1)S(1)} %collective-permute-done.15.o, bf16[2,64,256]{2,1,0:T(8,128)(2,1)S(1)} %collective-permute-done.16.o_across, bf16[2,64,256]{2,1,0:T(8,128)(2,1)S(1)} %collective-permute-done.17.o_c, ...), custom_call_target="tpu_custom_call" | custom-call | tf_op jit(solution)/shard_map/pallas_call | solution.py:370
  (23 shorter events, 0.2 us)
Async XLA Ops:
  1.9 15.5 %collective-permute-start.3 = (bf16[2,4,64,256]{3,2,1,0:T(8,128)(2,1)S(1)}, bf16[2,4,64,256]{3,2,1,0:T(8,128)(2,1)S(1)}, u32[]{:S(2)}, u32[]{:S(2)}) collective-permute-start(bf16[2,4,64,256]{3,2,1,0:T(8,128)(2,1)S(1)} %get-tuple-element.31), channel_id=1, source_target_pairs={{0,4},{1,5},{2,6},{3,7},{4,0},{5,1},{6,2},{7,3},{8,12},{9,13},{10,... | collective-permute-start | bytes 786440 | tf_op jit(solution)/shard_map/ppermute | solution.py:309
  3.2 14.4 %collective-permute-start = (bf16[2,4,64,256]{3,2,1,0:T(8,128)(2,1)S(1)}, bf16[2,4,64,256]{3,2,1,0:T(8,128)(2,1)S(1)}, u32[]{:S(2)}, u32[]{:S(2)}) collective-permute-start(bf16[2,4,64,256]{3,2,1,0:T(8,128)(2,1)S(1)} %get-tuple-element.26), channel_id=1, source_target_pairs={{0,1},{1,0},{2,3},{3,2},{4,8},{5,9},{6,10},{7,11},{8,4},{9,5},{10,... | collective-permute-start | bytes 786440 | tf_op jit(solution)/shard_map/ppermute | solution.py:309
  11.0 3.5 %collective-permute-start.1 = (bf16[2,2,64,256]{3,2,1,0:T(8,128)(2,1)S(1)}, bf16[2,2,64,256]{3,2,1,0:T(8,128)(2,1)S(1)}, u32[]{:S(2)}, u32[]{:S(2)}) collective-permute-start(bf16[2,2,64,256]{3,2,1,0:T(8,128)(2,1)S(1)} %get-tuple-element.28), channel_id=1, source_target_pairs={{0,1},{1,0},{2,3},{3,2},{4,5},{5,4},{6,7},{7,6},{8,9},{9,8},{10,11... | collective-permute-start | bytes 393224 | tf_op jit(solution)/shard_map/ppermute | solution.py:309
  12.2 4.1 %collective-permute-start.2 = (bf16[2,2,64,256]{3,2,1,0:T(8,128)(2,1)S(1)}, bf16[2,2,64,256]{3,2,1,0:T(8,128)(2,1)S(1)}, u32[]{:S(2)}, u32[]{:S(2)}) collective-permute-start(bf16[2,2,64,256]{3,2,1,0:T(8,128)(2,1)S(1)} %get-tuple-element.29), channel_id=1, source_target_pairs={{0,16},{1,2},{2,1},{3,19},{4,20},{5,6},{6,5},{7,23},{8,24},{9,10},... | collective-permute-start | bytes 393224 | tf_op jit(solution)/shard_map/ppermute | solution.py:309
  17.5 3.7 %collective-permute-start.7 = (bf16[2,80,256]{2,1,0:T(8,128)(2,1)S(1)}, bf16[2,80,256]{2,1,0:T(8,128)(2,1)S(1)}, u32[]{:S(2)}, u32[]{:S(2)}) collective-permute-start(bf16[2,80,256]{2,1,0:T(8,128)(2,1)S(1)} %get-tuple-element.35), channel_id=1, source_target_pairs={{0,16},{1,2},{2,1},{3,19},{4,20},{5,6},{6,5},{7,23},{8,24},{9,10},... | collective-permute-start | bytes 245768 | tf_op jit(solution)/shard_map/ppermute | solution.py:309
  17.6 4.4 %collective-permute-start.5 = (bf16[2,80,256]{2,1,0:T(8,128)(2,1)S(1)}, bf16[2,80,256]{2,1,0:T(8,128)(2,1)S(1)}, u32[]{:S(2)}, u32[]{:S(2)}) collective-permute-start(bf16[2,80,256]{2,1,0:T(8,128)(2,1)S(1)} %get-tuple-element.34), channel_id=1, source_target_pairs={{0,16},{1,2},{2,1},{3,19},{4,20},{5,6},{6,5},{7,23},{8,24},{9,10},... | collective-permute-start | bytes 245768 | tf_op jit(solution)/shard_map/ppermute | solution.py:309
  19.1 1.5 %collective-permute-start.6 = (bf16[2,64,256]{2,1,0:T(8,128)(2,1)S(1)}, bf16[2,64,256]{2,1,0:T(8,128)(2,1)S(1)}, u32[]{:S(2)}, u32[]{:S(2)}) collective-permute-start(bf16[2,64,256]{2,1,0:T(8,128)(2,1)S(1)} %get-tuple-element.32.rest_1_), channel_id=1, source_target_pairs={{0,1},{1,0},{2,3},{3,2},{4,5},{5,4},{6,7},{7,6},{8,9},{9,8},{10,11... | collective-permute-start | bytes 196616 | tf_op jit(solution)/shard_map/ppermute | solution.py:309
  19.7 2.3 %collective-permute-start.4 = (bf16[2,64,256]{2,1,0:T(8,128)(2,1)S(1)}, bf16[2,64,256]{2,1,0:T(8,128)(2,1)S(1)}, u32[]{:S(2)}, u32[]{:S(2)}) collective-permute-start(bf16[2,64,256]{2,1,0:T(8,128)(2,1)S(1)} %get-tuple-element.33), channel_id=1, source_target_pairs={{0,1},{1,0},{2,3},{3,2},{4,5},{5,4},{6,7},{7,6},{8,9},{9,8},{10,11... | collective-permute-start | bytes 196616 | tf_op jit(solution)/shard_map/ppermute | solution.py:309
  22.9 6.2 %collective-permute-start.11 = (bf16[2,64,256]{2,1,0:T(8,128)(2,1)S(1)}, bf16[2,64,256]{2,1,0:T(8,128)(2,1)S(1)}, u32[]{:S(2)}, u32[]{:S(2)}) collective-permute-start(bf16[2,64,256]{2,1,0:T(8,128)(2,1)S(1)} %get-tuple-element.37.own), channel_id=1, source_target_pairs={{0,4},{1,5},{2,6},{3,7},{4,0},{5,1},{6,2},{7,3},{8,12},{9,13},{10,... | collective-permute-start | bytes 196616 | tf_op jit(solution)/shard_map/ppermute | solution.py:309
  23.0 10.1 %collective-permute-start.15 = (bf16[2,64,256]{2,1,0:T(8,128)(2,1)S(1)}, bf16[2,64,256]{2,1,0:T(8,128)(2,1)S(1)}, u32[]{:S(2)}, u32[]{:S(2)}) collective-permute-start(bf16[2,64,256]{2,1,0:T(8,128)(2,1)S(1)} %get-tuple-element.37.own), channel_id=1, source_target_pairs={{0,1},{1,0},{2,3},{3,2},{4,8},{5,9},{6,10},{7,11},{8,4},{9,5},{10,... | collective-permute-start | bytes 196616 | tf_op jit(solution)/shard_map/ppermute | solution.py:309
  29.1 4.3 %collective-permute-start.8 = (bf16[2,64,256]{2,1,0:T(8,128)(2,1)S(1)}, bf16[2,64,256]{2,1,0:T(8,128)(2,1)S(1)}, u32[]{:S(2)}, u32[]{:S(2)}) collective-permute-start(bf16[2,64,256]{2,1,0:T(8,128)(2,1)S(1)} %get-tuple-element.37.own), channel_id=1, source_target_pairs={{0,2},{1,3},{2,0},{3,1},{4,6},{5,7},{6,4},{7,5},{8,10},{9,11},{10,... | collective-permute-start | bytes 196616 | tf_op jit(solution)/shard_map/ppermute | solution.py:309
  29.1 6.3 %collective-permute-start.12 = (bf16[2,64,256]{2,1,0:T(8,128)(2,1)S(1)}, bf16[2,64,256]{2,1,0:T(8,128)(2,1)S(1)}, u32[]{:S(2)}, u32[]{:S(2)}) collective-permute-start(bf16[2,64,256]{2,1,0:T(8,128)(2,1)S(1)} %collective-permute-done.11.e), channel_id=1, source_target_pairs={{0,2},{1,3},{2,0},{3,1},{4,6},{5,7},{6,4},{7,5},{8,10},{9,11},{10,... | collective-permute-start | bytes 196616 | tf_op jit(solution)/shard_map/ppermute | solution.py:309
  30.5 5.5 %collective-permute-start.9 = (bf16[2,64,256]{2,1,0:T(8,128)(2,1)S(1)}, bf16[2,64,256]{2,1,0:T(8,128)(2,1)S(1)}, u32[]{:S(2)}, u32[]{:S(2)}) collective-permute-start(bf16[2,64,256]{2,1,0:T(8,128)(2,1)S(1)} %get-tuple-element.37.own), channel_id=1, source_target_pairs={{0,1},{1,0},{2,3},{3,2},{4,5},{5,4},{6,7},{7,6},{8,9},{9,8},{10,11... | collective-permute-start | bytes 196616 | tf_op jit(solution)/shard_map/ppermute | solution.py:309
  33.1 3.1 %collective-permute-start.16 = (bf16[2,64,256]{2,1,0:T(8,128)(2,1)S(1)}, bf16[2,64,256]{2,1,0:T(8,128)(2,1)S(1)}, u32[]{:S(2)}, u32[]{:S(2)}) collective-permute-start(bf16[2,64,256]{2,1,0:T(8,128)(2,1)S(1)} %collective-permute-done.15.o), channel_id=1, source_target_pairs={{0,2},{1,3},{2,0},{3,1},{4,6},{5,7},{6,4},{7,5},{8,10},{9,11},{10,... | collective-permute-start | bytes 196616 | tf_op jit(solution)/shard_map/ppermute | solution.py:309
  33.1 4.5 %collective-permute-start.13 = (bf16[2,64,256]{2,1,0:T(8,128)(2,1)S(1)}, bf16[2,64,256]{2,1,0:T(8,128)(2,1)S(1)}, u32[]{:S(2)}, u32[]{:S(2)}) collective-permute-start(bf16[2,64,256]{2,1,0:T(8,128)(2,1)S(1)} %collective-permute-done.11.e), channel_id=1, source_target_pairs={{0,1},{1,0},{2,3},{3,2},{4,5},{5,4},{6,7},{7,6},{8,9},{9,8},{10,11... | collective-permute-start | bytes 196616 | tf_op jit(solution)/shard_map/ppermute | solution.py:309
  33.3 4.3 %collective-permute-start.10 = (bf16[2,64,256]{2,1,0:T(8,128)(2,1)S(1)}, bf16[2,64,256]{2,1,0:T(8,128)(2,1)S(1)}, u32[]{:S(2)}, u32[]{:S(2)}) collective-permute-start(bf16[2,64,256]{2,1,0:T(8,128)(2,1)S(1)} %collective-permute-done.8.across), channel_id=1, source_target_pairs={{0,1},{1,0},{2,3},{3,2},{4,5},{5,4},{6,7},{7,6},{8,9},{9,8},{10,11... | collective-permute-start | bytes 196616 | tf_op jit(solution)/shard_map/ppermute | solution.py:309
  35.3 2.3 %collective-permute-start.14 = (bf16[2,64,256]{2,1,0:T(8,128)(2,1)S(1)}, bf16[2,64,256]{2,1,0:T(8,128)(2,1)S(1)}, u32[]{:S(2)}, u32[]{:S(2)}) collective-permute-start(bf16[2,64,256]{2,1,0:T(8,128)(2,1)S(1)} %collective-permute-done.12.e_across), channel_id=1, source_target_pairs={{0,1},{1,0},{2,3},{3,2},{4,5},{5,4},{6,7},{7,6},{8,9},{9,8},{10,11... | collective-permute-start | bytes 196616 | tf_op jit(solution)/shard_map/ppermute | solution.py:309
  36.0 3.0 %collective-permute-start.17 = (bf16[2,64,256]{2,1,0:T(8,128)(2,1)S(1)}, bf16[2,64,256]{2,1,0:T(8,128)(2,1)S(1)}, u32[]{:S(2)}, u32[]{:S(2)}) collective-permute-start(bf16[2,64,256]{2,1,0:T(8,128)(2,1)S(1)} %collective-permute-done.15.o), channel_id=1, source_target_pairs={{0,1},{1,0},{2,3},{3,2},{4,5},{5,4},{6,7},{7,6},{8,9},{9,8},{10,11... | collective-permute-start | bytes 196616 | tf_op jit(solution)/shard_map/ppermute | solution.py:309
  36.2 2.8 %collective-permute-start.18 = (bf16[2,64,256]{2,1,0:T(8,128)(2,1)S(1)}, bf16[2,64,256]{2,1,0:T(8,128)(2,1)S(1)}, u32[]{:S(2)}, u32[]{:S(2)}) collective-permute-start(bf16[2,64,256]{2,1,0:T(8,128)(2,1)S(1)} %collective-permute-done.16.o_across), channel_id=1, source_target_pairs={{0,1},{1,0},{2,3},{3,2},{4,5},{5,4},{6,7},{7,6},{8,9},{9,8},{10,11... | collective-permute-start | bytes 196616 | tf_op jit(solution)/shard_map/ppermute | solution.py:309

commit v4 on v3

--- a/solution.py
+++ b/solution.py
@@ -34,10 +34,10 @@
                 pn = n
             elif route == "core":
                 pn = n ^ 1
-            elif route == "mirror" and 0 < n < narrow - 1:
+            elif route in ("mirror", "corner") and 0 < n < narrow - 1:
                 pn = narrow - 1 - n
-            elif route == "mirror":
-                if wide % 8 == 0 and (w | 4) % (wide // 2) != wide // 2 - 1:
+            elif route in ("mirror", "corner"):
+                if wide % 8 == 0 and (route == "corner" or (w | 4) % (wide // 2) != wide // 2 - 1):
                     pw, pn = w ^ 4, n
                 else:
                     pw, pn = (w + wide // 2) % wide, narrow - 1 - n
@@ -67,12 +67,11 @@
     row_m = jnp.where(n < 2, last, 0)
     copies = []
     for t, src in enumerate((vol, tan)):
-        copies += [
-            (src.at[odd], s_o.at[t]),
-            (src.at[1 - odd], s_e.at[t]),
-            (src.at[:, row_c], s_c.at[:, t]),
-            (src.at[:, row_m], s_m.at[:, t]),
-        ]
+        for plane, face in ((odd, s_o), (1 - odd, s_e)):
+            for half in range(2):
+                rows = pl.ds(2 * half, 2)
+                copies.append((src.at[plane, rows], face.at[t, rows]))
+        copies += [(src.at[:, row_c], s_c.at[:, t]), (src.at[:, row_m], s_m.at[:, t])]
     run_copies(copies, sems)()
 
 
@@ -131,10 +130,7 @@
 
 
 def pool_plane(out, pairing):
-    halves = []
-    for value in out:
-        half = jnp.dot(value, pairing, preferred_element_type=F32)
-        halves.append(half[0:64] + half[64:128])
+    halves = [jnp.dot(value, pairing, preferred_element_type=F32) for value in out]
     return jnp.concatenate(halves, axis=1)
 
 
@@ -160,9 +156,11 @@
     n = lax.axis_index("narrow")
     last = face.shape[1] - 1
     for t in range(2):
-        row_c[t] = jnp.where(lax.rem(n, 2) == 0, face[t, last], face[t, 0])
-        row_m[t, 0 : face.shape[2]] = jnp.where(n < 2, face[t, last], face[t, 0])
-        row_m[t, face.shape[2] :] = jnp.zeros((PAD, face.shape[3]), BF16)
+        for row, is_last in ((row_c, lax.rem(n, 2) == 0), (row_m, n < 2)):
+            chans = face.shape[2]
+            row[t, 0:chans] = jnp.where(is_last, face[t, last], face[t, 0])
+            if row.shape[1] > chans:
+                row[t, chans:] = jnp.zeros((row.shape[1] - chans, face.shape[3]), BF16)
 
 
 def own_kernel(narrow, x, r_c, r_m, t_s, part):
@@ -184,39 +182,78 @@
     chans, cells = face.shape[2:]
     lane, first, final = shallow_lanes(cells)
     pairing = pair_matrix(cells)
-    stacks = [row_windows(face[t], core_row[t], far_row[t, 0:chans], n, narrow) for t in range(2)]
+    stacks = []
+    for t in range(2):
+        far = jnp.zeros((chans, cells), BF16) if far_row is None else far_row[t, 0:chans]
+        stacks.append(row_windows(face[t], core_row[t, 0:chans], far, n, narrow))
     for win in range(2):
         pre = []
         for t in range(2):
             acc = jnp.dot(taps, stacks[t][win], preferred_element_type=F32)
             pre.append(part[q, t, win] + shifted_sum(acc, lane, first, final))
         out = activate(*pre)
-        emit(win, [v.reshape(2, 64, cells) for v in out], pool_plane(out, pairing))
+        emit(win, pre, [v.reshape(2, 64, cells) for v in out], pool_plane(out, pairing))
 
 
 def near_kernel(narrow, r_e, c_e, m_e, t_s, part, skip_f, skip_t, pool_part):
     odd = lax.rem(lax.axis_index("wide"), 2)
 
-    def emit(win, out, pool):
+    def emit(win, pre, out, pool):
         for t, ref in enumerate((skip_f, skip_t)):
             ref[2 * win : 2 * win + 2] = out[t]
-        pool_part[win] = pool
+        pool_part[win] = pool[0:64] + pool[64:128]
 
     finish_plane(narrow, 1 - odd, t_s[2 - 2 * odd], r_e, c_e, m_e, part, emit)
 
 
-def far_kernel(wide, narrow, r_o, c_o, m_o, t_s, part, pool_part, skip_f, skip_t, pooled):
+def far_taps(wide, t_s):
     w = lax.axis_index("wide")
-    odd = lax.rem(w, 2)
-
-    def emit(win, out, pool):
+    taps = t_s[2 * lax.rem(w, 2)]
+    return jnp.where((w > 0) & (w < wide - 1), taps, jnp.zeros_like(taps))
+
+
+def far_kernel(wide, narrow, r_o, c_o, t_s, part, pool_part, skip_f, skip_t, pool_far, edge_pre):
+    odd = lax.rem(lax.axis_index("wide"), 2)
+    even_n = lax.rem(lax.axis_index("narrow"), 2) == 0
+
+    def emit(win, pre, out, pool):
         for t, ref in enumerate((skip_f, skip_t)):
             ref[2 * win : 2 * win + 2] = out[t]
-        pooled[win] = (pool_part[win] + pool).astype(BF16)
-
-    taps = t_s[2 * odd]
-    taps = jnp.where((w > 0) & (w < wide - 1), taps, jnp.zeros_like(taps))
-    finish_plane(narrow, odd, taps, r_o, c_o, m_o, part, emit)
+        none = jnp.zeros_like(pool[0:64])
+        if win == 0:
+            pool_far[0] = pool_part[0] + jnp.where(even_n, none, pool[0:64]) + pool[64:128]
+            for t in range(2):
+                edge_pre[t] = pre[t][0:64]
+        else:
+            pool_far[1] = pool_part[1] + pool[0:64] + jnp.where(even_n, pool[64:128], none)
+            for t in range(2):
+                edge_pre[t] = jnp.where(even_n, edge_pre[t], pre[t][64:128])
+
+    finish_plane(narrow, odd, far_taps(wide, t_s), r_o, c_o, None, part, emit)
+
+
+def edge_row_kernel(wide, narrow, m_o, t_s, edge_pre, pool_far, edge_f, edge_t, pooled):
+    n = lax.axis_index("narrow")
+    chans, cells = edge_pre.shape[1:]
+    even_n = lax.rem(n, 2) == 0
+    has_m = (n > 0) & (n < narrow - 1)
+    lane, first, final = shallow_lanes(cells)
+    taps = far_taps(wide, t_s)
+    pre = []
+    for t in range(2):
+        row = m_o[t, 0:chans]
+        row = jnp.where(has_m, row, jnp.zeros_like(row))
+        none = jnp.zeros_like(row)
+        stack = [jnp.where(even_n, row, none), none, none, jnp.where(even_n, none, row)]
+        acc = jnp.dot(taps, jnp.concatenate(stack, axis=0), preferred_element_type=F32)
+        both = shifted_sum(acc, lane, first, final)
+        pre.append(edge_pre[t] + jnp.where(even_n, both[0:chans], both[chans:]))
+    out = activate(*pre)
+    edge_f[...], edge_t[...] = out
+    pool = pool_plane(out, pair_matrix(cells))
+    for win in range(2):
+        mine = even_n if win == 0 else jnp.logical_not(even_n)
+        pooled[win] = (pool_far[win] + jnp.where(mine, pool, jnp.zeros_like(pool))).astype(BF16)
 
 
 def deep_lanes(cells):
@@ -246,18 +283,20 @@
     return shifted_sum(acc, lane, first, final)
 
 
-def deep_near_kernel(narrow, own, across, own_c, across_c, e, e_across, e_c, e_across_c, t_d, near_f, near_t, far_f, far_t,
-                     total, skip_f, skip_t, x, y, sems):
+def deep_near_kernel(narrow, own, across, own_c, across_c, e, e_across, e_c, e_across_c, t_d, near_f, near_t,
+                     far_f, far_t, edge_f, edge_t, total, skip_f, skip_t, x, y, sems):
     odd = lax.rem(lax.axis_index("wide"), 2)
-    wait = run_copies(
-        [
-            (near_f, skip_f.at[1 - odd]),
-            (near_t, skip_t.at[1 - odd]),
-            (far_f, skip_f.at[odd]),
-            (far_t, skip_t.at[odd]),
-        ],
-        sems,
-    )
+    even_n = lax.rem(lax.axis_index("narrow"), 2) == 0
+    last = far_f.shape[0] - 1
+    edge, rest = jnp.where(even_n, 0, last), pl.ds(jnp.where(even_n, 1, 0), last)
+    copies = []
+    for near, far, row, skip in ((near_f, far_f, edge_f, skip_f), (near_t, far_t, edge_t, skip_t)):
+        copies += [
+            (near, skip.at[1 - odd]),
+            (far.at[rest], skip.at[odd, rest]),
+            (row, skip.at[odd, edge]),
+        ]
+    wait = run_copies(copies, sems)
     gather_rows(x, (own, across, own_c, across_c), None, narrow)
     gather_rows(y, (e, e_across, e_c, e_across_c), None, narrow)
     cells = x.shape[2]
@@ -270,19 +309,25 @@
     wait()
 
 
-def deep_far_kernel(wide, narrow, o, o_across, o_c, o_across_c, t_d, part, out_f, out_t, x):
+def deep_far_kernel(wide, narrow, o, o_across, o_c, o_across_c, t_d, part, out_f, out_t, x, staged, sems):
     w = lax.axis_index("wide")
     cells = x.shape[2] // 2
     far = (w == wide // 2 - 1) | (w == wide // 2)
     gather_rows(x, (o, o_across, o_c, o_across_c), far, narrow)
     lanes = deep_lanes(cells)
-    taps = t_d[2 * lax.rem(w, 2)]
-    taps = jnp.where((w > 0) & (w < wide - 1), taps, jnp.zeros_like(taps))
+    taps = far_taps(wide, t_d)
+    waits = []
     for j in range(part.shape[0]):
         both = part[j] + deep_sum(x, taps, j, *lanes)
-        primal, tangent = activate(both[:, :cells], both[:, cells:])
-        out_f[0, 2 * j : 2 * j + 2] = primal.reshape(2, 64, cells)
-        out_t[0, 2 * j : 2 * j + 2] = tangent.reshape(2, 64, cells)
+        out = activate(both[:, :cells], both[:, cells:])
+        rows = pl.ds(2 * j, 2)
+        copies = []
+        for t, ref in enumerate((out_f, out_t)):
+            staged[t, 2 * j : 2 * j + 2] = out[t].reshape(2, 64, cells)
+            copies.append((staged.at[t, rows], ref.at[0, rows]))
+        waits.append(run_copies(copies, sems.at[j]))
+    for wait in waits:
+        wait()
 
 
 def call(body, outs, in_specs, out_specs, scratch=()):
@@ -314,7 +359,7 @@
     plane, edge = (rows, chans, cells), (planes, 2, chans, cells)
     s_o, s_e, s_c, s_m = call(
         slices_kernel, [(2,) + plane, (2,) + plane, edge, edge],
-        [HBM] * 2, [ANY] * 4, [dma((8,))],
+        [HBM] * 2, [ANY] * 4, [dma((12,))],
     )(volume, volume_tangent)
     r_o = swap(s_o, "O", "same")
     r_e = swap(s_e, "E", "same")
@@ -337,19 +382,22 @@
         functools.partial(own_kernel, narrow),
         [full(planes, 2, wins, 128, cells)], [VMEM] * 4, [VMEM],
     )(own, r_c, r_m, t_s)
-    corners = [(2, chans, cells), (2, chans + PAD, cells)]
-    row_ec, row_em = call(edge_kernel, corners, [VMEM], [VMEM] * 2)(r_e)
-    c_e, m_e = swap(row_ec, "", "core"), swap(row_em, "", "mirror")
-    row_oc, row_om = call(edge_kernel, corners, [VMEM] * 3, [VMEM] * 2)(r_o, part, row_ec)
-    c_o, m_o = swap(row_oc, "", "core"), swap(row_om, "", "mirror")
+    row_ec, row_em = call(edge_kernel, [(2, chans + 2 * PAD, cells)] * 2, [VMEM], [VMEM] * 2)(r_e)
+    c_e, m_e = swap(row_ec, "", "core"), swap(row_em, "", "corner")
+    row_oc, row_om = call(edge_kernel, [(2, chans, cells), (2, chans + PAD, cells)], [VMEM] * 3, [VMEM] * 2)(r_o, part, row_ec)
+    c_o, m_o = swap(row_oc, "", "core"), swap(row_om, "", "corner")
     near_f, near_t, pool_part = call(
         functools.partial(near_kernel, narrow),
         [plane, plane, full(wins, chans, cells)], [VMEM] * 5, [VMEM] * 3,
     )(r_e, c_e, m_e, t_s, part)
-    far_f, far_t, pooled = call(
+    far_f, far_t, pool_far, edge_pre = call(
         functools.partial(far_kernel, wide, narrow),
-        [plane, plane, (wins, chans, cells)], [VMEM] * 6, [VMEM] * 3,
-    )(r_o, c_o, m_o, t_s, part, pool_part)
+        [plane, plane, full(wins, chans, cells), full(2, chans, cells)], [VMEM] * 5, [VMEM] * 4,
+    )(r_o, c_o, t_s, part, pool_part)
+    edge_f, edge_t, pooled = call(
+        functools.partial(edge_row_kernel, wide, narrow),
+        [(chans, cells)] * 2 + [(wins, chans, cells)], [VMEM] * 4, [VMEM] * 3,
+    )(m_o, t_s, edge_pre, pool_far)
     o2 = swap(pooled, "O", "near")
     e2 = swap(pooled, "E", "same")
     across = swap(pooled, "", "across")
@@ -364,12 +412,13 @@
     total_d, skip_f, skip_t = call(
         functools.partial(deep_near_kernel, narrow),
         [sums, volume.shape, volume.shape],
-        [VMEM] * 13, [VMEM, HBM, HBM], [gathered, gathered, dma((4,))],
-    )(pooled, across, own_c, across_c, e2, e_across, e_c, e_across_c, t_d, near_f, near_t, far_f, far_t)
+        [VMEM] * 15, [VMEM, HBM, HBM], [gathered, gathered, dma((6,))],
+    )(pooled, across, own_c, across_c, e2, e_across, e_c, e_across_c, t_d, near_f, near_t, far_f, far_t, edge_f, edge_t)
     deep_shape = (1, deep_rows, 64, cells // 2)
     deep_f, deep_t = call(
         functools.partial(deep_far_kernel, wide, narrow),
-        [deep_shape, deep_shape], [VMEM] * 6, [VMEM] * 2, [gathered],
+        [deep_shape, deep_shape], [VMEM] * 6, [HBM] * 2,
+        [gathered, pltpu.VMEM((2, deep_rows, 64, cells // 2), BF16), dma((deep_rows // 2, 2))],
     )(o2, o_across, o_c, o_across_c, t_d, total_d)
     return skip_f, skip_t, deep_f, deep_t
 

time: 40.9 us -> 40.2 us (0.983)
  waiting for transfers between devices: 3.53 us -> 1.25 us
  starting transfers between devices: 27 us -> 28.1 us
  Pallas kernels: 9.02 us -> 9.6 us
    ppermute x19, waiting for transfers between devices: 3.53 us -> 1.25 us  [swap(): return lax.ppermute(v, BOTH, exchange(wide, narrow, kind, route))]
    ppermute x19, starting transfers between devices: 27 us -> 28.1 us  [swap(): return lax.ppermute(v, BOTH, exchange(wide, narrow, kind, route))]
    pallas_call x3 -> x4, Pallas kernels: 0.93 us -> 1.42 us  [the longest x1 0.86 us: local(): call(functools.partial(far_kernel, wide, narrow), [plane, plane, full(win...]
  transfers between devices with their start and end apart: 19 -> 19, of which waited for: 4 -> 3; matrix products, arithmetic and copies ran while one was open for 0% -> 0% of each run, Pallas kernels for 14% -> 16%
where the time goes in v4:
time: 40.2 us; the launch traced here: 39.9 us
  starting transfers between devices  28.1 us (70%)
  Pallas kernels  9.6 us (24%)
  waiting for transfers between devices  1.25 us (3%)
  between operations  0.93 us (2%)
    ppermute x19, starting transfers between devices, swap(): return lax.ppermute(v, BOTH, exchange(wide, narrow, kind, route))  28.1 us
    pallas_call x1, Pallas kernels, local(): call(weights_kernel, [band, band, (2,) + volume.shape], [HBM] * 4, [VMEM,...  2.22 us
    pallas_call x1, Pallas kernels, local(): call(functools.partial(deep_near_kernel, narrow), [sums, volume.shape, vo...  1.44 us
    pallas_call x1, Pallas kernels, local(): call(functools.partial(deep_far_kernel, wide, narrow), [deep_shape, deep_...  1.29 us
    pallas_call x1, Pallas kernels, local(): call(slices_kernel, [(2,) + plane, (2,) + plane, edge, edge], [HBM] * 2,...  1.28 us
    ppermute x19, waiting for transfers between devices, swap(): return lax.ppermute(v, BOTH, exchange(wide, narrow, kind, route))  1.25 us
    pallas_call x1, Pallas kernels, local(): call(functools.partial(own_kernel, narrow), [full(planes, 2, wins, 128, c...  1.09 us
    pallas_call x1, Pallas kernels, local(): call(functools.partial(near_kernel, narrow), [plane, plane, full(wins, ch...  0.87 us
  transfers between devices with their start and end apart: 19, of which 3 were waited for; matrix products, arithmetic and copies ran while one was open for 0% of the time, Pallas kernels for 16%

profile of v4, /device:TPU:25, one launch (start us, length us, event | category | flops | bytes accessed | tf_op | source)
XLA Modules:
  0.0 39.9 jit_solution(12201333735112365842)
XLA Ops:
  0.6 1.3 %shard_map.75 = (bf16[2,4,64,256]{3,2,1,0:T(8,128)(2,1)S(1)}, bf16[2,4,64,256]{3,2,1,0:T(8,128)(2,1)S(1)}, bf16[2,2,64,256]{3,2,1,0:T(8,128)(2,1)S(1)}, bf16[2,2,64,256]{3,2,1,0:T(8,128)(2,1)S(1)}) custom-call(bf16[2,4,64,256]{3,2,1,0:T(8,128)(2,1)} %vol.3, bf16[2,4,64,256]{3,2,1,0:T(8,128)(2,1)} %tan.3), custom_call_target="tpu_custom_call" | custom-call | tf_op jit(solution)/shard_map/pallas_call | solution.py:360
  1.9 1.3 %collective-permute-start.3 = (bf16[2,4,64,256]{3,2,1,0:T(8,128)(2,1)S(1)}, bf16[2,4,64,256]{3,2,1,0:T(8,128)(2,1)S(1)}, u32[]{:S(2)}, u32[]{:S(2)}) collective-permute-start(bf16[2,4,64,256]{3,2,1,0:T(8,128)(2,1)S(1)} %get-tuple-element.35), channel_id=1, source_target_pairs={{0,4},{1,5},{2,6},{3,7},{4,0},{5,1},{6,2},{7,3},{8,12},{9,13},{10,... | collective-permute-start | bytes 786440 | tf_op jit(solution)/shard_map/ppermute | solution.py:354
  3.2 7.8 %collective-permute-start = (bf16[2,4,64,256]{3,2,1,0:T(8,128)(2,1)S(1)}, bf16[2,4,64,256]{3,2,1,0:T(8,128)(2,1)S(1)}, u32[]{:S(2)}, u32[]{:S(2)}) collective-permute-start(bf16[2,4,64,256]{3,2,1,0:T(8,128)(2,1)S(1)} %get-tuple-element.30), channel_id=1, source_target_pairs={{0,1},{1,0},{2,3},{3,2},{4,8},{5,9},{6,10},{7,11},{8,4},{9,5},{10,... | collective-permute-start | bytes 786440 | tf_op jit(solution)/shard_map/ppermute | solution.py:354
  11.0 1.2 %collective-permute-start.1 = (bf16[2,2,64,256]{3,2,1,0:T(8,128)(2,1)S(1)}, bf16[2,2,64,256]{3,2,1,0:T(8,128)(2,1)S(1)}, u32[]{:S(2)}, u32[]{:S(2)}) collective-permute-start(bf16[2,2,64,256]{3,2,1,0:T(8,128)(2,1)S(1)} %get-tuple-element.32), channel_id=1, source_target_pairs={{0,1},{1,0},{2,3},{3,2},{4,5},{5,4},{6,7},{7,6},{8,9},{9,8},{10,11... | collective-permute-start | bytes 393224 | tf_op jit(solution)/shard_map/ppermute | solution.py:354
  12.4 1.5 %collective-permute-start.7 = (bf16[2,96,256]{2,1,0:T(8,128)(2,1)S(1)}, bf16[2,96,256]{2,1,0:T(8,128)(2,1)S(1)}, u32[]{:S(2)}, u32[]{:S(2)}) collective-permute-start(bf16[2,96,256]{2,1,0:T(8,128)(2,1)S(1)} %get-tuple-element.39), channel_id=1, source_target_pairs={{0,16},{1,2},{2,1},{3,19},{4,20},{5,6},{6,5},{7,23},{8,24},{9,10},... | collective-permute-start | bytes 294920 | tf_op jit(solution)/shard_map/ppermute | solution.py:354
  13.9 2.2 %shard_map.76 = (bf16[3,384,256]{2,1,0:T(8,128)(2,1)S(1)}, bf16[3,384,256]{2,1,0:T(8,128)(2,1)S(1)}, bf16[2,2,4,64,256]{4,3,2,1,0:T(8,128)(2,1)S(1)}) custom-call(bf16[2,4,64,256]{3,2,1,0:T(8,128)(2,1)} %vol.3, bf16[2,4,64,256]{3,2,1,0:T(8,128)(2,1)} %tan.3, bf16[3,3,3,64,64]{4,3,2,1,0:T(8,128)(2,1)} %sw.1, bf16[3,3,3,64,256]{4,3,2,1,0:T(8,128)(2,1)} %dw.1), custom_call_target="tpu_custom_call" | custom-call | tf_op jit(solution)/shard_map/pallas_call | solution.py:369
  16.1 0.2 collective-permute-done.2.r_m
  16.3 1.1 %shard_map.77.rest_0_.part = f32[2,2,2,128,256]{4,3,2,1,0:T(8,128)S(1)} custom-call(bf16[2,2,4,64,256]{4,3,2,1,0:T(8,128)(2,1)S(1)} %get-tuple-element.31.x, bf16[2,2,64,256]{3,2,1,0:T(8,128)(2,1)S(1)} %collective-permute-done.1.r_c, bf16[2,2,64,256]{3,2,1,0:T(8,128)(2,1)S(1)} %collective-permute-done.2.r_m, bf16[3,384,256]{2,1,0:T(8,128)(2,1)S(1)} %get-tuple-element.34.t_s), custom_call_target="tpu_custom_call" | custom-call | tf_op jit(solution)/shard_map/pallas_call | solution.py:381
  17.6 1.0 %collective-permute-start.5 = (bf16[2,64,256]{2,1,0:T(8,128)(2,1)S(1)}, bf16[2,64,256]{2,1,0:T(8,128)(2,1)S(1)}, u32[]{:S(2)}, u32[]{:S(2)}) collective-permute-start(bf16[2,64,256]{2,1,0:T(8,128)(2,1)S(1)} %get-tuple-element.38), channel_id=1, source_target_pairs={{0,1},{1,0},{2,3},{3,2},{4,5},{5,4},{6,7},{7,6},{8,9},{9,8},{10,11... | collective-permute-start | bytes 196616 | tf_op jit(solution)/shard_map/ppermute | solution.py:354
  18.6 0.9 %shard_map.80 = (bf16[4,64,256]{2,1,0:T(8,128)(2,1)S(1)}, bf16[4,64,256]{2,1,0:T(8,128)(2,1)S(1)}, f32[2,64,256]{2,1,0:T(8,128)S(1)}) custom-call(bf16[2,4,64,256]{3,2,1,0:T(8,128)(2,1)S(1)} %collective-permute-done.3.face.r_e, bf16[2,96,256]{2,1,0:T(8,128)(2,1)S(1)} %collective-permute-done.6.c_e, bf16[2,96,256]{2,1,0:T(8,128)(2,1)S(1)} %collective-permute-done.7.m_e, ...), custom_call_target="tpu_custom_call" | custom-call | tf_op jit(solution)/shard_map/pallas_call | solution.py:389
  19.5 0.9 %shard_map.81 = (bf16[4,64,256]{2,1,0:T(8,128)(2,1)S(1)}, bf16[4,64,256]{2,1,0:T(8,128)(2,1)S(1)}, f32[2,64,256]{2,1,0:T(8,128)S(1)}, f32[2,64,256]{2,1,0:T(8,128)S(1)}) custom-call(bf16[2,4,64,256]{3,2,1,0:T(8,128)(2,1)S(1)} %collective-permute-done.face.r_o, bf16[2,64,256]{2,1,0:T(8,128)(2,1)S(1)} %collective-permute-done.5.c_o, ...), custom_call_target="tpu_custom_call" | custom-call | tf_op jit(solution)/shard_map/pallas_call | solution.py:393
  20.3 0.8 %collective-permute-done.4.m_o = bf16[2,80,256]{2,1,0:T(8,128)(2,1)S(1)} collective-permute-done((bf16[2,80,256]{2,1,0:T(8,128)(2,1)S(1)}, bf16[2,80,256]{2,1,0:T(8,128)(2,1)S(1)}, u32[]{:S(2)}, u32[]{:S(2)}) %collective-permute-start.4) | collective-permute-done | bytes 81952 | tf_op jit(solution)/shard_map/ppermute | solution.py:354
  21.2 0.5 %shard_map.82 = (bf16[64,256]{1,0:T(8,128)(2,1)S(1)}, bf16[64,256]{1,0:T(8,128)(2,1)S(1)}, bf16[2,64,256]{2,1,0:T(8,128)(2,1)S(1)}) custom-call(bf16[2,80,256]{2,1,0:T(8,128)(2,1)S(1)} %collective-permute-done.4.m_o, bf16[3,384,256]{2,1,0:T(8,128)(2,1)S(1)} %get-tuple-element.34.t_s, f32[2,64,256]{2,1,0:T(8,128)S(1)} %get-tuple-element.41.edge_pre, ...), custom_call_target="tpu_custom_call" | custom-call | tf_op jit(solution)/shard_map/pallas_call | solution.py:397
  21.8 7.2 %collective-permute-start.15 = (bf16[2,64,256]{2,1,0:T(8,128)(2,1)S(1)}, bf16[2,64,256]{2,1,0:T(8,128)(2,1)S(1)}, u32[]{:S(2)}, u32[]{:S(2)}) collective-permute-start(bf16[2,64,256]{2,1,0:T(8,128)(2,1)S(1)} %get-tuple-element.43.own), channel_id=1, source_target_pairs={{0,1},{1,0},{2,3},{3,2},{4,8},{5,9},{6,10},{7,11},{8,4},{9,5},{10,... | collective-permute-start | bytes 196616 | tf_op jit(solution)/shard_map/ppermute | solution.py:354
  28.9 1.5 %collective-permute-start.12 = (bf16[2,64,256]{2,1,0:T(8,128)(2,1)S(1)}, bf16[2,64,256]{2,1,0:T(8,128)(2,1)S(1)}, u32[]{:S(2)}, u32[]{:S(2)}) collective-permute-start(bf16[2,64,256]{2,1,0:T(8,128)(2,1)S(1)} %collective-permute-done.11.e), channel_id=1, source_target_pairs={{0,2},{1,3},{2,0},{3,1},{4,6},{5,7},{6,4},{7,5},{8,10},{9,11},{10,... | collective-permute-start | bytes 196616 | tf_op jit(solution)/shard_map/ppermute | solution.py:354
  30.4 1.6 %collective-permute-start.9 = (bf16[2,64,256]{2,1,0:T(8,128)(2,1)S(1)}, bf16[2,64,256]{2,1,0:T(8,128)(2,1)S(1)}, u32[]{:S(2)}, u32[]{:S(2)}) collective-permute-start(bf16[2,64,256]{2,1,0:T(8,128)(2,1)S(1)} %get-tuple-element.43.own), channel_id=1, source_target_pairs={{0,1},{1,0},{2,3},{3,2},{4,5},{5,4},{6,7},{7,6},{8,9},{9,8},{10,11... | collective-permute-start | bytes 196616 | tf_op jit(solution)/shard_map/ppermute | solution.py:354
  32.0 0.2 collective-permute-start.16
  32.2 0.5 %collective-permute-start.13 = (bf16[2,64,256]{2,1,0:T(8,128)(2,1)S(1)}, bf16[2,64,256]{2,1,0:T(8,128)(2,1)S(1)}, u32[]{:S(2)}, u32[]{:S(2)}) collective-permute-start(bf16[2,64,256]{2,1,0:T(8,128)(2,1)S(1)} %collective-permute-done.11.e), channel_id=1, source_target_pairs={{0,1},{1,0},{2,3},{3,2},{4,5},{5,4},{6,7},{7,6},{8,9},{9,8},{10,11... | collective-permute-start | bytes 196616 | tf_op jit(solution)/shard_map/ppermute | solution.py:354
  32.7 1.6 %collective-permute-start.10 = (bf16[2,64,256]{2,1,0:T(8,128)(2,1)S(1)}, bf16[2,64,256]{2,1,0:T(8,128)(2,1)S(1)}, u32[]{:S(2)}, u32[]{:S(2)}) collective-permute-start(bf16[2,64,256]{2,1,0:T(8,128)(2,1)S(1)} %collective-permute-done.8.across), channel_id=1, source_target_pairs={{0,1},{1,0},{2,3},{3,2},{4,5},{5,4},{6,7},{7,6},{8,9},{9,8},{10,11... | collective-permute-start | bytes 196616 | tf_op jit(solution)/shard_map/ppermute | solution.py:354
  34.3 0.7 %collective-permute-start.14 = (bf16[2,64,256]{2,1,0:T(8,128)(2,1)S(1)}, bf16[2,64,256]{2,1,0:T(8,128)(2,1)S(1)}, u32[]{:S(2)}, u32[]{:S(2)}) collective-permute-start(bf16[2,64,256]{2,1,0:T(8,128)(2,1)S(1)} %collective-permute-done.12.e_across), channel_id=1, source_target_pairs={{0,1},{1,0},{2,3},{3,2},{4,5},{5,4},{6,7},{7,6},{8,9},{9,8},{10,11... | collective-permute-start | bytes 196616 | tf_op jit(solution)/shard_map/ppermute | solution.py:354
  35.0 0.2 collective-permute-done.16.o_across
  35.2 1.8 %collective-permute-start.18 = (bf16[2,64,256]{2,1,0:T(8,128)(2,1)S(1)}, bf16[2,64,256]{2,1,0:T(8,128)(2,1)S(1)}, u32[]{:S(2)}, u32[]{:S(2)}) collective-permute-start(bf16[2,64,256]{2,1,0:T(8,128)(2,1)S(1)} %collective-permute-done.16.o_across), channel_id=1, source_target_pairs={{0,1},{1,0},{2,3},{3,2},{4,5},{5,4},{6,7},{7,6},{8,9},{9,8},{10,11... | collective-permute-start | bytes 196616 | tf_op jit(solution)/shard_map/ppermute | solution.py:354
  37.0 1.4 %shard_map.83 = (f32[4,128,256]{2,1,0:T(8,128)S(1)}, bf16[2,4,64,256]{3,2,1,0:T(8,128)(2,1)}, bf16[2,4,64,256]{3,2,1,0:T(8,128)(2,1)}) custom-call(bf16[2,64,256]{2,1,0:T(8,128)(2,1)S(1)} %get-tuple-element.43.own, bf16[2,64,256]{2,1,0:T(8,128)(2,1)S(1)} %collective-permute-done.8.across, bf16[2,64,256]{2,1,0:T(8,128)(2,1)S(1)} %collective-permute-done.9.own_c, ...), custom_call_target="tpu_custom_call" | custom-call | tf_op jit(solution)/shard_map/pallas_call | solution.py:412
  38.5 1.3 %shard_map.84 = (bf16[1,8,64,128]{3,2,1,0:T(8,128)(2,1)}, bf16[1,8,64,128]{3,2,1,0:T(8,128)(2,1)}) custom-call(bf16[2,64,256]{2,1,0:T(8,128)(2,1)S(1)} %collective-permute-done.15.o, bf16[2,64,256]{2,1,0:T(8,128)(2,1)S(1)} %collective-permute-done.16.o_across, bf16[2,64,256]{2,1,0:T(8,128)(2,1)S(1)} %collective-permute-done.17.o_c, ...), custom_call_target="tpu_custom_call" | custom-call | tf_op jit(solution)/shard_map/pallas_call | solution.py:418
  (24 shorter events, 0.4 us)
Async XLA Ops:
  1.9 10.3 %collective-permute-start.3 = (bf16[2,4,64,256]{3,2,1,0:T(8,128)(2,1)S(1)}, bf16[2,4,64,256]{3,2,1,0:T(8,128)(2,1)S(1)}, u32[]{:S(2)}, u32[]{:S(2)}) collective-permute-start(bf16[2,4,64,256]{3,2,1,0:T(8,128)(2,1)S(1)} %get-tuple-element.35), channel_id=1, source_target_pairs={{0,4},{1,5},{2,6},{3,7},{4,0},{5,1},{6,2},{7,3},{8,12},{9,13},{10,... | collective-permute-start | bytes 786440 | tf_op jit(solution)/shard_map/ppermute | solution.py:354
  3.2 14.2 %collective-permute-start = (bf16[2,4,64,256]{3,2,1,0:T(8,128)(2,1)S(1)}, bf16[2,4,64,256]{3,2,1,0:T(8,128)(2,1)S(1)}, u32[]{:S(2)}, u32[]{:S(2)}) collective-permute-start(bf16[2,4,64,256]{3,2,1,0:T(8,128)(2,1)S(1)} %get-tuple-element.30), channel_id=1, source_target_pairs={{0,1},{1,0},{2,3},{3,2},{4,8},{5,9},{6,10},{7,11},{8,4},{9,5},{10,... | collective-permute-start | bytes 786440 | tf_op jit(solution)/shard_map/ppermute | solution.py:354
  11.0 5.2 %collective-permute-start.1 = (bf16[2,2,64,256]{3,2,1,0:T(8,128)(2,1)S(1)}, bf16[2,2,64,256]{3,2,1,0:T(8,128)(2,1)S(1)}, u32[]{:S(2)}, u32[]{:S(2)}) collective-permute-start(bf16[2,2,64,256]{3,2,1,0:T(8,128)(2,1)S(1)} %get-tuple-element.32), channel_id=1, source_target_pairs={{0,1},{1,0},{2,3},{3,2},{4,5},{5,4},{6,7},{7,6},{8,9},{9,8},{10,11... | collective-permute-start | bytes 393224 | tf_op jit(solution)/shard_map/ppermute | solution.py:354
  12.2 4.1 %collective-permute-start.2 = (bf16[2,2,64,256]{3,2,1,0:T(8,128)(2,1)S(1)}, bf16[2,2,64,256]{3,2,1,0:T(8,128)(2,1)S(1)}, u32[]{:S(2)}, u32[]{:S(2)}) collective-permute-start(bf16[2,2,64,256]{3,2,1,0:T(8,128)(2,1)S(1)} %get-tuple-element.33), channel_id=1, source_target_pairs={{0,16},{1,2},{2,1},{3,19},{4,20},{5,6},{6,5},{7,23},{8,24},{9,10},... | collective-permute-start | bytes 393224 | tf_op jit(solution)/shard_map/ppermute | solution.py:354
  12.3 6.3 %collective-permute-start.6 = (bf16[2,96,256]{2,1,0:T(8,128)(2,1)S(1)}, bf16[2,96,256]{2,1,0:T(8,128)(2,1)S(1)}, u32[]{:S(2)}, u32[]{:S(2)}) collective-permute-start(bf16[2,96,256]{2,1,0:T(8,128)(2,1)S(1)} %get-tuple-element.36.rest_1_), channel_id=1, source_target_pairs={{0,1},{1,0},{2,3},{3,2},{4,5},{5,4},{6,7},{7,6},{8,9},{9,8},{10,11... | collective-permute-start | bytes 294920 | tf_op jit(solution)/shard_map/ppermute | solution.py:354
  12.4 6.2 %collective-permute-start.7 = (bf16[2,96,256]{2,1,0:T(8,128)(2,1)S(1)}, bf16[2,96,256]{2,1,0:T(8,128)(2,1)S(1)}, u32[]{:S(2)}, u32[]{:S(2)}) collective-permute-start(bf16[2,96,256]{2,1,0:T(8,128)(2,1)S(1)} %get-tuple-element.39), channel_id=1, source_target_pairs={{0,16},{1,2},{2,1},{3,19},{4,20},{5,6},{6,5},{7,23},{8,24},{9,10},... | collective-permute-start | bytes 294920 | tf_op jit(solution)/shard_map/ppermute | solution.py:354
  17.5 3.7 %collective-permute-start.4 = (bf16[2,80,256]{2,1,0:T(8,128)(2,1)S(1)}, bf16[2,80,256]{2,1,0:T(8,128)(2,1)S(1)}, u32[]{:S(2)}, u32[]{:S(2)}) collective-permute-start(bf16[2,80,256]{2,1,0:T(8,128)(2,1)S(1)} %get-tuple-element.37), channel_id=1, source_target_pairs={{0,16},{1,2},{2,1},{3,19},{4,20},{5,6},{6,5},{7,23},{8,24},{9,10},... | collective-permute-start | bytes 245768 | tf_op jit(solution)/shard_map/ppermute | solution.py:354
  17.6 1.9 %collective-permute-start.5 = (bf16[2,64,256]{2,1,0:T(8,128)(2,1)S(1)}, bf16[2,64,256]{2,1,0:T(8,128)(2,1)S(1)}, u32[]{:S(2)}, u32[]{:S(2)}) collective-permute-start(bf16[2,64,256]{2,1,0:T(8,128)(2,1)S(1)} %get-tuple-element.38), channel_id=1, source_target_pairs={{0,1},{1,0},{2,3},{3,2},{4,5},{5,4},{6,7},{7,6},{8,9},{9,8},{10,11... | collective-permute-start | bytes 196616 | tf_op jit(solution)/shard_map/ppermute | solution.py:354
  21.7 7.3 %collective-permute-start.11 = (bf16[2,64,256]{2,1,0:T(8,128)(2,1)S(1)}, bf16[2,64,256]{2,1,0:T(8,128)(2,1)S(1)}, u32[]{:S(2)}, u32[]{:S(2)}) collective-permute-start(bf16[2,64,256]{2,1,0:T(8,128)(2,1)S(1)} %get-tuple-element.43.own), channel_id=1, source_target_pairs={{0,4},{1,5},{2,6},{3,7},{4,0},{5,1},{6,2},{7,3},{8,12},{9,13},{10,... | collective-permute-start | bytes 196616 | tf_op jit(solution)/shard_map/ppermute | solution.py:354
  21.8 10.3 %collective-permute-start.15 = (bf16[2,64,256]{2,1,0:T(8,128)(2,1)S(1)}, bf16[2,64,256]{2,1,0:T(8,128)(2,1)S(1)}, u32[]{:S(2)}, u32[]{:S(2)}) collective-permute-start(bf16[2,64,256]{2,1,0:T(8,128)(2,1)S(1)} %get-tuple-element.43.own), channel_id=1, source_target_pairs={{0,1},{1,0},{2,3},{3,2},{4,8},{5,9},{6,10},{7,11},{8,4},{9,5},{10,... | collective-permute-start | bytes 196616 | tf_op jit(solution)/shard_map/ppermute | solution.py:354
  28.9 3.8 %collective-permute-start.8 = (bf16[2,64,256]{2,1,0:T(8,128)(2,1)S(1)}, bf16[2,64,256]{2,1,0:T(8,128)(2,1)S(1)}, u32[]{:S(2)}, u32[]{:S(2)}) collective-permute-start(bf16[2,64,256]{2,1,0:T(8,128)(2,1)S(1)} %get-tuple-element.43.own), channel_id=1, source_target_pairs={{0,2},{1,3},{2,0},{3,1},{4,6},{5,7},{6,4},{7,5},{8,10},{9,11},{10,... | collective-permute-start | bytes 196616 | tf_op jit(solution)/shard_map/ppermute | solution.py:354
  28.9 5.3 %collective-permute-start.12 = (bf16[2,64,256]{2,1,0:T(8,128)(2,1)S(1)}, bf16[2,64,256]{2,1,0:T(8,128)(2,1)S(1)}, u32[]{:S(2)}, u32[]{:S(2)}) collective-permute-start(bf16[2,64,256]{2,1,0:T(8,128)(2,1)S(1)} %collective-permute-done.11.e), channel_id=1, source_target_pairs={{0,2},{1,3},{2,0},{3,1},{4,6},{5,7},{6,4},{7,5},{8,10},{9,11},{10,... | collective-permute-start | bytes 196616 | tf_op jit(solution)/shard_map/ppermute | solution.py:354
  30.4 4.6 %collective-permute-start.9 = (bf16[2,64,256]{2,1,0:T(8,128)(2,1)S(1)}, bf16[2,64,256]{2,1,0:T(8,128)(2,1)S(1)}, u32[]{:S(2)}, u32[]{:S(2)}) collective-permute-start(bf16[2,64,256]{2,1,0:T(8,128)(2,1)S(1)} %get-tuple-element.43.own), channel_id=1, source_target_pairs={{0,1},{1,0},{2,3},{3,2},{4,5},{5,4},{6,7},{7,6},{8,9},{9,8},{10,11... | collective-permute-start | bytes 196616 | tf_op jit(solution)/shard_map/ppermute | solution.py:354
  32.0 3.1 %collective-permute-start.16 = (bf16[2,64,256]{2,1,0:T(8,128)(2,1)S(1)}, bf16[2,64,256]{2,1,0:T(8,128)(2,1)S(1)}, u32[]{:S(2)}, u32[]{:S(2)}) collective-permute-start(bf16[2,64,256]{2,1,0:T(8,128)(2,1)S(1)} %collective-permute-done.15.o), channel_id=1, source_target_pairs={{0,2},{1,3},{2,0},{3,1},{4,6},{5,7},{6,4},{7,5},{8,10},{9,11},{10,... | collective-permute-start | bytes 196616 | tf_op jit(solution)/shard_map/ppermute | solution.py:354
  32.2 4.8 %collective-permute-start.13 = (bf16[2,64,256]{2,1,0:T(8,128)(2,1)S(1)}, bf16[2,64,256]{2,1,0:T(8,128)(2,1)S(1)}, u32[]{:S(2)}, u32[]{:S(2)}) collective-permute-start(bf16[2,64,256]{2,1,0:T(8,128)(2,1)S(1)} %collective-permute-done.11.e), channel_id=1, source_target_pairs={{0,1},{1,0},{2,3},{3,2},{4,5},{5,4},{6,7},{7,6},{8,9},{9,8},{10,11... | collective-permute-start | bytes 196616 | tf_op jit(solution)/shard_map/ppermute | solution.py:354
  32.7 4.3 %collective-permute-start.10 = (bf16[2,64,256]{2,1,0:T(8,128)(2,1)S(1)}, bf16[2,64,256]{2,1,0:T(8,128)(2,1)S(1)}, u32[]{:S(2)}, u32[]{:S(2)}) collective-permute-start(bf16[2,64,256]{2,1,0:T(8,128)(2,1)S(1)} %collective-permute-done.8.across), channel_id=1, source_target_pairs={{0,1},{1,0},{2,3},{3,2},{4,5},{5,4},{6,7},{7,6},{8,9},{9,8},{10,11... | collective-permute-start | bytes 196616 | tf_op jit(solution)/shard_map/ppermute | solution.py:354
  34.3 2.7 %collective-permute-start.14 = (bf16[2,64,256]{2,1,0:T(8,128)(2,1)S(1)}, bf16[2,64,256]{2,1,0:T(8,128)(2,1)S(1)}, u32[]{:S(2)}, u32[]{:S(2)}) collective-permute-start(bf16[2,64,256]{2,1,0:T(8,128)(2,1)S(1)} %collective-permute-done.12.e_across), channel_id=1, source_target_pairs={{0,1},{1,0},{2,3},{3,2},{4,5},{5,4},{6,7},{7,6},{8,9},{9,8},{10,11... | collective-permute-start | bytes 196616 | tf_op jit(solution)/shard_map/ppermute | solution.py:354
  35.0 3.5 %collective-permute-start.17 = (bf16[2,64,256]{2,1,0:T(8,128)(2,1)S(1)}, bf16[2,64,256]{2,1,0:T(8,128)(2,1)S(1)}, u32[]{:S(2)}, u32[]{:S(2)}) collective-permute-start(bf16[2,64,256]{2,1,0:T(8,128)(2,1)S(1)} %collective-permute-done.15.o), channel_id=1, source_target_pairs={{0,1},{1,0},{2,3},{3,2},{4,5},{5,4},{6,7},{7,6},{8,9},{9,8},{10,11... | collective-permute-start | bytes 196616 | tf_op jit(solution)/shard_map/ppermute | solution.py:354
  35.2 3.3 %collective-permute-start.18 = (bf16[2,64,256]{2,1,0:T(8,128)(2,1)S(1)}, bf16[2,64,256]{2,1,0:T(8,128)(2,1)S(1)}, u32[]{:S(2)}, u32[]{:S(2)}) collective-permute-start(bf16[2,64,256]{2,1,0:T(8,128)(2,1)S(1)} %collective-permute-done.16.o_across), channel_id=1, source_target_pairs={{0,1},{1,0},{2,3},{3,2},{4,5},{5,4},{6,7},{7,6},{8,9},{9,8},{10,11... | collective-permute-start | bytes 196616 | tf_op jit(solution)/shard_map/ppermute | solution.py:354

commit v5 on v4

--- a/solution.py
+++ b/solution.py
@@ -283,8 +283,7 @@
     return shifted_sum(acc, lane, first, final)
 
 
-def deep_near_kernel(narrow, own, across, own_c, across_c, e, e_across, e_c, e_across_c, t_d, near_f, near_t,
-                     far_f, far_t, edge_f, edge_t, total, skip_f, skip_t, x, y, sems):
+def copy_planes(near_f, near_t, far_f, far_t, edge_f, edge_t, skip_f, skip_t, sems):
     odd = lax.rem(lax.axis_index("wide"), 2)
     even_n = lax.rem(lax.axis_index("narrow"), 2) == 0
     last = far_f.shape[0] - 1
@@ -296,7 +295,11 @@
             (far.at[rest], skip.at[odd, rest]),
             (row, skip.at[odd, edge]),
         ]
-    wait = run_copies(copies, sems)
+    return run_copies(copies, sems)
+
+
+def deep_near_kernel(narrow, own, across, own_c, across_c, e, e_across, e_c, e_across_c, t_d, total, x, y):
+    odd = lax.rem(lax.axis_index("wide"), 2)
     gather_rows(x, (own, across, own_c, across_c), None, narrow)
     gather_rows(y, (e, e_across, e_c, e_across_c), None, narrow)
     cells = x.shape[2]
@@ -306,17 +309,18 @@
         stack = [v[2 * j : 2 * j + 4].reshape(256, cells) for v in (x, y)]
         acc = jnp.dot(taps, jnp.concatenate(stack, axis=0), preferred_element_type=F32)
         total[j] = shifted_sum(acc, *lanes)
-    wait()
-
-
-def deep_far_kernel(wide, narrow, o, o_across, o_c, o_across_c, t_d, part, out_f, out_t, x, staged, sems):
+
+
+def deep_far_kernel(wide, narrow, o, o_across, o_c, o_across_c, t_d, part, near_f, near_t,
+                    far_f, far_t, edge_f, edge_t, out_f, out_t, skip_f, skip_t, x, staged, sems, skip_sems):
+    planes = (near_f, near_t, far_f, far_t, edge_f, edge_t, skip_f, skip_t)
+    waits = [copy_planes(*planes, skip_sems)]
     w = lax.axis_index("wide")
     cells = x.shape[2] // 2
     far = (w == wide // 2 - 1) | (w == wide // 2)
     gather_rows(x, (o, o_across, o_c, o_across_c), far, narrow)
     lanes = deep_lanes(cells)
     taps = far_taps(wide, t_d)
-    waits = []
     for j in range(part.shape[0]):
         both = part[j] + deep_sum(x, taps, j, *lanes)
         out = activate(both[:, :cells], both[:, cells:])
@@ -409,17 +413,17 @@
     deep_rows = wins * narrow
     sums = full(deep_rows // 2, 128, cells)
     gathered = pltpu.VMEM((deep_rows + 2, chans, cells), BF16)
-    total_d, skip_f, skip_t = call(
+    (total_d,) = call(
         functools.partial(deep_near_kernel, narrow),
-        [sums, volume.shape, volume.shape],
-        [VMEM] * 15, [VMEM, HBM, HBM], [gathered, gathered, dma((6,))],
-    )(pooled, across, own_c, across_c, e2, e_across, e_c, e_across_c, t_d, near_f, near_t, far_f, far_t, edge_f, edge_t)
+        [sums], [VMEM] * 9, [VMEM], [gathered, gathered],
+    )(pooled, across, own_c, across_c, e2, e_across, e_c, e_across_c, t_d)
     deep_shape = (1, deep_rows, 64, cells // 2)
-    deep_f, deep_t = call(
+    staged = pltpu.VMEM((2, deep_rows, 64, cells // 2), BF16)
+    deep_f, deep_t, skip_f, skip_t = call(
         functools.partial(deep_far_kernel, wide, narrow),
-        [deep_shape, deep_shape], [VMEM] * 6, [HBM] * 2,
-        [gathered, pltpu.VMEM((2, deep_rows, 64, cells // 2), BF16), dma((deep_rows // 2, 2))],
-    )(o2, o_across, o_c, o_across_c, t_d, total_d)
+        [deep_shape, deep_shape, volume.shape, volume.shape], [VMEM] * 12, [HBM] * 4,
+        [gathered, staged, dma((deep_rows // 2, 2)), dma((6,))],
+    )(o2, o_across, o_c, o_across_c, t_d, total_d, near_f, near_t, far_f, far_t, edge_f, edge_t)
     return skip_f, skip_t, deep_f, deep_t
 
 

time: 40.2 us -> 39.6 us (0.985)
  Pallas kernels: 9.6 us -> 9 us
    pallas_call x1, Pallas kernels: 1.44 us -> 0.72 us  [local(): call(functools.partial(deep_near_kernel, narrow), [sums], [VMEM] * 9, [VM...]
  transfers between devices with their start and end apart: 19 -> 19, of which waited for: 3 -> 4; matrix products, arithmetic and copies ran while one was open for 0% -> 0% of each run, Pallas kernels for 16% -> 15%
where the time goes in v5:
time: 39.6 us; the launch traced here: 39.5 us
  starting transfers between devices  28.1 us (71%)
  Pallas kernels  9 us (23%)
  waiting for transfers between devices  1.4 us (4%)
  between operations  0.92 us (2%)
    ppermute x19, starting transfers between devices, swap(): return lax.ppermute(v, BOTH, exchange(wide, narrow, kind, route))  28.1 us
    pallas_call x1, Pallas kernels, local(): call(weights_kernel, [band, band, (2,) + volume.shape], [HBM] * 4, [VMEM,...  2.22 us
    pallas_call x1, Pallas kernels, local(): call(functools.partial(deep_far_kernel, wide, narrow), [deep_shape, deep_...  1.41 us
    ppermute x19, waiting for transfers between devices, swap(): return lax.ppermute(v, BOTH, exchange(wide, narrow, kind, route))  1.4 us
    pallas_call x1, Pallas kernels, local(): call(slices_kernel, [(2,) + plane, (2,) + plane, edge, edge], [HBM] * 2,...  1.28 us
    pallas_call x1, Pallas kernels, local(): call(functools.partial(own_kernel, narrow), [full(planes, 2, wins, 128, c...  1.09 us
    pallas_call x1, Pallas kernels, local(): call(functools.partial(near_kernel, narrow), [plane, plane, full(wins, ch...  0.87 us
    pallas_call x1, Pallas kernels, local(): call(functools.partial(far_kernel, wide, narrow), [plane, plane, full(win...  0.86 us
  transfers between devices with their start and end apart: 19, of which 4 were waited for; matrix products, arithmetic and copies ran while one was open for 0% of the time, Pallas kernels for 15%

profile of v5, /device:TPU:25, one launch (start us, length us, event | category | flops | bytes accessed | tf_op | source)
XLA Modules:
  0.0 39.5 jit_solution(14544511727073800636)
XLA Ops:
  0.6 1.3 %shard_map.75 = (bf16[2,4,64,256]{3,2,1,0:T(8,128)(2,1)S(1)}, bf16[2,4,64,256]{3,2,1,0:T(8,128)(2,1)S(1)}, bf16[2,2,64,256]{3,2,1,0:T(8,128)(2,1)S(1)}, bf16[2,2,64,256]{3,2,1,0:T(8,128)(2,1)S(1)}) custom-call(bf16[2,4,64,256]{3,2,1,0:T(8,128)(2,1)} %vol.3, bf16[2,4,64,256]{3,2,1,0:T(8,128)(2,1)} %tan.3), custom_call_target="tpu_custom_call" | custom-call | tf_op jit(solution)/shard_map/pallas_call | solution.py:364
  1.9 1.3 %collective-permute-start.3 = (bf16[2,4,64,256]{3,2,1,0:T(8,128)(2,1)S(1)}, bf16[2,4,64,256]{3,2,1,0:T(8,128)(2,1)S(1)}, u32[]{:S(2)}, u32[]{:S(2)}) collective-permute-start(bf16[2,4,64,256]{3,2,1,0:T(8,128)(2,1)S(1)} %get-tuple-element.34), channel_id=1, source_target_pairs={{0,4},{1,5},{2,6},{3,7},{4,0},{5,1},{6,2},{7,3},{8,12},{9,13},{10,... | collective-permute-start | bytes 786440 | tf_op jit(solution)/shard_map/ppermute | solution.py:358
  3.2 7.8 %collective-permute-start = (bf16[2,4,64,256]{3,2,1,0:T(8,128)(2,1)S(1)}, bf16[2,4,64,256]{3,2,1,0:T(8,128)(2,1)S(1)}, u32[]{:S(2)}, u32[]{:S(2)}) collective-permute-start(bf16[2,4,64,256]{3,2,1,0:T(8,128)(2,1)S(1)} %get-tuple-element.29), channel_id=1, source_target_pairs={{0,1},{1,0},{2,3},{3,2},{4,8},{5,9},{6,10},{7,11},{8,4},{9,5},{10,... | collective-permute-start | bytes 786440 | tf_op jit(solution)/shard_map/ppermute | solution.py:358
  11.0 1.2 %collective-permute-start.1 = (bf16[2,2,64,256]{3,2,1,0:T(8,128)(2,1)S(1)}, bf16[2,2,64,256]{3,2,1,0:T(8,128)(2,1)S(1)}, u32[]{:S(2)}, u32[]{:S(2)}) collective-permute-start(bf16[2,2,64,256]{3,2,1,0:T(8,128)(2,1)S(1)} %get-tuple-element.31), channel_id=1, source_target_pairs={{0,1},{1,0},{2,3},{3,2},{4,5},{5,4},{6,7},{7,6},{8,9},{9,8},{10,11... | collective-permute-start | bytes 393224 | tf_op jit(solution)/shard_map/ppermute | solution.py:358
  12.4 1.5 %collective-permute-start.7 = (bf16[2,96,256]{2,1,0:T(8,128)(2,1)S(1)}, bf16[2,96,256]{2,1,0:T(8,128)(2,1)S(1)}, u32[]{:S(2)}, u32[]{:S(2)}) collective-permute-start(bf16[2,96,256]{2,1,0:T(8,128)(2,1)S(1)} %get-tuple-element.38), channel_id=1, source_target_pairs={{0,16},{1,2},{2,1},{3,19},{4,20},{5,6},{6,5},{7,23},{8,24},{9,10},... | collective-permute-start | bytes 294920 | tf_op jit(solution)/shard_map/ppermute | solution.py:358
  13.9 2.2 %shard_map.76 = (bf16[3,384,256]{2,1,0:T(8,128)(2,1)S(1)}, bf16[3,384,256]{2,1,0:T(8,128)(2,1)S(1)}, bf16[2,2,4,64,256]{4,3,2,1,0:T(8,128)(2,1)S(1)}) custom-call(bf16[2,4,64,256]{3,2,1,0:T(8,128)(2,1)} %vol.3, bf16[2,4,64,256]{3,2,1,0:T(8,128)(2,1)} %tan.3, bf16[3,3,3,64,64]{4,3,2,1,0:T(8,128)(2,1)} %sw.1, bf16[3,3,3,64,256]{4,3,2,1,0:T(8,128)(2,1)} %dw.1), custom_call_target="tpu_custom_call" | custom-call | tf_op jit(solution)/shard_map/pallas_call | solution.py:373
  16.1 0.2 collective-permute-done.2.r_m
  16.3 1.1 %shard_map.77.rest_0_.part = f32[2,2,2,128,256]{4,3,2,1,0:T(8,128)S(1)} custom-call(bf16[2,2,4,64,256]{4,3,2,1,0:T(8,128)(2,1)S(1)} %get-tuple-element.30.x, bf16[2,2,64,256]{3,2,1,0:T(8,128)(2,1)S(1)} %collective-permute-done.1.r_c, bf16[2,2,64,256]{3,2,1,0:T(8,128)(2,1)S(1)} %collective-permute-done.2.r_m, bf16[3,384,256]{2,1,0:T(8,128)(2,1)S(1)} %get-tuple-element.33.t_s), custom_call_target="tpu_custom_call" | custom-call | tf_op jit(solution)/shard_map/pallas_call | solution.py:385
  17.6 1.0 %collective-permute-start.5 = (bf16[2,64,256]{2,1,0:T(8,128)(2,1)S(1)}, bf16[2,64,256]{2,1,0:T(8,128)(2,1)S(1)}, u32[]{:S(2)}, u32[]{:S(2)}) collective-permute-start(bf16[2,64,256]{2,1,0:T(8,128)(2,1)S(1)} %get-tuple-element.37), channel_id=1, source_target_pairs={{0,1},{1,0},{2,3},{3,2},{4,5},{5,4},{6,7},{7,6},{8,9},{9,8},{10,11... | collective-permute-start | bytes 196616 | tf_op jit(solution)/shard_map/ppermute | solution.py:358
  18.6 0.9 %shard_map.80 = (bf16[4,64,256]{2,1,0:T(8,128)(2,1)S(1)}, bf16[4,64,256]{2,1,0:T(8,128)(2,1)S(1)}, f32[2,64,256]{2,1,0:T(8,128)S(1)}) custom-call(bf16[2,4,64,256]{3,2,1,0:T(8,128)(2,1)S(1)} %collective-permute-done.3.face.r_e, bf16[2,96,256]{2,1,0:T(8,128)(2,1)S(1)} %collective-permute-done.6.c_e, bf16[2,96,256]{2,1,0:T(8,128)(2,1)S(1)} %collective-permute-done.7.m_e, ...), custom_call_target="tpu_custom_call" | custom-call | tf_op jit(solution)/shard_map/pallas_call | solution.py:393
  19.5 0.9 %shard_map.81 = (bf16[4,64,256]{2,1,0:T(8,128)(2,1)S(1)}, bf16[4,64,256]{2,1,0:T(8,128)(2,1)S(1)}, f32[2,64,256]{2,1,0:T(8,128)S(1)}, f32[2,64,256]{2,1,0:T(8,128)S(1)}) custom-call(bf16[2,4,64,256]{3,2,1,0:T(8,128)(2,1)S(1)} %collective-permute-done.face.r_o, bf16[2,64,256]{2,1,0:T(8,128)(2,1)S(1)} %collective-permute-done.5.c_o, ...), custom_call_target="tpu_custom_call" | custom-call | tf_op jit(solution)/shard_map/pallas_call | solution.py:397
  20.3 0.8 %collective-permute-done.4.m_o = bf16[2,80,256]{2,1,0:T(8,128)(2,1)S(1)} collective-permute-done((bf16[2,80,256]{2,1,0:T(8,128)(2,1)S(1)}, bf16[2,80,256]{2,1,0:T(8,128)(2,1)S(1)}, u32[]{:S(2)}, u32[]{:S(2)}) %collective-permute-start.4) | collective-permute-done | bytes 81952 | tf_op jit(solution)/shard_map/ppermute | solution.py:358
  21.2 0.5 %shard_map.82 = (bf16[64,256]{1,0:T(8,128)(2,1)S(1)}, bf16[64,256]{1,0:T(8,128)(2,1)S(1)}, bf16[2,64,256]{2,1,0:T(8,128)(2,1)S(1)}) custom-call(bf16[2,80,256]{2,1,0:T(8,128)(2,1)S(1)} %collective-permute-done.4.m_o, bf16[3,384,256]{2,1,0:T(8,128)(2,1)S(1)} %get-tuple-element.33.t_s, f32[2,64,256]{2,1,0:T(8,128)S(1)} %get-tuple-element.40.edge_pre, ...), custom_call_target="tpu_custom_call" | custom-call | tf_op jit(solution)/shard_map/pallas_call | solution.py:401
  21.8 7.2 %collective-permute-start.8 = (bf16[2,64,256]{2,1,0:T(8,128)(2,1)S(1)}, bf16[2,64,256]{2,1,0:T(8,128)(2,1)S(1)}, u32[]{:S(2)}, u32[]{:S(2)}) collective-permute-start(bf16[2,64,256]{2,1,0:T(8,128)(2,1)S(1)} %get-tuple-element.42.own), channel_id=1, source_target_pairs={{0,1},{1,0},{2,3},{3,2},{4,8},{5,9},{6,10},{7,11},{8,4},{9,5},{10,... | collective-permute-start | bytes 196616 | tf_op jit(solution)/shard_map/ppermute | solution.py:358
  28.9 1.5 %collective-permute-start.16 = (bf16[2,64,256]{2,1,0:T(8,128)(2,1)S(1)}, bf16[2,64,256]{2,1,0:T(8,128)(2,1)S(1)}, u32[]{:S(2)}, u32[]{:S(2)}) collective-permute-start(bf16[2,64,256]{2,1,0:T(8,128)(2,1)S(1)} %collective-permute-done.15.e), channel_id=1, source_target_pairs={{0,2},{1,3},{2,0},{3,1},{4,6},{5,7},{6,4},{7,5},{8,10},{9,11},{10,... | collective-permute-start | bytes 196616 | tf_op jit(solution)/shard_map/ppermute | solution.py:358
  30.4 1.6 %collective-permute-start.13 = (bf16[2,64,256]{2,1,0:T(8,128)(2,1)S(1)}, bf16[2,64,256]{2,1,0:T(8,128)(2,1)S(1)}, u32[]{:S(2)}, u32[]{:S(2)}) collective-permute-start(bf16[2,64,256]{2,1,0:T(8,128)(2,1)S(1)} %get-tuple-element.42.own), channel_id=1, source_target_pairs={{0,1},{1,0},{2,3},{3,2},{4,5},{5,4},{6,7},{7,6},{8,9},{9,8},{10,11... | collective-permute-start | bytes 196616 | tf_op jit(solution)/shard_map/ppermute | solution.py:358
  32.0 0.2 collective-permute-start.9
  32.2 0.5 %collective-permute-start.17 = (bf16[2,64,256]{2,1,0:T(8,128)(2,1)S(1)}, bf16[2,64,256]{2,1,0:T(8,128)(2,1)S(1)}, u32[]{:S(2)}, u32[]{:S(2)}) collective-permute-start(bf16[2,64,256]{2,1,0:T(8,128)(2,1)S(1)} %collective-permute-done.15.e), channel_id=1, source_target_pairs={{0,1},{1,0},{2,3},{3,2},{4,5},{5,4},{6,7},{7,6},{8,9},{9,8},{10,11... | collective-permute-start | bytes 196616 | tf_op jit(solution)/shard_map/ppermute | solution.py:358
  32.7 1.6 %collective-permute-start.14 = (bf16[2,64,256]{2,1,0:T(8,128)(2,1)S(1)}, bf16[2,64,256]{2,1,0:T(8,128)(2,1)S(1)}, u32[]{:S(2)}, u32[]{:S(2)}) collective-permute-start(bf16[2,64,256]{2,1,0:T(8,128)(2,1)S(1)} %collective-permute-done.12.across), channel_id=1, source_target_pairs={{0,1},{1,0},{2,3},{3,2},{4,5},{5,4},{6,7},{7,6},{8,9},{9,8},{10,11... | collective-permute-start | bytes 196616 | tf_op jit(solution)/shard_map/ppermute | solution.py:358
  34.3 0.7 %collective-permute-start.18 = (bf16[2,64,256]{2,1,0:T(8,128)(2,1)S(1)}, bf16[2,64,256]{2,1,0:T(8,128)(2,1)S(1)}, u32[]{:S(2)}, u32[]{:S(2)}) collective-permute-start(bf16[2,64,256]{2,1,0:T(8,128)(2,1)S(1)} %collective-permute-done.16.e_across), channel_id=1, source_target_pairs={{0,1},{1,0},{2,3},{3,2},{4,5},{5,4},{6,7},{7,6},{8,9},{9,8},{10,11... | collective-permute-start | bytes 196616 | tf_op jit(solution)/shard_map/ppermute | solution.py:358
  35.0 0.2 collective-permute-done.9.o_across
  35.2 1.8 %collective-permute-start.11 = (bf16[2,64,256]{2,1,0:T(8,128)(2,1)S(1)}, bf16[2,64,256]{2,1,0:T(8,128)(2,1)S(1)}, u32[]{:S(2)}, u32[]{:S(2)}) collective-permute-start(bf16[2,64,256]{2,1,0:T(8,128)(2,1)S(1)} %collective-permute-done.9.o_across), channel_id=1, source_target_pairs={{0,1},{1,0},{2,3},{3,2},{4,5},{5,4},{6,7},{7,6},{8,9},{9,8},{10,11... | collective-permute-start | bytes 196616 | tf_op jit(solution)/shard_map/ppermute | solution.py:358
  37.0 0.7 %shard_map.83.part = f32[4,128,256]{2,1,0:T(8,128)S(1)} custom-call(bf16[2,64,256]{2,1,0:T(8,128)(2,1)S(1)} %get-tuple-element.42.own, bf16[2,64,256]{2,1,0:T(8,128)(2,1)S(1)} %collective-permute-done.12.across, bf16[2,64,256]{2,1,0:T(8,128)(2,1)S(1)} %collective-permute-done.13.own_c, bf16[2,64,256]{2,1,0:T(8,128)(2,1)S(1)} %collective-permute-done.14.across_c, ...), custom_call_target="tpu_custom_call" | custom-call | tf_op jit(solution)/shard_map/pallas_call | solution.py:416
  37.9 1.4 %shard_map.84 = (bf16[1,8,64,128]{3,2,1,0:T(8,128)(2,1)}, bf16[1,8,64,128]{3,2,1,0:T(8,128)(2,1)}, bf16[2,4,64,256]{3,2,1,0:T(8,128)(2,1)}, bf16[2,4,64,256]{3,2,1,0:T(8,128)(2,1)}) custom-call(bf16[2,64,256]{2,1,0:T(8,128)(2,1)S(1)} %collective-permute-done.8.o, bf16[2,64,256]{2,1,0:T(8,128)(2,1)S(1)} %collective-permute-done.9.o_across, ...), custom_call_target="tpu_custom_call" | custom-call | tf_op jit(solution)/shard_map/pallas_call | solution.py:422
  (24 shorter events, 0.5 us)
Async XLA Ops:
  1.9 10.3 %collective-permute-start.3 = (bf16[2,4,64,256]{3,2,1,0:T(8,128)(2,1)S(1)}, bf16[2,4,64,256]{3,2,1,0:T(8,128)(2,1)S(1)}, u32[]{:S(2)}, u32[]{:S(2)}) collective-permute-start(bf16[2,4,64,256]{3,2,1,0:T(8,128)(2,1)S(1)} %get-tuple-element.34), channel_id=1, source_target_pairs={{0,4},{1,5},{2,6},{3,7},{4,0},{5,1},{6,2},{7,3},{8,12},{9,13},{10,... | collective-permute-start | bytes 786440 | tf_op jit(solution)/shard_map/ppermute | solution.py:358
  3.2 14.2 %collective-permute-start = (bf16[2,4,64,256]{3,2,1,0:T(8,128)(2,1)S(1)}, bf16[2,4,64,256]{3,2,1,0:T(8,128)(2,1)S(1)}, u32[]{:S(2)}, u32[]{:S(2)}) collective-permute-start(bf16[2,4,64,256]{3,2,1,0:T(8,128)(2,1)S(1)} %get-tuple-element.29), channel_id=1, source_target_pairs={{0,1},{1,0},{2,3},{3,2},{4,8},{5,9},{6,10},{7,11},{8,4},{9,5},{10,... | collective-permute-start | bytes 786440 | tf_op jit(solution)/shard_map/ppermute | solution.py:358
  11.0 5.2 %collective-permute-start.1 = (bf16[2,2,64,256]{3,2,1,0:T(8,128)(2,1)S(1)}, bf16[2,2,64,256]{3,2,1,0:T(8,128)(2,1)S(1)}, u32[]{:S(2)}, u32[]{:S(2)}) collective-permute-start(bf16[2,2,64,256]{3,2,1,0:T(8,128)(2,1)S(1)} %get-tuple-element.31), channel_id=1, source_target_pairs={{0,1},{1,0},{2,3},{3,2},{4,5},{5,4},{6,7},{7,6},{8,9},{9,8},{10,11... | collective-permute-start | bytes 393224 | tf_op jit(solution)/shard_map/ppermute | solution.py:358
  12.2 4.1 %collective-permute-start.2 = (bf16[2,2,64,256]{3,2,1,0:T(8,128)(2,1)S(1)}, bf16[2,2,64,256]{3,2,1,0:T(8,128)(2,1)S(1)}, u32[]{:S(2)}, u32[]{:S(2)}) collective-permute-start(bf16[2,2,64,256]{3,2,1,0:T(8,128)(2,1)S(1)} %get-tuple-element.32), channel_id=1, source_target_pairs={{0,16},{1,2},{2,1},{3,19},{4,20},{5,6},{6,5},{7,23},{8,24},{9,10},... | collective-permute-start | bytes 393224 | tf_op jit(solution)/shard_map/ppermute | solution.py:358
  12.3 6.3 %collective-permute-start.6 = (bf16[2,96,256]{2,1,0:T(8,128)(2,1)S(1)}, bf16[2,96,256]{2,1,0:T(8,128)(2,1)S(1)}, u32[]{:S(2)}, u32[]{:S(2)}) collective-permute-start(bf16[2,96,256]{2,1,0:T(8,128)(2,1)S(1)} %get-tuple-element.35.rest_1_), channel_id=1, source_target_pairs={{0,1},{1,0},{2,3},{3,2},{4,5},{5,4},{6,7},{7,6},{8,9},{9,8},{10,11... | collective-permute-start | bytes 294920 | tf_op jit(solution)/shard_map/ppermute | solution.py:358
  12.4 6.2 %collective-permute-start.7 = (bf16[2,96,256]{2,1,0:T(8,128)(2,1)S(1)}, bf16[2,96,256]{2,1,0:T(8,128)(2,1)S(1)}, u32[]{:S(2)}, u32[]{:S(2)}) collective-permute-start(bf16[2,96,256]{2,1,0:T(8,128)(2,1)S(1)} %get-tuple-element.38), channel_id=1, source_target_pairs={{0,16},{1,2},{2,1},{3,19},{4,20},{5,6},{6,5},{7,23},{8,24},{9,10},... | collective-permute-start | bytes 294920 | tf_op jit(solution)/shard_map/ppermute | solution.py:358
  17.5 3.7 %collective-permute-start.4 = (bf16[2,80,256]{2,1,0:T(8,128)(2,1)S(1)}, bf16[2,80,256]{2,1,0:T(8,128)(2,1)S(1)}, u32[]{:S(2)}, u32[]{:S(2)}) collective-permute-start(bf16[2,80,256]{2,1,0:T(8,128)(2,1)S(1)} %get-tuple-element.36), channel_id=1, source_target_pairs={{0,16},{1,2},{2,1},{3,19},{4,20},{5,6},{6,5},{7,23},{8,24},{9,10},... | collective-permute-start | bytes 245768 | tf_op jit(solution)/shard_map/ppermute | solution.py:358
  17.6 1.9 %collective-permute-start.5 = (bf16[2,64,256]{2,1,0:T(8,128)(2,1)S(1)}, bf16[2,64,256]{2,1,0:T(8,128)(2,1)S(1)}, u32[]{:S(2)}, u32[]{:S(2)}) collective-permute-start(bf16[2,64,256]{2,1,0:T(8,128)(2,1)S(1)} %get-tuple-element.37), channel_id=1, source_target_pairs={{0,1},{1,0},{2,3},{3,2},{4,5},{5,4},{6,7},{7,6},{8,9},{9,8},{10,11... | collective-permute-start | bytes 196616 | tf_op jit(solution)/shard_map/ppermute | solution.py:358
  21.7 7.3 %collective-permute-start.15 = (bf16[2,64,256]{2,1,0:T(8,128)(2,1)S(1)}, bf16[2,64,256]{2,1,0:T(8,128)(2,1)S(1)}, u32[]{:S(2)}, u32[]{:S(2)}) collective-permute-start(bf16[2,64,256]{2,1,0:T(8,128)(2,1)S(1)} %get-tuple-element.42.own), channel_id=1, source_target_pairs={{0,4},{1,5},{2,6},{3,7},{4,0},{5,1},{6,2},{7,3},{8,12},{9,13},{10,... | collective-permute-start | bytes 196616 | tf_op jit(solution)/shard_map/ppermute | solution.py:358
  21.8 10.3 %collective-permute-start.8 = (bf16[2,64,256]{2,1,0:T(8,128)(2,1)S(1)}, bf16[2,64,256]{2,1,0:T(8,128)(2,1)S(1)}, u32[]{:S(2)}, u32[]{:S(2)}) collective-permute-start(bf16[2,64,256]{2,1,0:T(8,128)(2,1)S(1)} %get-tuple-element.42.own), channel_id=1, source_target_pairs={{0,1},{1,0},{2,3},{3,2},{4,8},{5,9},{6,10},{7,11},{8,4},{9,5},{10,... | collective-permute-start | bytes 196616 | tf_op jit(solution)/shard_map/ppermute | solution.py:358
  28.9 3.8 %collective-permute-start.12 = (bf16[2,64,256]{2,1,0:T(8,128)(2,1)S(1)}, bf16[2,64,256]{2,1,0:T(8,128)(2,1)S(1)}, u32[]{:S(2)}, u32[]{:S(2)}) collective-permute-start(bf16[2,64,256]{2,1,0:T(8,128)(2,1)S(1)} %get-tuple-element.42.own), channel_id=1, source_target_pairs={{0,2},{1,3},{2,0},{3,1},{4,6},{5,7},{6,4},{7,5},{8,10},{9,11},{10,... | collective-permute-start | bytes 196616 | tf_op jit(solution)/shard_map/ppermute | solution.py:358
  28.9 5.3 %collective-permute-start.16 = (bf16[2,64,256]{2,1,0:T(8,128)(2,1)S(1)}, bf16[2,64,256]{2,1,0:T(8,128)(2,1)S(1)}, u32[]{:S(2)}, u32[]{:S(2)}) collective-permute-start(bf16[2,64,256]{2,1,0:T(8,128)(2,1)S(1)} %collective-permute-done.15.e), channel_id=1, source_target_pairs={{0,2},{1,3},{2,0},{3,1},{4,6},{5,7},{6,4},{7,5},{8,10},{9,11},{10,... | collective-permute-start | bytes 196616 | tf_op jit(solution)/shard_map/ppermute | solution.py:358
  30.4 4.6 %collective-permute-start.13 = (bf16[2,64,256]{2,1,0:T(8,128)(2,1)S(1)}, bf16[2,64,256]{2,1,0:T(8,128)(2,1)S(1)}, u32[]{:S(2)}, u32[]{:S(2)}) collective-permute-start(bf16[2,64,256]{2,1,0:T(8,128)(2,1)S(1)} %get-tuple-element.42.own), channel_id=1, source_target_pairs={{0,1},{1,0},{2,3},{3,2},{4,5},{5,4},{6,7},{7,6},{8,9},{9,8},{10,11... | collective-permute-start | bytes 196616 | tf_op jit(solution)/shard_map/ppermute | solution.py:358
  32.0 3.1 %collective-permute-start.9 = (bf16[2,64,256]{2,1,0:T(8,128)(2,1)S(1)}, bf16[2,64,256]{2,1,0:T(8,128)(2,1)S(1)}, u32[]{:S(2)}, u32[]{:S(2)}) collective-permute-start(bf16[2,64,256]{2,1,0:T(8,128)(2,1)S(1)} %collective-permute-done.8.o), channel_id=1, source_target_pairs={{0,2},{1,3},{2,0},{3,1},{4,6},{5,7},{6,4},{7,5},{8,10},{9,11},{10,... | collective-permute-start | bytes 196616 | tf_op jit(solution)/shard_map/ppermute | solution.py:358
  32.2 4.8 %collective-permute-start.17 = (bf16[2,64,256]{2,1,0:T(8,128)(2,1)S(1)}, bf16[2,64,256]{2,1,0:T(8,128)(2,1)S(1)}, u32[]{:S(2)}, u32[]{:S(2)}) collective-permute-start(bf16[2,64,256]{2,1,0:T(8,128)(2,1)S(1)} %collective-permute-done.15.e), channel_id=1, source_target_pairs={{0,1},{1,0},{2,3},{3,2},{4,5},{5,4},{6,7},{7,6},{8,9},{9,8},{10,11... | collective-permute-start | bytes 196616 | tf_op jit(solution)/shard_map/ppermute | solution.py:358
  32.7 4.3 %collective-permute-start.14 = (bf16[2,64,256]{2,1,0:T(8,128)(2,1)S(1)}, bf16[2,64,256]{2,1,0:T(8,128)(2,1)S(1)}, u32[]{:S(2)}, u32[]{:S(2)}) collective-permute-start(bf16[2,64,256]{2,1,0:T(8,128)(2,1)S(1)} %collective-permute-done.12.across), channel_id=1, source_target_pairs={{0,1},{1,0},{2,3},{3,2},{4,5},{5,4},{6,7},{7,6},{8,9},{9,8},{10,11... | collective-permute-start | bytes 196616 | tf_op jit(solution)/shard_map/ppermute | solution.py:358
  34.3 2.7 %collective-permute-start.18 = (bf16[2,64,256]{2,1,0:T(8,128)(2,1)S(1)}, bf16[2,64,256]{2,1,0:T(8,128)(2,1)S(1)}, u32[]{:S(2)}, u32[]{:S(2)}) collective-permute-start(bf16[2,64,256]{2,1,0:T(8,128)(2,1)S(1)} %collective-permute-done.16.e_across), channel_id=1, source_target_pairs={{0,1},{1,0},{2,3},{3,2},{4,5},{5,4},{6,7},{7,6},{8,9},{9,8},{10,11... | collective-permute-start | bytes 196616 | tf_op jit(solution)/shard_map/ppermute | solution.py:358
  35.0 2.7 %collective-permute-start.10 = (bf16[2,64,256]{2,1,0:T(8,128)(2,1)S(1)}, bf16[2,64,256]{2,1,0:T(8,128)(2,1)S(1)}, u32[]{:S(2)}, u32[]{:S(2)}) collective-permute-start(bf16[2,64,256]{2,1,0:T(8,128)(2,1)S(1)} %collective-permute-done.8.o), channel_id=1, source_target_pairs={{0,1},{1,0},{2,3},{3,2},{4,5},{5,4},{6,7},{7,6},{8,9},{9,8},{10,11... | collective-permute-start | bytes 196616 | tf_op jit(solution)/shard_map/ppermute | solution.py:358
  35.2 2.7 %collective-permute-start.11 = (bf16[2,64,256]{2,1,0:T(8,128)(2,1)S(1)}, bf16[2,64,256]{2,1,0:T(8,128)(2,1)S(1)}, u32[]{:S(2)}, u32[]{:S(2)}) collective-permute-start(bf16[2,64,256]{2,1,0:T(8,128)(2,1)S(1)} %collective-permute-done.9.o_across), channel_id=1, source_target_pairs={{0,1},{1,0},{2,3},{3,2},{4,5},{5,4},{6,7},{7,6},{8,9},{9,8},{10,11... | collective-permute-start | bytes 196616 | tf_op jit(solution)/shard_map/ppermute | solution.py:358

commit v6 on v5

--- a/solution.py
+++ b/solution.py
@@ -111,9 +111,10 @@
 
 
 def shifted_sum(acc, lane, first, final):
-    left = pltpu.roll(acc[0:128], 1, 1)
-    right = pltpu.roll(acc[256:384], acc.shape[1] - 1, 1)
-    return acc[128:256] + jnp.where(first(lane), 0.0, left) + jnp.where(final(lane), 0.0, right)
+    rows = acc.shape[0] // 3
+    left = pltpu.roll(acc[0:rows], 1, 1)
+    right = pltpu.roll(acc[2 * rows :], acc.shape[1] - 1, 1)
+    return acc[rows : 2 * rows] + jnp.where(first(lane), 0.0, left) + jnp.where(final(lane), 0.0, right)
 
 
 def activate(pre, dot):
@@ -239,6 +240,9 @@
     has_m = (n > 0) & (n < narrow - 1)
     lane, first, final = shallow_lanes(cells)
     taps = far_taps(wide, t_s)
+    upper = jnp.concatenate([taps[2 * c * chans : (2 * c + 1) * chans] for c in range(3)], axis=0)
+    lower = jnp.concatenate([taps[(2 * c + 1) * chans : (2 * c + 2) * chans] for c in range(3)], axis=0)
+    taps = jnp.where(even_n, upper, lower)
     pre = []
     for t in range(2):
         row = m_o[t, 0:chans]
@@ -246,8 +250,7 @@
         none = jnp.zeros_like(row)
         stack = [jnp.where(even_n, row, none), none, none, jnp.where(even_n, none, row)]
         acc = jnp.dot(taps, jnp.concatenate(stack, axis=0), preferred_element_type=F32)
-        both = shifted_sum(acc, lane, first, final)
-        pre.append(edge_pre[t] + jnp.where(even_n, both[0:chans], both[chans:]))
+        pre.append(edge_pre[t] + shifted_sum(acc, lane[0:chans], first, final))
     out = activate(*pre)
     edge_f[...], edge_t[...] = out
     pool = pool_plane(out, pair_matrix(cells))
@@ -388,8 +391,9 @@
     )(own, r_c, r_m, t_s)
     row_ec, row_em = call(edge_kernel, [(2, chans + 2 * PAD, cells)] * 2, [VMEM], [VMEM] * 2)(r_e)
     c_e, m_e = swap(row_ec, "", "core"), swap(row_em, "", "corner")
-    row_oc, row_om = call(edge_kernel, [(2, chans, cells), (2, chans + PAD, cells)], [VMEM] * 3, [VMEM] * 2)(r_o, part, row_ec)
-    c_o, m_o = swap(row_oc, "", "core"), swap(row_om, "", "corner")
+    row_oc, row_om = call(edge_kernel, [(2, chans, cells)] * 2, [VMEM] * 3, [VMEM] * 2)(r_o, part, row_ec)
+    m_o = swap(row_om, "", "corner")
+    c_o = swap(row_oc, "", "core")
     near_f, near_t, pool_part = call(
         functools.partial(near_kernel, narrow),
         [plane, plane, full(wins, chans, cells)], [VMEM] * 5, [VMEM] * 3,

time: 39.6 us -> 39.5 us (level)
  waiting for transfers between devices: 1.4 us -> 2.01 us
  starting transfers between devices: 28.1 us -> 27.5 us
    ppermute x19, starting transfers between devices: 28.1 us -> 27.5 us  [swap(): return lax.ppermute(v, BOTH, exchange(wide, narrow, kind, route))]
    ppermute x19, waiting for transfers between devices: 1.4 us -> 2.01 us  [swap(): return lax.ppermute(v, BOTH, exchange(wide, narrow, kind, route))]
  transfers between devices with their start and end apart: 19 -> 19, of which waited for: 4 -> 3; matrix products, arithmetic and copies ran while one was open for 0% -> 0% of each run, Pallas kernels for 15% -> 15%
where the time goes in v6:
time: 39.5 us; the launch traced here: 39.3 us
  starting transfers between devices  27.5 us (70%)
  Pallas kernels  8.94 us (23%)
  waiting for transfers between devices  2.01 us (5%)
  between operations  0.92 us (2%)
    ppermute x19, starting transfers between devices, swap(): return lax.ppermute(v, BOTH, exchange(wide, narrow, kind, route))  27.5 us
    pallas_call x1, Pallas kernels, local(): call(weights_kernel, [band, band, (2,) + volume.shape], [HBM] * 4, [VMEM,...  2.22 us
    ppermute x19, waiting for transfers between devices, swap(): return lax.ppermute(v, BOTH, exchange(wide, narrow, kind, route))  2.01 us
    pallas_call x1, Pallas kernels, local(): call(functools.partial(deep_far_kernel, wide, narrow), [deep_shape, deep_...  1.41 us
    pallas_call x1, Pallas kernels, local(): call(slices_kernel, [(2,) + plane, (2,) + plane, edge, edge], [HBM] * 2,...  1.28 us
    pallas_call x1, Pallas kernels, local(): call(functools.partial(own_kernel, narrow), [full(planes, 2, wins, 128, c...  1.09 us
    pallas_call x1, Pallas kernels, local(): call(functools.partial(far_kernel, wide, narrow), [plane, plane, full(win...  0.87 us
    pallas_call x1, Pallas kernels, local(): call(functools.partial(near_kernel, narrow), [plane, plane, full(wins, ch...  0.87 us
  transfers between devices with their start and end apart: 19, of which 3 were waited for; matrix products, arithmetic and copies ran while one was open for 0% of the time, Pallas kernels for 15%

profile of v6, /device:TPU:25, one launch (start us, length us, event | category | flops | bytes accessed | tf_op | source)
XLA Modules:
  0.0 39.3 jit_solution(1014314080612726721)
XLA Ops:
  0.6 1.3 %shard_map.75 = (bf16[2,4,64,256]{3,2,1,0:T(8,128)(2,1)S(1)}, bf16[2,4,64,256]{3,2,1,0:T(8,128)(2,1)S(1)}, bf16[2,2,64,256]{3,2,1,0:T(8,128)(2,1)S(1)}, bf16[2,2,64,256]{3,2,1,0:T(8,128)(2,1)S(1)}) custom-call(bf16[2,4,64,256]{3,2,1,0:T(8,128)(2,1)} %vol.3, bf16[2,4,64,256]{3,2,1,0:T(8,128)(2,1)} %tan.3), custom_call_target="tpu_custom_call" | custom-call | tf_op jit(solution)/shard_map/pallas_call | solution.py:367
  1.9 1.3 %collective-permute-start.3 = (bf16[2,4,64,256]{3,2,1,0:T(8,128)(2,1)S(1)}, bf16[2,4,64,256]{3,2,1,0:T(8,128)(2,1)S(1)}, u32[]{:S(2)}, u32[]{:S(2)}) collective-permute-start(bf16[2,4,64,256]{3,2,1,0:T(8,128)(2,1)S(1)} %get-tuple-element.34), channel_id=1, source_target_pairs={{0,4},{1,5},{2,6},{3,7},{4,0},{5,1},{6,2},{7,3},{8,12},{9,13},{10,... | collective-permute-start | bytes 786440 | tf_op jit(solution)/shard_map/ppermute | solution.py:361
  3.2 7.8 %collective-permute-start = (bf16[2,4,64,256]{3,2,1,0:T(8,128)(2,1)S(1)}, bf16[2,4,64,256]{3,2,1,0:T(8,128)(2,1)S(1)}, u32[]{:S(2)}, u32[]{:S(2)}) collective-permute-start(bf16[2,4,64,256]{3,2,1,0:T(8,128)(2,1)S(1)} %get-tuple-element.29), channel_id=1, source_target_pairs={{0,1},{1,0},{2,3},{3,2},{4,8},{5,9},{6,10},{7,11},{8,4},{9,5},{10,... | collective-permute-start | bytes 786440 | tf_op jit(solution)/shard_map/ppermute | solution.py:361
  11.0 1.2 %collective-permute-start.1 = (bf16[2,2,64,256]{3,2,1,0:T(8,128)(2,1)S(1)}, bf16[2,2,64,256]{3,2,1,0:T(8,128)(2,1)S(1)}, u32[]{:S(2)}, u32[]{:S(2)}) collective-permute-start(bf16[2,2,64,256]{3,2,1,0:T(8,128)(2,1)S(1)} %get-tuple-element.31), channel_id=1, source_target_pairs={{0,1},{1,0},{2,3},{3,2},{4,5},{5,4},{6,7},{7,6},{8,9},{9,8},{10,11... | collective-permute-start | bytes 393224 | tf_op jit(solution)/shard_map/ppermute | solution.py:361
  12.4 1.5 %collective-permute-start.7 = (bf16[2,96,256]{2,1,0:T(8,128)(2,1)S(1)}, bf16[2,96,256]{2,1,0:T(8,128)(2,1)S(1)}, u32[]{:S(2)}, u32[]{:S(2)}) collective-permute-start(bf16[2,96,256]{2,1,0:T(8,128)(2,1)S(1)} %get-tuple-element.38), channel_id=1, source_target_pairs={{0,16},{1,2},{2,1},{3,19},{4,20},{5,6},{6,5},{7,23},{8,24},{9,10},... | collective-permute-start | bytes 294920 | tf_op jit(solution)/shard_map/ppermute | solution.py:361
  13.9 2.2 %shard_map.76 = (bf16[3,384,256]{2,1,0:T(8,128)(2,1)S(1)}, bf16[3,384,256]{2,1,0:T(8,128)(2,1)S(1)}, bf16[2,2,4,64,256]{4,3,2,1,0:T(8,128)(2,1)S(1)}) custom-call(bf16[2,4,64,256]{3,2,1,0:T(8,128)(2,1)} %vol.3, bf16[2,4,64,256]{3,2,1,0:T(8,128)(2,1)} %tan.3, bf16[3,3,3,64,64]{4,3,2,1,0:T(8,128)(2,1)} %sw.1, bf16[3,3,3,64,256]{4,3,2,1,0:T(8,128)(2,1)} %dw.1), custom_call_target="tpu_custom_call" | custom-call | tf_op jit(solution)/shard_map/pallas_call | solution.py:376
  16.1 0.2 collective-permute-done.2.r_m
  16.3 1.1 %shard_map.77.rest_0_.part = f32[2,2,2,128,256]{4,3,2,1,0:T(8,128)S(1)} custom-call(bf16[2,2,4,64,256]{4,3,2,1,0:T(8,128)(2,1)S(1)} %get-tuple-element.30.x, bf16[2,2,64,256]{3,2,1,0:T(8,128)(2,1)S(1)} %collective-permute-done.1.r_c, bf16[2,2,64,256]{3,2,1,0:T(8,128)(2,1)S(1)} %collective-permute-done.2.r_m, bf16[3,384,256]{2,1,0:T(8,128)(2,1)S(1)} %get-tuple-element.33.t_s), custom_call_target="tpu_custom_call" | custom-call | tf_op jit(solution)/shard_map/pallas_call | solution.py:388
  17.5 1.0 %collective-permute-start.5 = (bf16[2,64,256]{2,1,0:T(8,128)(2,1)S(1)}, bf16[2,64,256]{2,1,0:T(8,128)(2,1)S(1)}, u32[]{:S(2)}, u32[]{:S(2)}) collective-permute-start(bf16[2,64,256]{2,1,0:T(8,128)(2,1)S(1)} %get-tuple-element.37), channel_id=1, source_target_pairs={{0,1},{1,0},{2,3},{3,2},{4,5},{5,4},{6,7},{7,6},{8,9},{9,8},{10,11... | collective-permute-start | bytes 196616 | tf_op jit(solution)/shard_map/ppermute | solution.py:361
  18.5 0.9 %shard_map.80 = (bf16[4,64,256]{2,1,0:T(8,128)(2,1)S(1)}, bf16[4,64,256]{2,1,0:T(8,128)(2,1)S(1)}, f32[2,64,256]{2,1,0:T(8,128)S(1)}) custom-call(bf16[2,4,64,256]{3,2,1,0:T(8,128)(2,1)S(1)} %collective-permute-done.3.face.r_e, bf16[2,96,256]{2,1,0:T(8,128)(2,1)S(1)} %collective-permute-done.6.c_e, bf16[2,96,256]{2,1,0:T(8,128)(2,1)S(1)} %collective-permute-done.7.m_e, ...), custom_call_target="tpu_custom_call" | custom-call | tf_op jit(solution)/shard_map/pallas_call | solution.py:397
  19.4 0.9 %shard_map.81 = (bf16[4,64,256]{2,1,0:T(8,128)(2,1)S(1)}, bf16[4,64,256]{2,1,0:T(8,128)(2,1)S(1)}, f32[2,64,256]{2,1,0:T(8,128)S(1)}, f32[2,64,256]{2,1,0:T(8,128)S(1)}) custom-call(bf16[2,4,64,256]{3,2,1,0:T(8,128)(2,1)S(1)} %collective-permute-done.face.r_o, bf16[2,64,256]{2,1,0:T(8,128)(2,1)S(1)} %collective-permute-done.5.c_o, ...), custom_call_target="tpu_custom_call" | custom-call | tf_op jit(solution)/shard_map/pallas_call | solution.py:401
  20.2 1.6 %collective-permute-done.4.m_o = bf16[2,64,256]{2,1,0:T(8,128)(2,1)S(1)} collective-permute-done((bf16[2,64,256]{2,1,0:T(8,128)(2,1)S(1)}, bf16[2,64,256]{2,1,0:T(8,128)(2,1)S(1)}, u32[]{:S(2)}, u32[]{:S(2)}) %collective-permute-start.4) | collective-permute-done | bytes 65568 | tf_op jit(solution)/shard_map/ppermute | solution.py:361
  21.9 0.4 %shard_map.82 = (bf16[64,256]{1,0:T(8,128)(2,1)S(1)}, bf16[64,256]{1,0:T(8,128)(2,1)S(1)}, bf16[2,64,256]{2,1,0:T(8,128)(2,1)S(1)}) custom-call(bf16[2,64,256]{2,1,0:T(8,128)(2,1)S(1)} %collective-permute-done.4.m_o, bf16[3,384,256]{2,1,0:T(8,128)(2,1)S(1)} %get-tuple-element.33.t_s, f32[2,64,256]{2,1,0:T(8,128)S(1)} %get-tuple-element.40.edge_pre, ...), custom_call_target="tpu_custom_call" | custom-call | tf_op jit(solution)/shard_map/pallas_call | solution.py:405
  22.4 6.8 %collective-permute-start.8 = (bf16[2,64,256]{2,1,0:T(8,128)(2,1)S(1)}, bf16[2,64,256]{2,1,0:T(8,128)(2,1)S(1)}, u32[]{:S(2)}, u32[]{:S(2)}) collective-permute-start(bf16[2,64,256]{2,1,0:T(8,128)(2,1)S(1)} %get-tuple-element.42.own), channel_id=1, source_target_pairs={{0,1},{1,0},{2,3},{3,2},{4,8},{5,9},{6,10},{7,11},{8,4},{9,5},{10,... | collective-permute-start | bytes 196616 | tf_op jit(solution)/shard_map/ppermute | solution.py:361
  29.4 1.3 %collective-permute-start.16 = (bf16[2,64,256]{2,1,0:T(8,128)(2,1)S(1)}, bf16[2,64,256]{2,1,0:T(8,128)(2,1)S(1)}, u32[]{:S(2)}, u32[]{:S(2)}) collective-permute-start(bf16[2,64,256]{2,1,0:T(8,128)(2,1)S(1)} %collective-permute-done.15.e), channel_id=1, source_target_pairs={{0,2},{1,3},{2,0},{3,1},{4,6},{5,7},{6,4},{7,5},{8,10},{9,11},{10,... | collective-permute-start | bytes 196616 | tf_op jit(solution)/shard_map/ppermute | solution.py:361
  30.7 1.2 %collective-permute-start.13 = (bf16[2,64,256]{2,1,0:T(8,128)(2,1)S(1)}, bf16[2,64,256]{2,1,0:T(8,128)(2,1)S(1)}, u32[]{:S(2)}, u32[]{:S(2)}) collective-permute-start(bf16[2,64,256]{2,1,0:T(8,128)(2,1)S(1)} %get-tuple-element.42.own), channel_id=1, source_target_pairs={{0,1},{1,0},{2,3},{3,2},{4,5},{5,4},{6,7},{7,6},{8,9},{9,8},{10,11... | collective-permute-start | bytes 196616 | tf_op jit(solution)/shard_map/ppermute | solution.py:361
  31.9 0.2 collective-permute-start.9
  32.1 0.6 %collective-permute-start.17 = (bf16[2,64,256]{2,1,0:T(8,128)(2,1)S(1)}, bf16[2,64,256]{2,1,0:T(8,128)(2,1)S(1)}, u32[]{:S(2)}, u32[]{:S(2)}) collective-permute-start(bf16[2,64,256]{2,1,0:T(8,128)(2,1)S(1)} %collective-permute-done.15.e), channel_id=1, source_target_pairs={{0,1},{1,0},{2,3},{3,2},{4,5},{5,4},{6,7},{7,6},{8,9},{9,8},{10,11... | collective-permute-start | bytes 196616 | tf_op jit(solution)/shard_map/ppermute | solution.py:361
  32.7 1.7 %collective-permute-start.14 = (bf16[2,64,256]{2,1,0:T(8,128)(2,1)S(1)}, bf16[2,64,256]{2,1,0:T(8,128)(2,1)S(1)}, u32[]{:S(2)}, u32[]{:S(2)}) collective-permute-start(bf16[2,64,256]{2,1,0:T(8,128)(2,1)S(1)} %collective-permute-done.12.across), channel_id=1, source_target_pairs={{0,1},{1,0},{2,3},{3,2},{4,5},{5,4},{6,7},{7,6},{8,9},{9,8},{10,11... | collective-permute-start | bytes 196616 | tf_op jit(solution)/shard_map/ppermute | solution.py:361
  34.4 0.7 %collective-permute-start.18 = (bf16[2,64,256]{2,1,0:T(8,128)(2,1)S(1)}, bf16[2,64,256]{2,1,0:T(8,128)(2,1)S(1)}, u32[]{:S(2)}, u32[]{:S(2)}) collective-permute-start(bf16[2,64,256]{2,1,0:T(8,128)(2,1)S(1)} %collective-permute-done.16.e_across), channel_id=1, source_target_pairs={{0,1},{1,0},{2,3},{3,2},{4,5},{5,4},{6,7},{7,6},{8,9},{9,8},{10,11... | collective-permute-start | bytes 196616 | tf_op jit(solution)/shard_map/ppermute | solution.py:361
  35.2 1.7 %collective-permute-start.11 = (bf16[2,64,256]{2,1,0:T(8,128)(2,1)S(1)}, bf16[2,64,256]{2,1,0:T(8,128)(2,1)S(1)}, u32[]{:S(2)}, u32[]{:S(2)}) collective-permute-start(bf16[2,64,256]{2,1,0:T(8,128)(2,1)S(1)} %collective-permute-done.9.o_across), channel_id=1, source_target_pairs={{0,1},{1,0},{2,3},{3,2},{4,5},{5,4},{6,7},{7,6},{8,9},{9,8},{10,11... | collective-permute-start | bytes 196616 | tf_op jit(solution)/shard_map/ppermute | solution.py:361
  36.9 0.7 %shard_map.83.part = f32[4,128,256]{2,1,0:T(8,128)S(1)} custom-call(bf16[2,64,256]{2,1,0:T(8,128)(2,1)S(1)} %get-tuple-element.42.own, bf16[2,64,256]{2,1,0:T(8,128)(2,1)S(1)} %collective-permute-done.12.across, bf16[2,64,256]{2,1,0:T(8,128)(2,1)S(1)} %collective-permute-done.13.own_c, bf16[2,64,256]{2,1,0:T(8,128)(2,1)S(1)} %collective-permute-done.14.across_c, ...), custom_call_target="tpu_custom_call" | custom-call | tf_op jit(solution)/shard_map/pallas_call | solution.py:420
  37.6 0.2 collective-permute-done.11.o_across_c
  37.8 1.4 %shard_map.84 = (bf16[1,8,64,128]{3,2,1,0:T(8,128)(2,1)}, bf16[1,8,64,128]{3,2,1,0:T(8,128)(2,1)}, bf16[2,4,64,256]{3,2,1,0:T(8,128)(2,1)}, bf16[2,4,64,256]{3,2,1,0:T(8,128)(2,1)}) custom-call(bf16[2,64,256]{2,1,0:T(8,128)(2,1)S(1)} %collective-permute-done.8.o, bf16[2,64,256]{2,1,0:T(8,128)(2,1)S(1)} %collective-permute-done.9.o_across, ...), custom_call_target="tpu_custom_call" | custom-call | tf_op jit(solution)/shard_map/pallas_call | solution.py:426
  (24 shorter events, 0.4 us)
Async XLA Ops:
  1.9 10.3 %collective-permute-start.3 = (bf16[2,4,64,256]{3,2,1,0:T(8,128)(2,1)S(1)}, bf16[2,4,64,256]{3,2,1,0:T(8,128)(2,1)S(1)}, u32[]{:S(2)}, u32[]{:S(2)}) collective-permute-start(bf16[2,4,64,256]{3,2,1,0:T(8,128)(2,1)S(1)} %get-tuple-element.34), channel_id=1, source_target_pairs={{0,4},{1,5},{2,6},{3,7},{4,0},{5,1},{6,2},{7,3},{8,12},{9,13},{10,... | collective-permute-start | bytes 786440 | tf_op jit(solution)/shard_map/ppermute | solution.py:361
  3.2 14.2 %collective-permute-start = (bf16[2,4,64,256]{3,2,1,0:T(8,128)(2,1)S(1)}, bf16[2,4,64,256]{3,2,1,0:T(8,128)(2,1)S(1)}, u32[]{:S(2)}, u32[]{:S(2)}) collective-permute-start(bf16[2,4,64,256]{3,2,1,0:T(8,128)(2,1)S(1)} %get-tuple-element.29), channel_id=1, source_target_pairs={{0,1},{1,0},{2,3},{3,2},{4,8},{5,9},{6,10},{7,11},{8,4},{9,5},{10,... | collective-permute-start | bytes 786440 | tf_op jit(solution)/shard_map/ppermute | solution.py:361
  11.0 5.2 %collective-permute-start.1 = (bf16[2,2,64,256]{3,2,1,0:T(8,128)(2,1)S(1)}, bf16[2,2,64,256]{3,2,1,0:T(8,128)(2,1)S(1)}, u32[]{:S(2)}, u32[]{:S(2)}) collective-permute-start(bf16[2,2,64,256]{3,2,1,0:T(8,128)(2,1)S(1)} %get-tuple-element.31), channel_id=1, source_target_pairs={{0,1},{1,0},{2,3},{3,2},{4,5},{5,4},{6,7},{7,6},{8,9},{9,8},{10,11... | collective-permute-start | bytes 393224 | tf_op jit(solution)/shard_map/ppermute | solution.py:361
  12.2 4.1 %collective-permute-start.2 = (bf16[2,2,64,256]{3,2,1,0:T(8,128)(2,1)S(1)}, bf16[2,2,64,256]{3,2,1,0:T(8,128)(2,1)S(1)}, u32[]{:S(2)}, u32[]{:S(2)}) collective-permute-start(bf16[2,2,64,256]{3,2,1,0:T(8,128)(2,1)S(1)} %get-tuple-element.32), channel_id=1, source_target_pairs={{0,16},{1,2},{2,1},{3,19},{4,20},{5,6},{6,5},{7,23},{8,24},{9,10},... | collective-permute-start | bytes 393224 | tf_op jit(solution)/shard_map/ppermute | solution.py:361
  12.3 6.2 %collective-permute-start.6 = (bf16[2,96,256]{2,1,0:T(8,128)(2,1)S(1)}, bf16[2,96,256]{2,1,0:T(8,128)(2,1)S(1)}, u32[]{:S(2)}, u32[]{:S(2)}) collective-permute-start(bf16[2,96,256]{2,1,0:T(8,128)(2,1)S(1)} %get-tuple-element.35.rest_1_), channel_id=1, source_target_pairs={{0,1},{1,0},{2,3},{3,2},{4,5},{5,4},{6,7},{7,6},{8,9},{9,8},{10,11... | collective-permute-start | bytes 294920 | tf_op jit(solution)/shard_map/ppermute | solution.py:361
  12.4 6.1 %collective-permute-start.7 = (bf16[2,96,256]{2,1,0:T(8,128)(2,1)S(1)}, bf16[2,96,256]{2,1,0:T(8,128)(2,1)S(1)}, u32[]{:S(2)}, u32[]{:S(2)}) collective-permute-start(bf16[2,96,256]{2,1,0:T(8,128)(2,1)S(1)} %get-tuple-element.38), channel_id=1, source_target_pairs={{0,16},{1,2},{2,1},{3,19},{4,20},{5,6},{6,5},{7,23},{8,24},{9,10},... | collective-permute-start | bytes 294920 | tf_op jit(solution)/shard_map/ppermute | solution.py:361
  17.5 1.9 %collective-permute-start.5 = (bf16[2,64,256]{2,1,0:T(8,128)(2,1)S(1)}, bf16[2,64,256]{2,1,0:T(8,128)(2,1)S(1)}, u32[]{:S(2)}, u32[]{:S(2)}) collective-permute-start(bf16[2,64,256]{2,1,0:T(8,128)(2,1)S(1)} %get-tuple-element.37), channel_id=1, source_target_pairs={{0,1},{1,0},{2,3},{3,2},{4,5},{5,4},{6,7},{7,6},{8,9},{9,8},{10,11... | collective-permute-start | bytes 196616 | tf_op jit(solution)/shard_map/ppermute | solution.py:361
  18.5 3.4 %collective-permute-start.4 = (bf16[2,64,256]{2,1,0:T(8,128)(2,1)S(1)}, bf16[2,64,256]{2,1,0:T(8,128)(2,1)S(1)}, u32[]{:S(2)}, u32[]{:S(2)}) collective-permute-start(bf16[2,64,256]{2,1,0:T(8,128)(2,1)S(1)} %get-tuple-element.36), channel_id=1, source_target_pairs={{0,16},{1,2},{2,1},{3,19},{4,20},{5,6},{6,5},{7,23},{8,24},{9,10},... | collective-permute-start | bytes 196616 | tf_op jit(solution)/shard_map/ppermute | solution.py:361
  22.3 7.1 %collective-permute-start.15 = (bf16[2,64,256]{2,1,0:T(8,128)(2,1)S(1)}, bf16[2,64,256]{2,1,0:T(8,128)(2,1)S(1)}, u32[]{:S(2)}, u32[]{:S(2)}) collective-permute-start(bf16[2,64,256]{2,1,0:T(8,128)(2,1)S(1)} %get-tuple-element.42.own), channel_id=1, source_target_pairs={{0,4},{1,5},{2,6},{3,7},{4,0},{5,1},{6,2},{7,3},{8,12},{9,13},{10,... | collective-permute-start | bytes 196616 | tf_op jit(solution)/shard_map/ppermute | solution.py:361
  22.4 9.5 %collective-permute-start.8 = (bf16[2,64,256]{2,1,0:T(8,128)(2,1)S(1)}, bf16[2,64,256]{2,1,0:T(8,128)(2,1)S(1)}, u32[]{:S(2)}, u32[]{:S(2)}) collective-permute-start(bf16[2,64,256]{2,1,0:T(8,128)(2,1)S(1)} %get-tuple-element.42.own), channel_id=1, source_target_pairs={{0,1},{1,0},{2,3},{3,2},{4,8},{5,9},{6,10},{7,11},{8,4},{9,5},{10,... | collective-permute-start | bytes 196616 | tf_op jit(solution)/shard_map/ppermute | solution.py:361
  29.2 3.5 %collective-permute-start.12 = (bf16[2,64,256]{2,1,0:T(8,128)(2,1)S(1)}, bf16[2,64,256]{2,1,0:T(8,128)(2,1)S(1)}, u32[]{:S(2)}, u32[]{:S(2)}) collective-permute-start(bf16[2,64,256]{2,1,0:T(8,128)(2,1)S(1)} %get-tuple-element.42.own), channel_id=1, source_target_pairs={{0,2},{1,3},{2,0},{3,1},{4,6},{5,7},{6,4},{7,5},{8,10},{9,11},{10,... | collective-permute-start | bytes 196616 | tf_op jit(solution)/shard_map/ppermute | solution.py:361
  29.4 5.1 %collective-permute-start.16 = (bf16[2,64,256]{2,1,0:T(8,128)(2,1)S(1)}, bf16[2,64,256]{2,1,0:T(8,128)(2,1)S(1)}, u32[]{:S(2)}, u32[]{:S(2)}) collective-permute-start(bf16[2,64,256]{2,1,0:T(8,128)(2,1)S(1)} %collective-permute-done.15.e), channel_id=1, source_target_pairs={{0,2},{1,3},{2,0},{3,1},{4,6},{5,7},{6,4},{7,5},{8,10},{9,11},{10,... | collective-permute-start | bytes 196616 | tf_op jit(solution)/shard_map/ppermute | solution.py:361
  30.7 4.5 %collective-permute-start.13 = (bf16[2,64,256]{2,1,0:T(8,128)(2,1)S(1)}, bf16[2,64,256]{2,1,0:T(8,128)(2,1)S(1)}, u32[]{:S(2)}, u32[]{:S(2)}) collective-permute-start(bf16[2,64,256]{2,1,0:T(8,128)(2,1)S(1)} %get-tuple-element.42.own), channel_id=1, source_target_pairs={{0,1},{1,0},{2,3},{3,2},{4,5},{5,4},{6,7},{7,6},{8,9},{9,8},{10,11... | collective-permute-start | bytes 196616 | tf_op jit(solution)/shard_map/ppermute | solution.py:361
  31.9 3.3 %collective-permute-start.9 = (bf16[2,64,256]{2,1,0:T(8,128)(2,1)S(1)}, bf16[2,64,256]{2,1,0:T(8,128)(2,1)S(1)}, u32[]{:S(2)}, u32[]{:S(2)}) collective-permute-start(bf16[2,64,256]{2,1,0:T(8,128)(2,1)S(1)} %collective-permute-done.8.o), channel_id=1, source_target_pairs={{0,2},{1,3},{2,0},{3,1},{4,6},{5,7},{6,4},{7,5},{8,10},{9,11},{10,... | collective-permute-start | bytes 196616 | tf_op jit(solution)/shard_map/ppermute | solution.py:361
  32.1 4.8 %collective-permute-start.17 = (bf16[2,64,256]{2,1,0:T(8,128)(2,1)S(1)}, bf16[2,64,256]{2,1,0:T(8,128)(2,1)S(1)}, u32[]{:S(2)}, u32[]{:S(2)}) collective-permute-start(bf16[2,64,256]{2,1,0:T(8,128)(2,1)S(1)} %collective-permute-done.15.e), channel_id=1, source_target_pairs={{0,1},{1,0},{2,3},{3,2},{4,5},{5,4},{6,7},{7,6},{8,9},{9,8},{10,11... | collective-permute-start | bytes 196616 | tf_op jit(solution)/shard_map/ppermute | solution.py:361
  32.7 4.2 %collective-permute-start.14 = (bf16[2,64,256]{2,1,0:T(8,128)(2,1)S(1)}, bf16[2,64,256]{2,1,0:T(8,128)(2,1)S(1)}, u32[]{:S(2)}, u32[]{:S(2)}) collective-permute-start(bf16[2,64,256]{2,1,0:T(8,128)(2,1)S(1)} %collective-permute-done.12.across), channel_id=1, source_target_pairs={{0,1},{1,0},{2,3},{3,2},{4,5},{5,4},{6,7},{7,6},{8,9},{9,8},{10,11... | collective-permute-start | bytes 196616 | tf_op jit(solution)/shard_map/ppermute | solution.py:361
  34.4 2.4 %collective-permute-start.18 = (bf16[2,64,256]{2,1,0:T(8,128)(2,1)S(1)}, bf16[2,64,256]{2,1,0:T(8,128)(2,1)S(1)}, u32[]{:S(2)}, u32[]{:S(2)}) collective-permute-start(bf16[2,64,256]{2,1,0:T(8,128)(2,1)S(1)} %collective-permute-done.16.e_across), channel_id=1, source_target_pairs={{0,1},{1,0},{2,3},{3,2},{4,5},{5,4},{6,7},{7,6},{8,9},{9,8},{10,11... | collective-permute-start | bytes 196616 | tf_op jit(solution)/shard_map/ppermute | solution.py:361
  35.2 2.4 %collective-permute-start.10 = (bf16[2,64,256]{2,1,0:T(8,128)(2,1)S(1)}, bf16[2,64,256]{2,1,0:T(8,128)(2,1)S(1)}, u32[]{:S(2)}, u32[]{:S(2)}) collective-permute-start(bf16[2,64,256]{2,1,0:T(8,128)(2,1)S(1)} %collective-permute-done.8.o), channel_id=1, source_target_pairs={{0,1},{1,0},{2,3},{3,2},{4,5},{5,4},{6,7},{7,6},{8,9},{9,8},{10,11... | collective-permute-start | bytes 196616 | tf_op jit(solution)/shard_map/ppermute | solution.py:361
  35.2 2.6 %collective-permute-start.11 = (bf16[2,64,256]{2,1,0:T(8,128)(2,1)S(1)}, bf16[2,64,256]{2,1,0:T(8,128)(2,1)S(1)}, u32[]{:S(2)}, u32[]{:S(2)}) collective-permute-start(bf16[2,64,256]{2,1,0:T(8,128)(2,1)S(1)} %collective-permute-done.9.o_across), channel_id=1, source_target_pairs={{0,1},{1,0},{2,3},{3,2},{4,5},{5,4},{6,7},{7,6},{8,9},{9,8},{10,11... | collective-permute-start | bytes 196616 | tf_op jit(solution)/shard_map/ppermute | solution.py:361

commit v7 on v6

--- a/solution.py
+++ b/solution.py
@@ -389,7 +389,7 @@
         functools.partial(own_kernel, narrow),
         [full(planes, 2, wins, 128, cells)], [VMEM] * 4, [VMEM],
     )(own, r_c, r_m, t_s)
-    row_ec, row_em = call(edge_kernel, [(2, chans + 2 * PAD, cells)] * 2, [VMEM], [VMEM] * 2)(r_e)
+    row_ec, row_em = call(edge_kernel, [(2, chans + PAD, cells)] * 2, [VMEM], [VMEM] * 2)(r_e)
     c_e, m_e = swap(row_ec, "", "core"), swap(row_em, "", "corner")
     row_oc, row_om = call(edge_kernel, [(2, chans, cells)] * 2, [VMEM] * 3, [VMEM] * 2)(r_o, part, row_ec)
     m_o = swap(row_om, "", "corner")

time: 39.5 us -> 39.5 us (level)
  no operation moved by 1% of the time
where the time goes in v7:
time: 39.5 us; the launch traced here: 39.3 us
  starting transfers between devices  27.5 us (70%)
  Pallas kernels  8.94 us (23%)
  waiting for transfers between devices  2.01 us (5%)
  between operations  0.92 us (2%)
    ppermute x19, starting transfers between devices, swap(): return lax.ppermute(v, BOTH, exchange(wide, narrow, kind, route))  27.5 us
    pallas_call x1, Pallas kernels, local(): call(weights_kernel, [band, band, (2,) + volume.shape], [HBM] * 4, [VMEM,...  2.22 us
    ppermute x19, waiting for transfers between devices, swap(): return lax.ppermute(v, BOTH, exchange(wide, narrow, kind, route))  2.01 us
    pallas_call x1, Pallas kernels, local(): call(functools.partial(deep_far_kernel, wide, narrow), [deep_shape, deep_...  1.41 us
    pallas_call x1, Pallas kernels, local(): call(slices_kernel, [(2,) + plane, (2,) + plane, edge, edge], [HBM] * 2,...  1.28 us
    pallas_call x1, Pallas kernels, local(): call(functools.partial(own_kernel, narrow), [full(planes, 2, wins, 128, c...  1.09 us
    pallas_call x1, Pallas kernels, local(): call(functools.partial(far_kernel, wide, narrow), [plane, plane, full(win...  0.87 us
    pallas_call x1, Pallas kernels, local(): call(functools.partial(near_kernel, narrow), [plane, plane, full(wins, ch...  0.87 us
  transfers between devices with their start and end apart: 19, of which 3 were waited for; matrix products, arithmetic and copies ran while one was open for 0% of the time, Pallas kernels for 15%

profile of v7, /device:TPU:25, one launch (start us, length us, event | category | flops | bytes accessed | tf_op | source)
XLA Modules:
  0.0 39.3 jit_solution(1217112519672701153)
XLA Ops:
  0.6 1.3 %shard_map.75 = (bf16[2,4,64,256]{3,2,1,0:T(8,128)(2,1)S(1)}, bf16[2,4,64,256]{3,2,1,0:T(8,128)(2,1)S(1)}, bf16[2,2,64,256]{3,2,1,0:T(8,128)(2,1)S(1)}, bf16[2,2,64,256]{3,2,1,0:T(8,128)(2,1)S(1)}) custom-call(bf16[2,4,64,256]{3,2,1,0:T(8,128)(2,1)} %vol.3, bf16[2,4,64,256]{3,2,1,0:T(8,128)(2,1)} %tan.3), custom_call_target="tpu_custom_call" | custom-call | tf_op jit(solution)/shard_map/pallas_call | solution.py:367
  1.9 1.3 %collective-permute-start.3 = (bf16[2,4,64,256]{3,2,1,0:T(8,128)(2,1)S(1)}, bf16[2,4,64,256]{3,2,1,0:T(8,128)(2,1)S(1)}, u32[]{:S(2)}, u32[]{:S(2)}) collective-permute-start(bf16[2,4,64,256]{3,2,1,0:T(8,128)(2,1)S(1)} %get-tuple-element.34), channel_id=1, source_target_pairs={{0,4},{1,5},{2,6},{3,7},{4,0},{5,1},{6,2},{7,3},{8,12},{9,13},{10,... | collective-permute-start | bytes 786440 | tf_op jit(solution)/shard_map/ppermute | solution.py:361
  3.2 7.8 %collective-permute-start = (bf16[2,4,64,256]{3,2,1,0:T(8,128)(2,1)S(1)}, bf16[2,4,64,256]{3,2,1,0:T(8,128)(2,1)S(1)}, u32[]{:S(2)}, u32[]{:S(2)}) collective-permute-start(bf16[2,4,64,256]{3,2,1,0:T(8,128)(2,1)S(1)} %get-tuple-element.29), channel_id=1, source_target_pairs={{0,1},{1,0},{2,3},{3,2},{4,8},{5,9},{6,10},{7,11},{8,4},{9,5},{10,... | collective-permute-start | bytes 786440 | tf_op jit(solution)/shard_map/ppermute | solution.py:361
  11.0 1.2 %collective-permute-start.1 = (bf16[2,2,64,256]{3,2,1,0:T(8,128)(2,1)S(1)}, bf16[2,2,64,256]{3,2,1,0:T(8,128)(2,1)S(1)}, u32[]{:S(2)}, u32[]{:S(2)}) collective-permute-start(bf16[2,2,64,256]{3,2,1,0:T(8,128)(2,1)S(1)} %get-tuple-element.31), channel_id=1, source_target_pairs={{0,1},{1,0},{2,3},{3,2},{4,5},{5,4},{6,7},{7,6},{8,9},{9,8},{10,11... | collective-permute-start | bytes 393224 | tf_op jit(solution)/shard_map/ppermute | solution.py:361
  12.4 1.5 %collective-permute-start.7 = (bf16[2,80,256]{2,1,0:T(8,128)(2,1)S(1)}, bf16[2,80,256]{2,1,0:T(8,128)(2,1)S(1)}, u32[]{:S(2)}, u32[]{:S(2)}) collective-permute-start(bf16[2,80,256]{2,1,0:T(8,128)(2,1)S(1)} %get-tuple-element.38), channel_id=1, source_target_pairs={{0,16},{1,2},{2,1},{3,19},{4,20},{5,6},{6,5},{7,23},{8,24},{9,10},... | collective-permute-start | bytes 245768 | tf_op jit(solution)/shard_map/ppermute | solution.py:361
  13.9 2.2 %shard_map.76 = (bf16[3,384,256]{2,1,0:T(8,128)(2,1)S(1)}, bf16[3,384,256]{2,1,0:T(8,128)(2,1)S(1)}, bf16[2,2,4,64,256]{4,3,2,1,0:T(8,128)(2,1)S(1)}) custom-call(bf16[2,4,64,256]{3,2,1,0:T(8,128)(2,1)} %vol.3, bf16[2,4,64,256]{3,2,1,0:T(8,128)(2,1)} %tan.3, bf16[3,3,3,64,64]{4,3,2,1,0:T(8,128)(2,1)} %sw.1, bf16[3,3,3,64,256]{4,3,2,1,0:T(8,128)(2,1)} %dw.1), custom_call_target="tpu_custom_call" | custom-call | tf_op jit(solution)/shard_map/pallas_call | solution.py:376
  16.1 0.2 collective-permute-done.2.r_m
  16.3 1.1 %shard_map.77.rest_0_.part = f32[2,2,2,128,256]{4,3,2,1,0:T(8,128)S(1)} custom-call(bf16[2,2,4,64,256]{4,3,2,1,0:T(8,128)(2,1)S(1)} %get-tuple-element.30.x, bf16[2,2,64,256]{3,2,1,0:T(8,128)(2,1)S(1)} %collective-permute-done.1.r_c, bf16[2,2,64,256]{3,2,1,0:T(8,128)(2,1)S(1)} %collective-permute-done.2.r_m, bf16[3,384,256]{2,1,0:T(8,128)(2,1)S(1)} %get-tuple-element.33.t_s), custom_call_target="tpu_custom_call" | custom-call | tf_op jit(solution)/shard_map/pallas_call | solution.py:388
  17.5 1.0 %collective-permute-start.5 = (bf16[2,64,256]{2,1,0:T(8,128)(2,1)S(1)}, bf16[2,64,256]{2,1,0:T(8,128)(2,1)S(1)}, u32[]{:S(2)}, u32[]{:S(2)}) collective-permute-start(bf16[2,64,256]{2,1,0:T(8,128)(2,1)S(1)} %get-tuple-element.37), channel_id=1, source_target_pairs={{0,1},{1,0},{2,3},{3,2},{4,5},{5,4},{6,7},{7,6},{8,9},{9,8},{10,11... | collective-permute-start | bytes 196616 | tf_op jit(solution)/shard_map/ppermute | solution.py:361
  18.5 0.9 %shard_map.80 = (bf16[4,64,256]{2,1,0:T(8,128)(2,1)S(1)}, bf16[4,64,256]{2,1,0:T(8,128)(2,1)S(1)}, f32[2,64,256]{2,1,0:T(8,128)S(1)}) custom-call(bf16[2,4,64,256]{3,2,1,0:T(8,128)(2,1)S(1)} %collective-permute-done.3.face.r_e, bf16[2,80,256]{2,1,0:T(8,128)(2,1)S(1)} %collective-permute-done.6.c_e, bf16[2,80,256]{2,1,0:T(8,128)(2,1)S(1)} %collective-permute-done.7.m_e, ...), custom_call_target="tpu_custom_call" | custom-call | tf_op jit(solution)/shard_map/pallas_call | solution.py:397
  19.4 0.9 %shard_map.81 = (bf16[4,64,256]{2,1,0:T(8,128)(2,1)S(1)}, bf16[4,64,256]{2,1,0:T(8,128)(2,1)S(1)}, f32[2,64,256]{2,1,0:T(8,128)S(1)}, f32[2,64,256]{2,1,0:T(8,128)S(1)}) custom-call(bf16[2,4,64,256]{3,2,1,0:T(8,128)(2,1)S(1)} %collective-permute-done.face.r_o, bf16[2,64,256]{2,1,0:T(8,128)(2,1)S(1)} %collective-permute-done.5.c_o, ...), custom_call_target="tpu_custom_call" | custom-call | tf_op jit(solution)/shard_map/pallas_call | solution.py:401
  20.2 1.6 %collective-permute-done.4.m_o = bf16[2,64,256]{2,1,0:T(8,128)(2,1)S(1)} collective-permute-done((bf16[2,64,256]{2,1,0:T(8,128)(2,1)S(1)}, bf16[2,64,256]{2,1,0:T(8,128)(2,1)S(1)}, u32[]{:S(2)}, u32[]{:S(2)}) %collective-permute-start.4) | collective-permute-done | bytes 65568 | tf_op jit(solution)/shard_map/ppermute | solution.py:361
  21.9 0.4 %shard_map.82 = (bf16[64,256]{1,0:T(8,128)(2,1)S(1)}, bf16[64,256]{1,0:T(8,128)(2,1)S(1)}, bf16[2,64,256]{2,1,0:T(8,128)(2,1)S(1)}) custom-call(bf16[2,64,256]{2,1,0:T(8,128)(2,1)S(1)} %collective-permute-done.4.m_o, bf16[3,384,256]{2,1,0:T(8,128)(2,1)S(1)} %get-tuple-element.33.t_s, f32[2,64,256]{2,1,0:T(8,128)S(1)} %get-tuple-element.40.edge_pre, ...), custom_call_target="tpu_custom_call" | custom-call | tf_op jit(solution)/shard_map/pallas_call | solution.py:405
  22.4 6.8 %collective-permute-start.8 = (bf16[2,64,256]{2,1,0:T(8,128)(2,1)S(1)}, bf16[2,64,256]{2,1,0:T(8,128)(2,1)S(1)}, u32[]{:S(2)}, u32[]{:S(2)}) collective-permute-start(bf16[2,64,256]{2,1,0:T(8,128)(2,1)S(1)} %get-tuple-element.42.own), channel_id=1, source_target_pairs={{0,1},{1,0},{2,3},{3,2},{4,8},{5,9},{6,10},{7,11},{8,4},{9,5},{10,... | collective-permute-start | bytes 196616 | tf_op jit(solution)/shard_map/ppermute | solution.py:361
  29.4 1.3 %collective-permute-start.16 = (bf16[2,64,256]{2,1,0:T(8,128)(2,1)S(1)}, bf16[2,64,256]{2,1,0:T(8,128)(2,1)S(1)}, u32[]{:S(2)}, u32[]{:S(2)}) collective-permute-start(bf16[2,64,256]{2,1,0:T(8,128)(2,1)S(1)} %collective-permute-done.15.e), channel_id=1, source_target_pairs={{0,2},{1,3},{2,0},{3,1},{4,6},{5,7},{6,4},{7,5},{8,10},{9,11},{10,... | collective-permute-start | bytes 196616 | tf_op jit(solution)/shard_map/ppermute | solution.py:361
  30.7 1.2 %collective-permute-start.13 = (bf16[2,64,256]{2,1,0:T(8,128)(2,1)S(1)}, bf16[2,64,256]{2,1,0:T(8,128)(2,1)S(1)}, u32[]{:S(2)}, u32[]{:S(2)}) collective-permute-start(bf16[2,64,256]{2,1,0:T(8,128)(2,1)S(1)} %get-tuple-element.42.own), channel_id=1, source_target_pairs={{0,1},{1,0},{2,3},{3,2},{4,5},{5,4},{6,7},{7,6},{8,9},{9,8},{10,11... | collective-permute-start | bytes 196616 | tf_op jit(solution)/shard_map/ppermute | solution.py:361
  31.9 0.2 collective-permute-start.9
  32.1 0.6 %collective-permute-start.17 = (bf16[2,64,256]{2,1,0:T(8,128)(2,1)S(1)}, bf16[2,64,256]{2,1,0:T(8,128)(2,1)S(1)}, u32[]{:S(2)}, u32[]{:S(2)}) collective-permute-start(bf16[2,64,256]{2,1,0:T(8,128)(2,1)S(1)} %collective-permute-done.15.e), channel_id=1, source_target_pairs={{0,1},{1,0},{2,3},{3,2},{4,5},{5,4},{6,7},{7,6},{8,9},{9,8},{10,11... | collective-permute-start | bytes 196616 | tf_op jit(solution)/shard_map/ppermute | solution.py:361
  32.7 1.7 %collective-permute-start.14 = (bf16[2,64,256]{2,1,0:T(8,128)(2,1)S(1)}, bf16[2,64,256]{2,1,0:T(8,128)(2,1)S(1)}, u32[]{:S(2)}, u32[]{:S(2)}) collective-permute-start(bf16[2,64,256]{2,1,0:T(8,128)(2,1)S(1)} %collective-permute-done.12.across), channel_id=1, source_target_pairs={{0,1},{1,0},{2,3},{3,2},{4,5},{5,4},{6,7},{7,6},{8,9},{9,8},{10,11... | collective-permute-start | bytes 196616 | tf_op jit(solution)/shard_map/ppermute | solution.py:361
  34.4 0.7 %collective-permute-start.18 = (bf16[2,64,256]{2,1,0:T(8,128)(2,1)S(1)}, bf16[2,64,256]{2,1,0:T(8,128)(2,1)S(1)}, u32[]{:S(2)}, u32[]{:S(2)}) collective-permute-start(bf16[2,64,256]{2,1,0:T(8,128)(2,1)S(1)} %collective-permute-done.16.e_across), channel_id=1, source_target_pairs={{0,1},{1,0},{2,3},{3,2},{4,5},{5,4},{6,7},{7,6},{8,9},{9,8},{10,11... | collective-permute-start | bytes 196616 | tf_op jit(solution)/shard_map/ppermute | solution.py:361
  35.2 1.7 %collective-permute-start.11 = (bf16[2,64,256]{2,1,0:T(8,128)(2,1)S(1)}, bf16[2,64,256]{2,1,0:T(8,128)(2,1)S(1)}, u32[]{:S(2)}, u32[]{:S(2)}) collective-permute-start(bf16[2,64,256]{2,1,0:T(8,128)(2,1)S(1)} %collective-permute-done.9.o_across), channel_id=1, source_target_pairs={{0,1},{1,0},{2,3},{3,2},{4,5},{5,4},{6,7},{7,6},{8,9},{9,8},{10,11... | collective-permute-start | bytes 196616 | tf_op jit(solution)/shard_map/ppermute | solution.py:361
  36.9 0.7 %shard_map.83.part = f32[4,128,256]{2,1,0:T(8,128)S(1)} custom-call(bf16[2,64,256]{2,1,0:T(8,128)(2,1)S(1)} %get-tuple-element.42.own, bf16[2,64,256]{2,1,0:T(8,128)(2,1)S(1)} %collective-permute-done.12.across, bf16[2,64,256]{2,1,0:T(8,128)(2,1)S(1)} %collective-permute-done.13.own_c, bf16[2,64,256]{2,1,0:T(8,128)(2,1)S(1)} %collective-permute-done.14.across_c, ...), custom_call_target="tpu_custom_call" | custom-call | tf_op jit(solution)/shard_map/pallas_call | solution.py:420
  37.6 0.2 collective-permute-done.11.o_across_c
  37.8 1.4 %shard_map.84 = (bf16[1,8,64,128]{3,2,1,0:T(8,128)(2,1)}, bf16[1,8,64,128]{3,2,1,0:T(8,128)(2,1)}, bf16[2,4,64,256]{3,2,1,0:T(8,128)(2,1)}, bf16[2,4,64,256]{3,2,1,0:T(8,128)(2,1)}) custom-call(bf16[2,64,256]{2,1,0:T(8,128)(2,1)S(1)} %collective-permute-done.8.o, bf16[2,64,256]{2,1,0:T(8,128)(2,1)S(1)} %collective-permute-done.9.o_across, ...), custom_call_target="tpu_custom_call" | custom-call | tf_op jit(solution)/shard_map/pallas_call | solution.py:426
  (24 shorter events, 0.4 us)
Async XLA Ops:
  1.9 10.3 %collective-permute-start.3 = (bf16[2,4,64,256]{3,2,1,0:T(8,128)(2,1)S(1)}, bf16[2,4,64,256]{3,2,1,0:T(8,128)(2,1)S(1)}, u32[]{:S(2)}, u32[]{:S(2)}) collective-permute-start(bf16[2,4,64,256]{3,2,1,0:T(8,128)(2,1)S(1)} %get-tuple-element.34), channel_id=1, source_target_pairs={{0,4},{1,5},{2,6},{3,7},{4,0},{5,1},{6,2},{7,3},{8,12},{9,13},{10,... | collective-permute-start | bytes 786440 | tf_op jit(solution)/shard_map/ppermute | solution.py:361
  3.2 14.2 %collective-permute-start = (bf16[2,4,64,256]{3,2,1,0:T(8,128)(2,1)S(1)}, bf16[2,4,64,256]{3,2,1,0:T(8,128)(2,1)S(1)}, u32[]{:S(2)}, u32[]{:S(2)}) collective-permute-start(bf16[2,4,64,256]{3,2,1,0:T(8,128)(2,1)S(1)} %get-tuple-element.29), channel_id=1, source_target_pairs={{0,1},{1,0},{2,3},{3,2},{4,8},{5,9},{6,10},{7,11},{8,4},{9,5},{10,... | collective-permute-start | bytes 786440 | tf_op jit(solution)/shard_map/ppermute | solution.py:361
  11.0 5.2 %collective-permute-start.1 = (bf16[2,2,64,256]{3,2,1,0:T(8,128)(2,1)S(1)}, bf16[2,2,64,256]{3,2,1,0:T(8,128)(2,1)S(1)}, u32[]{:S(2)}, u32[]{:S(2)}) collective-permute-start(bf16[2,2,64,256]{3,2,1,0:T(8,128)(2,1)S(1)} %get-tuple-element.31), channel_id=1, source_target_pairs={{0,1},{1,0},{2,3},{3,2},{4,5},{5,4},{6,7},{7,6},{8,9},{9,8},{10,11... | collective-permute-start | bytes 393224 | tf_op jit(solution)/shard_map/ppermute | solution.py:361
  12.2 4.1 %collective-permute-start.2 = (bf16[2,2,64,256]{3,2,1,0:T(8,128)(2,1)S(1)}, bf16[2,2,64,256]{3,2,1,0:T(8,128)(2,1)S(1)}, u32[]{:S(2)}, u32[]{:S(2)}) collective-permute-start(bf16[2,2,64,256]{3,2,1,0:T(8,128)(2,1)S(1)} %get-tuple-element.32), channel_id=1, source_target_pairs={{0,16},{1,2},{2,1},{3,19},{4,20},{5,6},{6,5},{7,23},{8,24},{9,10},... | collective-permute-start | bytes 393224 | tf_op jit(solution)/shard_map/ppermute | solution.py:361
  12.3 6.2 %collective-permute-start.6 = (bf16[2,80,256]{2,1,0:T(8,128)(2,1)S(1)}, bf16[2,80,256]{2,1,0:T(8,128)(2,1)S(1)}, u32[]{:S(2)}, u32[]{:S(2)}) collective-permute-start(bf16[2,80,256]{2,1,0:T(8,128)(2,1)S(1)} %get-tuple-element.35.rest_1_), channel_id=1, source_target_pairs={{0,1},{1,0},{2,3},{3,2},{4,5},{5,4},{6,7},{7,6},{8,9},{9,8},{10,11... | collective-permute-start | bytes 245768 | tf_op jit(solution)/shard_map/ppermute | solution.py:361
  12.4 6.1 %collective-permute-start.7 = (bf16[2,80,256]{2,1,0:T(8,128)(2,1)S(1)}, bf16[2,80,256]{2,1,0:T(8,128)(2,1)S(1)}, u32[]{:S(2)}, u32[]{:S(2)}) collective-permute-start(bf16[2,80,256]{2,1,0:T(8,128)(2,1)S(1)} %get-tuple-element.38), channel_id=1, source_target_pairs={{0,16},{1,2},{2,1},{3,19},{4,20},{5,6},{6,5},{7,23},{8,24},{9,10},... | collective-permute-start | bytes 245768 | tf_op jit(solution)/shard_map/ppermute | solution.py:361
  17.5 1.9 %collective-permute-start.5 = (bf16[2,64,256]{2,1,0:T(8,128)(2,1)S(1)}, bf16[2,64,256]{2,1,0:T(8,128)(2,1)S(1)}, u32[]{:S(2)}, u32[]{:S(2)}) collective-permute-start(bf16[2,64,256]{2,1,0:T(8,128)(2,1)S(1)} %get-tuple-element.37), channel_id=1, source_target_pairs={{0,1},{1,0},{2,3},{3,2},{4,5},{5,4},{6,7},{7,6},{8,9},{9,8},{10,11... | collective-permute-start | bytes 196616 | tf_op jit(solution)/shard_map/ppermute | solution.py:361
  18.5 3.4 %collective-permute-start.4 = (bf16[2,64,256]{2,1,0:T(8,128)(2,1)S(1)}, bf16[2,64,256]{2,1,0:T(8,128)(2,1)S(1)}, u32[]{:S(2)}, u32[]{:S(2)}) collective-permute-start(bf16[2,64,256]{2,1,0:T(8,128)(2,1)S(1)} %get-tuple-element.36), channel_id=1, source_target_pairs={{0,16},{1,2},{2,1},{3,19},{4,20},{5,6},{6,5},{7,23},{8,24},{9,10},... | collective-permute-start | bytes 196616 | tf_op jit(solution)/shard_map/ppermute | solution.py:361
  22.3 7.1 %collective-permute-start.15 = (bf16[2,64,256]{2,1,0:T(8,128)(2,1)S(1)}, bf16[2,64,256]{2,1,0:T(8,128)(2,1)S(1)}, u32[]{:S(2)}, u32[]{:S(2)}) collective-permute-start(bf16[2,64,256]{2,1,0:T(8,128)(2,1)S(1)} %get-tuple-element.42.own), channel_id=1, source_target_pairs={{0,4},{1,5},{2,6},{3,7},{4,0},{5,1},{6,2},{7,3},{8,12},{9,13},{10,... | collective-permute-start | bytes 196616 | tf_op jit(solution)/shard_map/ppermute | solution.py:361
  22.4 9.5 %collective-permute-start.8 = (bf16[2,64,256]{2,1,0:T(8,128)(2,1)S(1)}, bf16[2,64,256]{2,1,0:T(8,128)(2,1)S(1)}, u32[]{:S(2)}, u32[]{:S(2)}) collective-permute-start(bf16[2,64,256]{2,1,0:T(8,128)(2,1)S(1)} %get-tuple-element.42.own), channel_id=1, source_target_pairs={{0,1},{1,0},{2,3},{3,2},{4,8},{5,9},{6,10},{7,11},{8,4},{9,5},{10,... | collective-permute-start | bytes 196616 | tf_op jit(solution)/shard_map/ppermute | solution.py:361
  29.2 3.5 %collective-permute-start.12 = (bf16[2,64,256]{2,1,0:T(8,128)(2,1)S(1)}, bf16[2,64,256]{2,1,0:T(8,128)(2,1)S(1)}, u32[]{:S(2)}, u32[]{:S(2)}) collective-permute-start(bf16[2,64,256]{2,1,0:T(8,128)(2,1)S(1)} %get-tuple-element.42.own), channel_id=1, source_target_pairs={{0,2},{1,3},{2,0},{3,1},{4,6},{5,7},{6,4},{7,5},{8,10},{9,11},{10,... | collective-permute-start | bytes 196616 | tf_op jit(solution)/shard_map/ppermute | solution.py:361
  29.4 5.1 %collective-permute-start.16 = (bf16[2,64,256]{2,1,0:T(8,128)(2,1)S(1)}, bf16[2,64,256]{2,1,0:T(8,128)(2,1)S(1)}, u32[]{:S(2)}, u32[]{:S(2)}) collective-permute-start(bf16[2,64,256]{2,1,0:T(8,128)(2,1)S(1)} %collective-permute-done.15.e), channel_id=1, source_target_pairs={{0,2},{1,3},{2,0},{3,1},{4,6},{5,7},{6,4},{7,5},{8,10},{9,11},{10,... | collective-permute-start | bytes 196616 | tf_op jit(solution)/shard_map/ppermute | solution.py:361
  30.7 4.5 %collective-permute-start.13 = (bf16[2,64,256]{2,1,0:T(8,128)(2,1)S(1)}, bf16[2,64,256]{2,1,0:T(8,128)(2,1)S(1)}, u32[]{:S(2)}, u32[]{:S(2)}) collective-permute-start(bf16[2,64,256]{2,1,0:T(8,128)(2,1)S(1)} %get-tuple-element.42.own), channel_id=1, source_target_pairs={{0,1},{1,0},{2,3},{3,2},{4,5},{5,4},{6,7},{7,6},{8,9},{9,8},{10,11... | collective-permute-start | bytes 196616 | tf_op jit(solution)/shard_map/ppermute | solution.py:361
  31.9 3.3 %collective-permute-start.9 = (bf16[2,64,256]{2,1,0:T(8,128)(2,1)S(1)}, bf16[2,64,256]{2,1,0:T(8,128)(2,1)S(1)}, u32[]{:S(2)}, u32[]{:S(2)}) collective-permute-start(bf16[2,64,256]{2,1,0:T(8,128)(2,1)S(1)} %collective-permute-done.8.o), channel_id=1, source_target_pairs={{0,2},{1,3},{2,0},{3,1},{4,6},{5,7},{6,4},{7,5},{8,10},{9,11},{10,... | collective-permute-start | bytes 196616 | tf_op jit(solution)/shard_map/ppermute | solution.py:361
  32.1 4.8 %collective-permute-start.17 = (bf16[2,64,256]{2,1,0:T(8,128)(2,1)S(1)}, bf16[2,64,256]{2,1,0:T(8,128)(2,1)S(1)}, u32[]{:S(2)}, u32[]{:S(2)}) collective-permute-start(bf16[2,64,256]{2,1,0:T(8,128)(2,1)S(1)} %collective-permute-done.15.e), channel_id=1, source_target_pairs={{0,1},{1,0},{2,3},{3,2},{4,5},{5,4},{6,7},{7,6},{8,9},{9,8},{10,11... | collective-permute-start | bytes 196616 | tf_op jit(solution)/shard_map/ppermute | solution.py:361
  32.7 4.2 %collective-permute-start.14 = (bf16[2,64,256]{2,1,0:T(8,128)(2,1)S(1)}, bf16[2,64,256]{2,1,0:T(8,128)(2,1)S(1)}, u32[]{:S(2)}, u32[]{:S(2)}) collective-permute-start(bf16[2,64,256]{2,1,0:T(8,128)(2,1)S(1)} %collective-permute-done.12.across), channel_id=1, source_target_pairs={{0,1},{1,0},{2,3},{3,2},{4,5},{5,4},{6,7},{7,6},{8,9},{9,8},{10,11... | collective-permute-start | bytes 196616 | tf_op jit(solution)/shard_map/ppermute | solution.py:361
  34.4 2.4 %collective-permute-start.18 = (bf16[2,64,256]{2,1,0:T(8,128)(2,1)S(1)}, bf16[2,64,256]{2,1,0:T(8,128)(2,1)S(1)}, u32[]{:S(2)}, u32[]{:S(2)}) collective-permute-start(bf16[2,64,256]{2,1,0:T(8,128)(2,1)S(1)} %collective-permute-done.16.e_across), channel_id=1, source_target_pairs={{0,1},{1,0},{2,3},{3,2},{4,5},{5,4},{6,7},{7,6},{8,9},{9,8},{10,11... | collective-permute-start | bytes 196616 | tf_op jit(solution)/shard_map/ppermute | solution.py:361
  35.2 2.4 %collective-permute-start.10 = (bf16[2,64,256]{2,1,0:T(8,128)(2,1)S(1)}, bf16[2,64,256]{2,1,0:T(8,128)(2,1)S(1)}, u32[]{:S(2)}, u32[]{:S(2)}) collective-permute-start(bf16[2,64,256]{2,1,0:T(8,128)(2,1)S(1)} %collective-permute-done.8.o), channel_id=1, source_target_pairs={{0,1},{1,0},{2,3},{3,2},{4,5},{5,4},{6,7},{7,6},{8,9},{9,8},{10,11... | collective-permute-start | bytes 196616 | tf_op jit(solution)/shard_map/ppermute | solution.py:361
  35.2 2.6 %collective-permute-start.11 = (bf16[2,64,256]{2,1,0:T(8,128)(2,1)S(1)}, bf16[2,64,256]{2,1,0:T(8,128)(2,1)S(1)}, u32[]{:S(2)}, u32[]{:S(2)}) collective-permute-start(bf16[2,64,256]{2,1,0:T(8,128)(2,1)S(1)} %collective-permute-done.9.o_across), channel_id=1, source_target_pairs={{0,1},{1,0},{2,3},{3,2},{4,5},{5,4},{6,7},{7,6},{8,9},{9,8},{10,11... | collective-permute-start | bytes 196616 | tf_op jit(solution)/shard_map/ppermute | solution.py:361
